TPU v7x, 512 devices: a whole 4x8x8 slice. The times are simulated.
512 devices in a mesh: seq: 64 (over z_hi, y, x), head: 8 (over z_lo, core).
Axes of the slice: x: 4, y: 8, z: 8 (z_hi: 2, z_lo: 4; z = z_hi * 4 + z_lo), core: 2. Of those that a mesh axis runs over, the one named last changes fastest.
Arguments:
- query_raw: bfloat16 [64, 512, 5120], P('seq', 'head'), may hold values from -60 to 60
- key_raw: bfloat16 [64, 512, 1024], P('seq', 'head'), may hold values from -60 to 60
- value_in: bfloat16 [64, 512, 1024], P('seq', 'head'), may hold values from -6 to 6
- out_grad: bfloat16 [64, 512, 5120], P('seq', 'head'), may hold values from -6 to 6
- query_gain: float32 [5120], replicated, may hold values from 0.25 to 1.75
- key_gain: float32 [1024], replicated, may hold values from 0.25 to 1.75
- doc_blocks: int32 [96], replicated, may hold values from 1 to 4, as said below
Outputs:
- d_query: bfloat16 [64, 512, 5120], P('seq', 'head')
- d_key: bfloat16 [64, 512, 1024], P('seq', 'head')
- d_value: bfloat16 [64, 512, 1024], P('seq', 'head')
- d_query_gain: float32 [5120], replicated
- d_key_gain: float32 [1024], replicated
Inputs may be any that keep to these rules, and one draw needn't show every extreme that they name: `doc_blocks`: lengths of the documents in order, in blocks of 128 tokens; they sum to 256; the first document has 1 block and the second exactly 4.
All inputs are finite; a program needn't handle non-finite values.
Results may differ from a plain program's by a relative error of at most 0.0095.
The roundings to bfloat16 on the way count: a program that leaves them out, or rounds other values in their place, can miss the bound.
Values may be sent and summed in bfloat16 or wider, within the bound.
No kernel may reach another device: no remote copies, remote signals or barrier semaphores. Data moves between devices by JAX's collectives and lax.ppermute only.
A program may use at most 64 MiB of HBM per device.

v0:
```python
import math

import jax
import jax.numpy as jnp
from jax import lax
from jax.sharding import PartitionSpec as P

GROUP = 5
HEAD_DIM = 128
BLOCK = 128
REACH = 2


EPSILON = 1e-06
MASKED = -1e30


def from_behind(value, axis, steps):
    count = lax.axis_size(axis)
    leading, last = (max(0, -steps), min(count, count - steps))
    return lax.ppermute(value, axis, [(source, source + steps) for source in range(leading, last)])


def normalize(rows, gain):
    values = rows.astype(jnp.float32)
    inverse = lax.rsqrt(jnp.mean(values * values, axis=-1, keepdims=True) + EPSILON)
    return ((values * inverse * gain).astype(jnp.bfloat16), inverse)


def norm_backward(rows, inverse, gain, grad):
    values = rows.astype(jnp.float32)
    upstream = grad.astype(jnp.float32)
    scaled = upstream * gain
    inner = jnp.mean(scaled * values, axis=-1, keepdims=True)
    d_rows = inverse * scaled - values * inverse * inverse * inverse * inner
    d_gain = jnp.sum(upstream * values * inverse, axis=0)
    return (d_rows.astype(jnp.bfloat16), d_gain)


def span_labels(start, count, limit, ends, missing):
    places = start + jnp.arange(count, dtype=jnp.int32)
    inside = (places >= 0) & (places < limit)
    blocks = places // BLOCK
    found = jnp.sum((ends[None, :] <= blocks[:, None]).astype(jnp.int32), axis=1)
    return (places, jnp.where(inside, found, missing))


def allowed_pairs(query_places, query_docs, key_places, key_docs):
    return (query_docs[:, None] == key_docs[None, :]) & (
        key_places[None, :] <= query_places[:, None]
    )


def attend(query_block, grad_block, key_window, value_window, allowed):
    scale = 1.0 / math.sqrt(query_block.shape[-1])
    scores = (
        jnp.einsum("qgrd,kgd->grqk", query_block, key_window, preferred_element_type=jnp.float32)
        * scale
    )
    scores = jnp.where(allowed[None, None], scores, MASKED)
    highest = jnp.max(scores, axis=-1, keepdims=True)
    log_total = highest + jnp.log(jnp.sum(jnp.exp(scores - highest), axis=-1, keepdims=True))
    weights = jnp.where(allowed[None, None], jnp.exp(scores - log_total), 0.0)
    probs = weights.astype(jnp.bfloat16)
    attended = jnp.einsum("grqk,kgd->qgrd", probs, value_window, preferred_element_type=jnp.float32)
    delta = jnp.transpose(jnp.sum(grad_block.astype(jnp.float32) * attended, axis=-1), (1, 2, 0))
    weight_grads = jnp.einsum(
        "qgrd,kgd->grqk", grad_block, value_window, preferred_element_type=jnp.float32
    )
    score_grads = (weights * (weight_grads - delta[..., None])).astype(jnp.bfloat16)
    query_grad = (
        jnp.einsum("grqk,kgd->qgrd", score_grads, key_window, preferred_element_type=jnp.float32)
        * scale
    )
    key_grad = (
        jnp.einsum("grqk,qgrd->kgd", score_grads, query_block, preferred_element_type=jnp.float32)
        * scale
    )
    value_grad = jnp.einsum("grqk,qgrd->kgd", probs, grad_block, preferred_element_type=jnp.float32)
    return (log_total[..., 0], delta, query_grad, key_grad, value_grad)


def body(query_raw, key_raw, value_in, out_grad, query_gain, key_gain, doc_blocks):
    seq_count = lax.axis_size("seq")
    seq_at = lax.axis_index("seq")
    total = 2 * seq_count
    query_rows = query_raw[0]
    key_rows = key_raw[0]
    query_norm, query_inverse = normalize(query_rows, query_gain)
    key_norm, key_inverse = normalize(key_rows, key_gain)
    moved = (
        lax.all_to_all(query_norm[None], "head", split_axis=2, concat_axis=1, tiled=True),
        lax.all_to_all(key_norm[None], "head", split_axis=2, concat_axis=1, tiled=True),
        lax.all_to_all(value_in, "head", split_axis=2, concat_axis=1, tiled=True),
        lax.all_to_all(out_grad, "head", split_axis=2, concat_axis=1, tiled=True),
    )
    length = moved[1].shape[1] // 2
    kv_local = moved[1].shape[2] // HEAD_DIM
    limit = total * length
    query_tail = (kv_local, GROUP, HEAD_DIM)
    key_tail = (kv_local, HEAD_DIM)

    def halves(array, tail):
        split_up = array[0].reshape((2, length) + tail)
        return (split_up[0], split_up[1])

    query_first, query_far = halves(moved[0], query_tail)
    key_first, key_far = halves(moved[1], key_tail)
    value_first, value_far = halves(moved[2], key_tail)
    grad_first, grad_far = halves(moved[3], query_tail)
    ends = jnp.cumsum(doc_blocks)
    far_index = total - 1 - seq_at
    middle = seq_at == seq_count - 1
    carry_first = jnp.stack([key_first, value_first])
    carry_far = jnp.stack([key_far, value_far])
    windows_first = [carry_first]
    windows_far = [carry_far]
    for repeat in range(REACH):
        got_first = from_behind(carry_first, "seq", 1)
        got_far = from_behind(carry_far, "seq", -1)
        carry_far = jnp.where(middle, carry_first, got_far)
        carry_first = got_first
        windows_first.insert(0, carry_first)
        windows_far.insert(0, carry_far)
    window_first = jnp.concatenate(windows_first, axis=1)
    window_far = jnp.concatenate(windows_far, axis=1)

    def query_pass(index, query_block, grad_block, window):
        query_places, query_docs = span_labels(index * length, length, limit, ends, -2)
        key_places, key_docs = span_labels(
            (index - REACH) * length, length * (REACH + 1), limit, ends, -1
        )
        allowed = allowed_pairs(query_places, query_docs, key_places, key_docs)
        return attend(query_block, grad_block, window[0], window[1], allowed)

    log_first, delta_first, qgrad_first, kpart_first, vpart_first = query_pass(
        seq_at, query_first, grad_first, window_first
    )
    log_far, delta_far, qgrad_far, kpart_far, vpart_far = query_pass(
        far_index, query_far, grad_far, window_far
    )
    stacked_first = jnp.stack([kpart_first, vpart_first]).reshape(
        2, REACH + 1, length, kv_local, HEAD_DIM
    )
    stacked_far = jnp.stack([kpart_far, vpart_far]).reshape(
        2, REACH + 1, length, kv_local, HEAD_DIM
    )
    summed_first = jnp.zeros((2, length, kv_local, HEAD_DIM), jnp.float32)
    summed_far = jnp.zeros((2, length, kv_local, HEAD_DIM), jnp.float32)
    for offset in range(REACH, 0, -1):
        summed_first = summed_first + stacked_first[:, REACH - offset]
        summed_far = summed_far + stacked_far[:, REACH - offset]
        back_first = from_behind(summed_first, "seq", -1)
        back_far = from_behind(summed_far, "seq", 1)
        summed_first = jnp.where(middle, summed_far, back_first)
        summed_far = back_far
    own_first = summed_first + stacked_first[:, REACH]
    own_far = summed_far + stacked_far[:, REACH]
    query_flat = (2 * length, kv_local * GROUP * HEAD_DIM)
    key_flat = (2 * length, kv_local * HEAD_DIM)
    query_grads = (
        jnp.concatenate([qgrad_first, qgrad_far], axis=0).reshape(query_flat).astype(jnp.bfloat16)
    )
    key_grads = (
        jnp.concatenate([own_first[0], own_far[0]], axis=0).reshape(key_flat).astype(jnp.bfloat16)
    )
    value_grads = (
        jnp.concatenate([own_first[1], own_far[1]], axis=0).reshape(key_flat).astype(jnp.bfloat16)
    )
    back = (
        lax.all_to_all(query_grads[None], "head", split_axis=1, concat_axis=2, tiled=True),
        lax.all_to_all(key_grads[None], "head", split_axis=1, concat_axis=2, tiled=True),
        lax.all_to_all(value_grads[None], "head", split_axis=1, concat_axis=2, tiled=True),
    )
    d_query, query_gain_part = norm_backward(query_rows, query_inverse, query_gain, back[0][0])
    d_key, key_gain_part = norm_backward(key_rows, key_inverse, key_gain, back[1][0])
    gains = lax.psum((query_gain_part, key_gain_part), ("seq", "head"))
    return (d_query[None], d_key[None], back[2], gains[0], gains[1])


def solution(mesh):
    in_specs = (
        P("seq", "head", None),
        P("seq", "head", None),
        P("seq", "head", None),
        P("seq", "head", None),
        P(),
        P(),
        P(),
    )
    out_specs = (P("seq", "head", None), P("seq", "head", None), P("seq", "head", None), P(), P())
    return jax.shard_map(body, mesh=mesh, in_specs=in_specs, out_specs=out_specs, check_vma=False)
```

profile of v0, /device:TPU:1, one launch (start us, length us, event | category | flops | bytes accessed | tf_op | source)
XLA Modules:
  0.0 430.3 jit_solution(4244944374695996867)
XLA Ops:
  6.9 11.1 %all-to-all-start = ((bf16[8,2,4096]{2,1,0:T(2,128)(2,1)}), bf16[8,2,4096]{2,1,0:T(2,128)(2,1)}, u32[]{:S(2)}, u32[]{:S(2)}) async-start(bf16[8,2,4096]{2,1,0:T(2,128)(2,1)} %reshape.828), calls=%async_computation | async-start | bytes 262144 | tf_op jit(solution)/shard_map/all_to_all | solution.py:93
  24.4 4.7 %copy.337 = bf16[1,64,5120]{1,0,2:T(2,128)(2,1)S(1)} copy(bf16[1,64,5120]{2,1,0:T(8,128)(2,1)} %multiply_convert_fusion) | data formatting | bytes 1310720 | tf_op jit(solution)/shard_map/convert_element_type | solution.py:27
  29.1 28.9 %reduce.13 = bf16[5120,64]{1,0:T(8,128)(2,1)} reduce(bf16[5120,1,64]{2,1,0:T(2,128)(2,1)S(1)} %bitcast.370, bf16[]{:T(256)} %broadcast.556), dimensions={1}, to_apply=%bitcast.335.reduce_sub_computation | reduce | bytes 1310722
  61.4 4.7 %copy.341 = bf16[1,64,5120]{1,0,2:T(2,128)(2,1)S(1)} copy(bf16[1,64,5120]{2,1,0:T(8,128)(2,1)} %param.10) | data formatting | bytes 1310720 | tf_op args[3]
  66.1 29.4 %reduce.16 = bf16[5120,64]{1,0:T(8,128)(2,1)} reduce(bf16[5120,1,64]{2,1,0:T(2,128)(2,1)S(1)} %bitcast.373, bf16[]{:T(256)} %broadcast.556), dimensions={1}, to_apply=%bitcast.341.reduce_sub_computation | reduce | bytes 1310722
  99.2 5.1 %all-to-all-start.1 = ((bf16[8,2,4096]{2,1,0:T(2,128)(2,1)}), bf16[8,2,4096]{2,1,0:T(2,128)(2,1)S(1)}, u32[]{:S(2)}, u32[]{:S(2)}) async-start(bf16[8,2,4096]{2,1,0:T(2,128)(2,1)} %reshape.826), calls=%async_computation.1 | async-start | bytes 262144 | tf_op jit(solution)/shard_map/all_to_all | solution.py:94
  105.9 4.2 all-to-all-done.1
  110.1 4.4 %all-to-all-start.2 = ((bf16[8,2,20480]{2,1,0:T(2,128)(2,1)}), bf16[8,2,20480]{2,1,0:T(2,128)(2,1)S(1)}, u32[]{:S(2)}, u32[]{:S(2)}) async-start(bf16[8,2,20480]{2,1,0:T(2,128)(2,1)} %reshape.824), calls=%async_computation.2 | async-start | bytes 1310720 | tf_op jit(solution)/shard_map/all_to_all | solution.py:92
  116.7 5.5 %collective-permute-done.2 = bf16[2,256,1,128]{3,1,2,0:T(8,128)(2,1)S(1)} collective-permute-done((bf16[2,256,1,128]{3,1,2,0:T(8,128)(2,1)S(1)}, bf16[2,256,1,128]{3,1,2,0:T(8,128)(2,1)S(1)}, u32[]{:S(2)}, u32[]{:S(2)}) %collective-permute-start.2) | collective-permute-done | bytes 131104 | tf_op jit(solution)/shard_map/ppermute | solution.py:21
  125.8 4.0 collective-permute-start.1
  133.3 7.3 %all-to-all-start.3 = ((bf16[8,2,20480]{2,1,0:T(2,128)(2,1)}), bf16[8,2,20480]{2,1,0:T(2,128)(2,1)}, u32[]{:S(2)}, u32[]{:S(2)}) async-start(bf16[8,2,20480]{2,1,0:T(2,128)(2,1)} %reshape.830), calls=%async_computation.3 | async-start | bytes 1310720 | tf_op jit(solution)/shard_map/all_to_all | solution.py:95
  140.6 4.4 %reshape.825 = bf16[5120,1,64]{2,1,0:T(2,128)(2,1)S(1)} reshape(bf16[8,2,20480]{2,1,0:T(2,128)(2,1)} %copy-done.10) | data formatting | bytes 1310720
  158.0 4.4 %reshape.831 = bf16[5120,1,64]{2,1,0:T(2,128)(2,1)S(1)} reshape(bf16[8,2,20480]{2,1,0:T(2,128)(2,1)} %all-to-all-done.3) | data formatting | bytes 1310720
  195.8 3.6 fusion.45
  209.5 5.0 %collective-permute-start.4 = (f32[2,256,1,128]{3,1,0,2:T(8,128)S(1)}, f32[2,256,1,128]{3,1,0,2:T(8,128)S(1)}, u32[]{:S(2)}, u32[]{:S(2)}) collective-permute-start(f32[2,256,1,128]{3,1,0,2:T(8,128)S(1)} %get-tuple-element.38), channel_id=1, source_target_pairs={{0,8},{8,16},{16,24},{24,32},{32,40},{40,48},{48,56},{56,64},{64,7... | collective-permute-start | bytes 786440 | tf_op jit(solution)/shard_map/ppermute | solution.py:21
  219.2 4.8 %collective-permute-done.6 = f32[2,256,1,128]{3,1,0,2:T(8,128)S(1)} collective-permute-done((f32[2,256,1,128]{3,1,0,2:T(8,128)S(1)}, f32[2,256,1,128]{3,1,0,2:T(8,128)S(1)}, u32[]{:S(2)}, u32[]{:S(2)}) %collective-permute-start.6) | collective-permute-done | bytes 262176 | tf_op jit(solution)/shard_map/ppermute | solution.py:21
  224.1 7.7 %collective-permute-start.7 = (f32[2,256,1,128]{3,1,0,2:T(8,128)S(1)}, f32[2,256,1,128]{3,1,0,2:T(8,128)S(1)}, u32[]{:S(2)}, u32[]{:S(2)}) collective-permute-start(f32[2,256,1,128]{3,1,0,2:T(8,128)S(1)} %get-tuple-element.36), channel_id=1, source_target_pairs={{0,8},{8,16},{16,24},{24,32},{32,40},{40,48},{48,56},{56,64},{64,7... | collective-permute-start | bytes 786440 | tf_op jit(solution)/shard_map/ppermute | solution.py:21
  231.9 3.8 collective-permute-done.7
  238.7 6.0 %all-to-all-start.5 = ((bf16[8,2,4096]{2,1,0:T(2,128)(2,1)}), bf16[8,2,4096]{2,1,0:T(2,128)(2,1)S(1)}, u32[]{:S(2)}, u32[]{:S(2)}) async-start(bf16[8,2,4096]{2,1,0:T(2,128)(2,1)} %reshape.834), calls=%async_computation.5 | async-start | bytes 262144 | tf_op jit(solution)/shard_map/all_to_all | solution.py:172
  250.5 5.2 %all-to-all-start.6 = ((bf16[8,2,4096]{2,1,0:T(2,128)(2,1)}), bf16[8,2,4096]{2,1,0:T(2,128)(2,1)}, u32[]{:S(2)}, u32[]{:S(2)}) async-start(bf16[8,2,4096]{2,1,0:T(2,128)(2,1)} %reshape.836), calls=%async_computation.6 | async-start | bytes 262144 | tf_op jit(solution)/shard_map/all_to_all | solution.py:173
  258.9 4.6 %reduce.17 = bf16[512,640]{1,0:T(8,128)(2,1)S(1)} reduce(bf16[512,1,640]{2,1,0:T(2,128)(2,1)S(1)} %bitcast.383, bf16[]{:T(256)} %broadcast.556), dimensions={1}, to_apply=%bitcast.343.reduce_sub_computation | reduce | bytes 1310722
  264.5 5.3 %all-to-all-start.4 = ((bf16[8,2,20480]{2,1,0:T(2,128)(2,1)}), bf16[8,2,20480]{2,1,0:T(2,128)(2,1)S(1)}, u32[]{:S(2)}, u32[]{:S(2)}) async-start(bf16[8,2,20480]{2,1,0:T(2,128)(2,1)} %reshape.832), calls=%async_computation.4 | async-start | bytes 1310720 | tf_op jit(solution)/shard_map/all_to_all | solution.py:171
  277.6 9.5 %all-to-all-done.4 = bf16[8,2,20480]{2,1,0:T(2,128)(2,1)S(1)} async-done(((bf16[8,2,20480]{2,1,0:T(2,128)(2,1)}), bf16[8,2,20480]{2,1,0:T(2,128)(2,1)S(1)}, u32[]{:S(2)}, u32[]{:S(2)}) %all-to-all-start.4) | async-done | bytes 655392 | tf_op jit(solution)/shard_map/all_to_all | solution.py:171
  291.1 137.7 %all-reduce = (f32[5120]{0:T(1024)}, f32[1024]{0:T(1024)}) all-reduce(f32[5120]{0:T(1024)S(1)} %reduce_sum.149, f32[1024]{0:T(1024)S(1)} %bitcast.422), channel_id=1, replica_groups=mesh['seq'=64,'head'=8] {'seq','head'}, use_global_device_ids=true, to_apply=%region_16.17 | all-reduce | flops 6144 | bytes 49152 | tf_op jit(solution)/shard_map/psum | solution.py:177
  (194 shorter events, 117.1 us)
Async XLA Ops:
  0.6 21.8 %copy-start.28 = (s32[96]{0:T(128)S(1)}, s32[96]{0:T(128)}, u32[]{:S(2)}) copy-start(s32[96]{0:T(128)} %param.13) | copy-start | bytes 1156
  0.6 22.5 %copy-start.4 = (bf16[1,64,5120]{2,1,0:T(8,128)(2,1)S(1)}, bf16[1,64,5120]{2,1,0:T(8,128)(2,1)}, u32[]{:S(2)}) copy-start(bf16[1,64,5120]{2,1,0:T(8,128)(2,1)} %param.7) | copy-start | bytes 1966084
  0.7 22.7 %copy-start.23 = (f32[5120]{0:T(1024)S(1)}, f32[5120]{0:T(1024)}, u32[]{:S(2)}) copy-start(f32[5120]{0:T(1024)} %param.11) | copy-start | bytes 61444
  6.9 92.3 %all-to-all-start = ((bf16[8,2,4096]{2,1,0:T(2,128)(2,1)}), bf16[8,2,4096]{2,1,0:T(2,128)(2,1)}, u32[]{:S(2)}, u32[]{:S(2)}) async-start(bf16[8,2,4096]{2,1,0:T(2,128)(2,1)} %reshape.828), calls=%async_computation | async-start | bytes 262144 | tf_op jit(solution)/shard_map/all_to_all | solution.py:93
  99.2 68.0 %copy-start.12 = (pred[256,768]{0,1:T(8,128)(4,1)}, pred[256,768]{0,1:T(8,128)(4,1)S(1)}, u32[]{:S(2)}) copy-start(pred[256,768]{0,1:T(8,128)(4,1)S(1)} %compare_and_fusion.1) | copy-start | bytes 589828
  99.2 11.0 %all-to-all-start.1 = ((bf16[8,2,4096]{2,1,0:T(2,128)(2,1)}), bf16[8,2,4096]{2,1,0:T(2,128)(2,1)S(1)}, u32[]{:S(2)}, u32[]{:S(2)}) async-start(bf16[8,2,4096]{2,1,0:T(2,128)(2,1)} %reshape.826), calls=%async_computation.1 | async-start | bytes 262144 | tf_op jit(solution)/shard_map/all_to_all | solution.py:94
  110.1 22.4 %all-to-all-start.2 = ((bf16[8,2,20480]{2,1,0:T(2,128)(2,1)}), bf16[8,2,20480]{2,1,0:T(2,128)(2,1)S(1)}, u32[]{:S(2)}, u32[]{:S(2)}) async-start(bf16[8,2,20480]{2,1,0:T(2,128)(2,1)} %reshape.824), calls=%async_computation.2 | async-start | bytes 1310720 | tf_op jit(solution)/shard_map/all_to_all | solution.py:92
  115.4 6.9 %collective-permute-start.2 = (bf16[2,256,1,128]{3,1,2,0:T(8,128)(2,1)S(1)}, bf16[2,256,1,128]{3,1,2,0:T(8,128)(2,1)S(1)}, u32[]{:S(2)}, u32[]{:S(2)}) collective-permute-start(bf16[2,256,1,128]{3,1,2,0:T(8,128)(2,1)S(1)} %pad_maximum_fusion.4), channel_id=1, source_target_pairs={{8,0},{16,8},{24,16},{32,24},{40,32},{48,40},{56,48},{64,56},{72,6... | collective-permute-start | bytes 393224 | tf_op jit(solution)/shard_map/ppermute | solution.py:21
  122.2 3.6 collective-permute-start
  123.5 6.3 %collective-permute-start.3 = (bf16[2,256,1,128]{3,1,2,0:T(8,128)(2,1)S(1)}, bf16[2,256,1,128]{3,1,2,0:T(8,128)(2,1)S(1)}, u32[]{:S(2)}, u32[]{:S(2)}) collective-permute-start(bf16[2,256,1,128]{3,1,2,0:T(8,128)(2,1)S(1)} %get-tuple-element.52), channel_id=1, source_target_pairs={{8,0},{16,8},{24,16},{32,24},{40,32},{48,40},{56,48},{64,56},{72,6... | collective-permute-start | bytes 393224 | tf_op jit(solution)/shard_map/ppermute | solution.py:21
  125.8 5.9 %collective-permute-start.1 = (bf16[2,256,1,128]{3,1,2,0:T(8,128)(2,1)S(1)}, bf16[2,256,1,128]{3,1,2,0:T(8,128)(2,1)S(1)}, u32[]{:S(2)}, u32[]{:S(2)}) collective-permute-start(bf16[2,256,1,128]{3,1,2,0:T(8,128)(2,1)S(1)} %collective-permute-done), channel_id=1, source_target_pairs={{0,8},{8,16},{16,24},{24,32},{32,40},{40,48},{48,56},{56,64},{64,7... | collective-permute-start | bytes 393224 | tf_op jit(solution)/shard_map/ppermute | solution.py:21
  133.3 24.6 %all-to-all-start.3 = ((bf16[8,2,20480]{2,1,0:T(2,128)(2,1)}), bf16[8,2,20480]{2,1,0:T(2,128)(2,1)}, u32[]{:S(2)}, u32[]{:S(2)}) async-start(bf16[8,2,20480]{2,1,0:T(2,128)(2,1)} %reshape.830), calls=%async_computation.3 | async-start | bytes 1310720 | tf_op jit(solution)/shard_map/all_to_all | solution.py:95
  179.1 29.4 %collective-permute-start.5 = (f32[2,256,1,128]{3,1,0,2:T(8,128)}, f32[2,256,1,128]{3,1,0,2:T(8,128)}, u32[]{:S(2)}, u32[]{:S(2)}) collective-permute-start(f32[2,256,1,128]{3,1,0,2:T(8,128)} %fusion.76), channel_id=1, source_target_pairs={{8,0},{16,8},{24,16},{32,24},{40,32},{48,40},{56,48},{64,56},{72,6... | collective-permute-start | bytes 786440 | tf_op jit(solution)/shard_map/ppermute | solution.py:21
  209.5 9.7 %collective-permute-start.4 = (f32[2,256,1,128]{3,1,0,2:T(8,128)S(1)}, f32[2,256,1,128]{3,1,0,2:T(8,128)S(1)}, u32[]{:S(2)}, u32[]{:S(2)}) collective-permute-start(f32[2,256,1,128]{3,1,0,2:T(8,128)S(1)} %get-tuple-element.38), channel_id=1, source_target_pairs={{0,8},{8,16},{16,24},{24,32},{32,40},{40,48},{48,56},{56,64},{64,7... | collective-permute-start | bytes 786440 | tf_op jit(solution)/shard_map/ppermute | solution.py:21
  214.5 9.5 %collective-permute-start.6 = (f32[2,256,1,128]{3,1,0,2:T(8,128)S(1)}, f32[2,256,1,128]{3,1,0,2:T(8,128)S(1)}, u32[]{:S(2)}, u32[]{:S(2)}) collective-permute-start(f32[2,256,1,128]{3,1,0,2:T(8,128)S(1)} %get-tuple-element.37), channel_id=1, source_target_pairs={{8,0},{16,8},{24,16},{32,24},{40,32},{48,40},{56,48},{64,56},{72,6... | collective-permute-start | bytes 786440 | tf_op jit(solution)/shard_map/ppermute | solution.py:21
  224.1 31.5 %copy-start.16 = (bf16[2,768,1,128]{3,1,2,0:T(8,128)(2,1)S(1)}, bf16[2,768,1,128]{3,1,2,0:T(8,128)(2,1)}, u32[]{:S(2)}) copy-start(bf16[2,768,1,128]{3,1,2,0:T(8,128)(2,1)} %maximum_maximum_fusion.1) | copy-start | bytes 1179652
  224.1 11.5 %collective-permute-start.7 = (f32[2,256,1,128]{3,1,0,2:T(8,128)S(1)}, f32[2,256,1,128]{3,1,0,2:T(8,128)S(1)}, u32[]{:S(2)}, u32[]{:S(2)}) collective-permute-start(f32[2,256,1,128]{3,1,0,2:T(8,128)S(1)} %get-tuple-element.36), channel_id=1, source_target_pairs={{0,8},{8,16},{16,24},{24,32},{32,40},{40,48},{48,56},{56,64},{64,7... | collective-permute-start | bytes 786440 | tf_op jit(solution)/shard_map/ppermute | solution.py:21
  238.7 11.8 %all-to-all-start.5 = ((bf16[8,2,4096]{2,1,0:T(2,128)(2,1)}), bf16[8,2,4096]{2,1,0:T(2,128)(2,1)S(1)}, u32[]{:S(2)}, u32[]{:S(2)}) async-start(bf16[8,2,4096]{2,1,0:T(2,128)(2,1)} %reshape.834), calls=%async_computation.5 | async-start | bytes 262144 | tf_op jit(solution)/shard_map/all_to_all | solution.py:172
  250.5 13.0 %copy-start.20 = (bf16[8,2,4096]{2,1,0:T(2,128)(2,1)}, bf16[8,2,4096]{2,1,0:T(2,128)(2,1)S(1)}, u32[]{:S(2)}) copy-start(bf16[8,2,4096]{2,1,0:T(2,128)(2,1)S(1)} %all-to-all-done.5) | copy-start | bytes 393220
  250.5 14.1 %all-to-all-start.6 = ((bf16[8,2,4096]{2,1,0:T(2,128)(2,1)}), bf16[8,2,4096]{2,1,0:T(2,128)(2,1)}, u32[]{:S(2)}, u32[]{:S(2)}) async-start(bf16[8,2,4096]{2,1,0:T(2,128)(2,1)} %reshape.836), calls=%async_computation.6 | async-start | bytes 262144 | tf_op jit(solution)/shard_map/all_to_all | solution.py:173
  257.7 12.8 %copy-start.11 = (bf16[1,64,1024]{2,1,0:T(8,128)(2,1)S(1)}, bf16[1,64,1024]{2,1,0:T(8,128)(2,1)}, u32[]{:S(2)}) copy-start(bf16[1,64,1024]{2,1,0:T(8,128)(2,1)} %param.8) | copy-start | bytes 393220
  264.5 22.6 %all-to-all-start.4 = ((bf16[8,2,20480]{2,1,0:T(2,128)(2,1)}), bf16[8,2,20480]{2,1,0:T(2,128)(2,1)S(1)}, u32[]{:S(2)}, u32[]{:S(2)}) async-start(bf16[8,2,20480]{2,1,0:T(2,128)(2,1)} %reshape.832), calls=%async_computation.4 | async-start | bytes 1310720 | tf_op jit(solution)/shard_map/all_to_all | solution.py:171
  277.6 12.9 %copy-start.26 = (f32[8,640]{1,0:T(8,128)S(1)}, f32[8,640]{1,0:T(8,128)}, u32[]{:S(2)}) copy-start(f32[8,640]{1,0:T(8,128)} %mul.312) | copy-start | bytes 61444
  289.0 139.8 %copy-start.25 = (f32[5120]{0:T(1024)S(1)}, f32[5120]{0:T(1024)}, u32[]{:S(2)}) copy-start(f32[5120]{0:T(1024)} %param.11) | copy-start | bytes 61444
  (20 other events, 84.2 us)
where the time goes:
time: 435 us; the launch traced here: 430 us
  blocking collectives  138 us (32%)
  other arithmetic  87.8 us (20%)
  local copies, waits for them, and re-layouts  73.4 us (17%)
  starting transfers between devices  67.6 us (16%)
  waiting for transfers between devices  36.1 us (8%)
  matrix products  25.9 us (6%)
    psum x1, blocking collectives, body(): gains = lax.psum((query_gain_part, key_gain_part), ('seq', 'head'))  138 us
    unnamed x9, other arithmetic  71.8 us
    unnamed x81, local copies, waits for them, and re-layouts  40.9 us
    ppermute x8, starting transfers between devices, from_behind(): lax.ppermute(value, axis, [(source, source + steps) for source in range(l...  23.3 us
    ppermute x8, waiting for transfers between devices, from_behind(): lax.ppermute(value, axis, [(source, source + steps) for source in range(l...  18.6 us
    all_to_all x1, starting transfers between devices, body(): lax.all_to_all(key_norm[None], 'head', split_axis=2, concat_axis=1, tiled...  11.1 us
    all_to_all x1, waiting for transfers between devices, body(): lax.all_to_all(query_grads[None], 'head', split_axis=1, concat_axis=2, ti...  9.52 us
  transfers between devices with their start and end apart: 15, of which 9 were waited for; matrix products, arithmetic and copies ran while one was open for 34% of the time, Pallas kernels for 0%

commit v1 on v0

v1 whole, which is shorter than its diff:
```python
import functools
import math

import jax
import jax.numpy as jnp
from jax import lax
from jax.experimental import pallas as pl
from jax.experimental.pallas import tpu as pltpu
from jax.sharding import PartitionSpec as P

GROUP = 5
HEAD_DIM = 128
BLOCK = 128
EPSILON = 1e-06
MASKED = -1e30
TEAM = 4
KV_EACH = 2
KV_COLS = KV_EACH * HEAD_DIM
Q_COLS = KV_EACH * GROUP * HEAD_DIM
SCALE = 1.0 / math.sqrt(HEAD_DIM)
LOG2E = math.log2(math.e)
F32 = jnp.float32
BF16 = jnp.bfloat16
VMEM_LIMIT = 48 * 1024 * 1024


def call(kernel, out_shape, args, smem=0, flops=0, size=0, scratch=()):
    whole = pl.BlockSpec(memory_space=pltpu.VMEM)
    scalar = pl.BlockSpec(memory_space=pltpu.SMEM)
    single = not isinstance(out_shape, (tuple, list))
    return pl.pallas_call(
        kernel,
        out_shape=out_shape,
        in_specs=[scalar] * smem + [whole] * (len(args) - smem),
        out_specs=whole if single else [whole] * len(out_shape),
        scratch_shapes=list(scratch),
        compiler_params=pltpu.CompilerParams(vmem_limit_bytes=VMEM_LIMIT),
        cost_estimate=pl.CostEstimate(flops=flops, bytes_accessed=size, transcendentals=0),
    )(*args)


def inverse_rms(values):
    return lax.rsqrt(jnp.mean(values * values, axis=-1, keepdims=True) + EPSILON)


def key_norm_kernel(key_ref, value_ref, gain_ref, out_ref):
    values = key_ref[...].astype(F32)
    normed = (values * inverse_rms(values) * gain_ref[...]).astype(BF16)
    for to in range(TEAM):
        columns = slice(to * KV_COLS, (to + 1) * KV_COLS)
        out_ref[to, :, :KV_COLS] = normed[:, columns]
        out_ref[to, :, KV_COLS:] = value_ref[:, columns]


def query_norm_kernel(segment_ref, query_ref, grad_ref, gain_ref, docs_ref, out_ref, flags_ref):
    values = query_ref[...].astype(F32)
    normed = (values * inverse_rms(values) * gain_ref[...]).astype(BF16)
    for to in range(TEAM):
        columns = slice(to * Q_COLS, (to + 1) * Q_COLS)
        out_ref[to, :, :Q_COLS] = normed[:, columns]
        out_ref[to, :, Q_COLS:] = grad_ref[:, columns]
    lengths = docs_ref[...]
    count = lengths.shape[1]
    earlier = lax.broadcasted_iota(jnp.int32, (count, count), 1) <= lax.broadcasted_iota(
        jnp.int32, (count, count), 0
    )
    ends = jnp.sum(jnp.where(earlier, lengths, 0), axis=1, keepdims=True)
    first = 2 * segment_ref[0] - 3
    places = first + lax.broadcasted_iota(jnp.int32, (count, 128), 1)
    found = jnp.sum((ends <= places).astype(jnp.int32), axis=0, keepdims=True)
    found = jnp.where(places[:1] >= 0, found, -1)
    flags_ref[...] = jnp.zeros_like(flags_ref)
    for at in range(5):
        flags_ref[at : at + 1, :] = jnp.broadcast_to(found[:, at : at + 1], (1, 128))


def contract(left, right, dims):
    return lax.dot_general(left, right, (dims, ((), ())), preferred_element_type=F32)


def attention_kernel(
    qd_ref,
    own_ref,
    near_ref,
    far_ref,
    flags_ref,
    query_gain_ref,
    key_gain_ref,
    dq_ref,
    d_own_ref,
    d_near_ref,
    d_far_ref,
    q_part_ref,
    k_part_ref,
    s_ref,
    g_ref,
    p_ref,
    ds_ref,
):
    def window(at, kind, head):
        columns = slice(kind * KV_COLS + head * HEAD_DIM, kind * KV_COLS + (head + 1) * HEAD_DIM)
        if at == 0:
            return far_ref[:, columns]
        ref = near_ref if at < 3 else own_ref
        row = (at - 1) % 2 * BLOCK
        return ref[row : row + BLOCK, columns]

    causal = lax.broadcasted_iota(jnp.int32, (BLOCK, BLOCK), 0) <= lax.broadcasted_iota(
        jnp.int32, (BLOCK, BLOCK), 1
    )
    diagonal = jnp.where(causal, 0.0, MASKED)
    factor = SCALE * LOG2E
    for head in range(KV_EACH):
        d_keys = [None] * 5
        d_values = [None] * 5
        q_part = [0.0] * GROUP
        for z in range(2):
            rows = slice(z * BLOCK, (z + 1) * BLOCK)
            blocks = list(range(z, z + 4))

            def heads_of(kind):
                base = kind * Q_COLS + head * GROUP * HEAD_DIM
                return jnp.concatenate(
                    [
                        qd_ref[rows, base + j * HEAD_DIM : base + (j + 1) * HEAD_DIM]
                        for j in range(GROUP)
                    ],
                    axis=0,
                )

            queries, grads = heads_of(0), heads_of(1)
            keys = jnp.concatenate([window(at, 0, head) for at in blocks], axis=0)
            values = jnp.concatenate([window(at, 1, head) for at in blocks], axis=0)
            s_ref[...] = contract(keys, queries, ((1,), (1,)))
            g_ref[...] = contract(values, grads, ((1,), (1,)))
            biases = []
            for place, at in enumerate(blocks):
                if place == 3:
                    biases.append(diagonal)
                else:
                    same = flags_ref[at : at + 1, :] == flags_ref[3 + z : 4 + z, :]
                    biases.append(jnp.where(same, 0.0, MASKED))
            for j in range(GROUP):
                lanes = slice(j * HEAD_DIM, (j + 1) * HEAD_DIM)
                tiles = [
                    s_ref[place * BLOCK : (place + 1) * BLOCK, lanes] * factor + biases[place]
                    for place in range(4)
                ]
                highest = functools.reduce(
                    jnp.maximum, [jnp.max(t, axis=0, keepdims=True) for t in tiles]
                )
                tiles = [jnp.exp2(t - highest) for t in tiles]
                total = functools.reduce(
                    jnp.add, [jnp.sum(t, axis=0, keepdims=True) for t in tiles]
                )
                recip = 1.0 / total
                delta = 0.0
                kept = []
                for place in range(4):
                    span = slice(place * BLOCK, (place + 1) * BLOCK)
                    weights = tiles[place] * recip
                    probs = weights.astype(BF16)
                    p_ref[span, lanes] = probs
                    kept.append(weights)
                    delta = delta + jnp.sum(
                        probs.astype(F32) * g_ref[span, lanes], axis=0, keepdims=True
                    )
                for place in range(4):
                    span = slice(place * BLOCK, (place + 1) * BLOCK)
                    ds_ref[span, lanes] = (kept[place] * (g_ref[span, lanes] - delta)).astype(BF16)
            score_grads = ds_ref[...]
            d_key = contract(score_grads, queries, ((1,), (0,)))
            d_value = contract(p_ref[...], grads, ((1,), (0,)))
            for place, at in enumerate(blocks):
                span = slice(place * BLOCK, (place + 1) * BLOCK)
                first = d_keys[at] is None
                d_keys[at] = d_key[span] if first else d_keys[at] + d_key[span]
                d_values[at] = d_value[span] if first else d_values[at] + d_value[span]
            d_query = contract(jnp.transpose(keys), score_grads, ((1,), (0,)))
            for j in range(GROUP):
                lanes = slice(j * HEAD_DIM, (j + 1) * HEAD_DIM)
                grad = (jnp.transpose(d_query[:, lanes]) * SCALE).astype(BF16)
                base = (head * GROUP + j) * HEAD_DIM
                half = BLOCK // 2
                dq_ref[2 * z, :, base : base + HEAD_DIM] = grad[:half]
                dq_ref[2 * z + 1, :, base : base + HEAD_DIM] = grad[half:]
                normed = qd_ref[rows, base : base + HEAD_DIM].astype(F32)
                q_part[j] = q_part[j] + jnp.sum(grad.astype(F32) * normed, axis=0, keepdims=True)
        for j in range(GROUP):
            base = (head * GROUP + j) * HEAD_DIM
            lanes = slice(base, base + HEAD_DIM)
            q_part_ref[:, lanes] = q_part[j] / query_gain_ref[:, lanes]
        k_part = 0.0
        key_columns = slice(head * HEAD_DIM, (head + 1) * HEAD_DIM)
        value_columns = slice(KV_COLS + head * HEAD_DIM, KV_COLS + (head + 1) * HEAD_DIM)
        for at in range(5):
            grad = d_keys[at] * SCALE
            k_part = k_part + jnp.sum(
                grad * window(at, 0, head).astype(F32), axis=0, keepdims=True
            )
            if at == 0:
                target, row = d_far_ref, 0
            else:
                target, row = (d_near_ref if at < 3 else d_own_ref), (at - 1) % 2 * BLOCK
            target[row : row + BLOCK, key_columns] = grad.astype(target.dtype)
            target[row : row + BLOCK, value_columns] = d_values[at].astype(target.dtype)
        k_part_ref[:, key_columns] = k_part / key_gain_ref[:, key_columns]


def combine_kernel(own_ref, near_ref, far_ref, out_ref):
    half = BLOCK // 2
    for to in range(TEAM):
        rows = slice(to * half, (to + 1) * half)
        total = own_ref[rows] + near_ref[rows].astype(F32)
        if to >= 2:
            total = total + far_ref[(to - 2) * half : (to - 1) * half].astype(F32)
        out_ref[to] = total.astype(BF16)


def norm_backward(rows, gain, grad):
    values = rows.astype(F32)
    inverse = inverse_rms(values)
    scaled = grad.astype(F32) * gain
    inner = jnp.mean(scaled * values, axis=-1, keepdims=True)
    return (inverse * scaled - values * (inverse * inverse * inverse * inner)).astype(BF16)


def query_back_kernel(query_ref, gain_ref, grad_ref, out_ref):
    grad = jnp.concatenate([grad_ref[at] for at in range(TEAM)], axis=1)
    out_ref[...] = norm_backward(query_ref[...], gain_ref[...], grad)


def key_back_kernel(key_ref, gain_ref, grad_ref, d_key_ref, d_value_ref):
    grad = jnp.concatenate([grad_ref[at, :, :KV_COLS] for at in range(TEAM)], axis=1)
    d_key_ref[...] = norm_backward(key_ref[...], gain_ref[...], grad)
    for at in range(TEAM):
        d_value_ref[:, at * KV_COLS : (at + 1) * KV_COLS] = grad_ref[at, :, KV_COLS:]


def shift_pairs(seq_count, steps):
    last = 2 * seq_count - 1

    def place(segment, member):
        if segment < seq_count:
            return segment * 2 * TEAM + member
        return (last - segment) * 2 * TEAM + TEAM + member

    return [
        (place(segment, member), place(segment + steps, member))
        for segment in range(2 * seq_count - steps)
        for member in range(TEAM)
    ]


def body(query_raw, key_raw, value_in, out_grad, query_gain, key_gain, doc_blocks):
    seq_count = lax.axis_size("seq")
    seq_at = lax.axis_index("seq")
    head_at = lax.axis_index("head")
    member = head_at % TEAM
    segment = jnp.where(head_at < TEAM, seq_at, 2 * seq_count - 1 - seq_at)
    teams = [list(range(TEAM)), list(range(TEAM, 2 * TEAM))]
    axes = ("seq", "head")
    rows = query_raw.shape[1]
    query_rows, key_rows, value_rows, grad_rows = (
        query_raw[0],
        key_raw[0],
        value_in[0],
        out_grad[0],
    )
    query_gain_row, key_gain_row = query_gain[None], key_gain[None]

    def exchange(array):
        return lax.all_to_all(array, "head", 0, 0, axis_index_groups=teams)

    def sent(array, steps, back=False):
        pairs = shift_pairs(seq_count, steps)
        if back:
            pairs = [(target, source) for source, target in pairs]
        return lax.ppermute(array, axes, pairs)

    kv_send = call(
        key_norm_kernel,
        jax.ShapeDtypeStruct((TEAM, rows, 2 * KV_COLS), BF16),
        (key_rows, value_rows, key_gain_row),
        size=600_000,
    )
    own = exchange(kv_send).reshape(TEAM * rows, 2 * KV_COLS)
    far = sent(own[BLOCK:], 2)
    near = sent(own, 1)
    qd_send, flags = call(
        query_norm_kernel,
        (
            jax.ShapeDtypeStruct((TEAM, rows, 2 * Q_COLS), BF16),
            jax.ShapeDtypeStruct((8, 128), jnp.int32),
        ),
        (segment[None].astype(jnp.int32), query_rows, grad_rows, query_gain_row, doc_blocks[None]),
        smem=1,
        size=3_000_000,
    )
    qd = exchange(qd_send).reshape(TEAM * rows, 2 * Q_COLS)
    my_query_gain = lax.dynamic_slice_in_dim(query_gain_row, member * Q_COLS, Q_COLS, 1)
    my_key_gain = lax.dynamic_slice_in_dim(key_gain_row, member * KV_COLS, KV_COLS, 1)
    window = 4 * BLOCK
    wide = GROUP * HEAD_DIM
    dq_send, d_own, d_near, d_far, q_part, k_part = call(
        attention_kernel,
        (
            jax.ShapeDtypeStruct((TEAM, rows, Q_COLS), BF16),
            jax.ShapeDtypeStruct((2 * BLOCK, 2 * KV_COLS), F32),
            jax.ShapeDtypeStruct((2 * BLOCK, 2 * KV_COLS), BF16),
            jax.ShapeDtypeStruct((BLOCK, 2 * KV_COLS), BF16),
            jax.ShapeDtypeStruct((1, Q_COLS), F32),
            jax.ShapeDtypeStruct((1, KV_COLS), F32),
        ),
        (qd, own, near, far, flags, my_query_gain, my_key_gain),
        flops=2 * 5 * 4 * window * wide * HEAD_DIM,
        size=5_000_000,
        scratch=[
            pltpu.VMEM((window, wide), F32),
            pltpu.VMEM((window, wide), F32),
            pltpu.VMEM((window, wide), BF16),
            pltpu.VMEM((window, wide), BF16),
        ],
    )
    back_far = sent(d_far, 2, back=True)
    back_near = sent(d_near, 1, back=True)

    part = jnp.concatenate([q_part, k_part], axis=1)
    width = part.shape[1]
    copies = lax.all_to_all(jnp.broadcast_to(part, (seq_count, width)), "seq", 0, 0, tiled=True)
    part = jnp.sum(copies, axis=0, keepdims=True)
    gains = lax.all_to_all(jnp.broadcast_to(part, (2 * TEAM, width)), "head", 0, 0, tiled=True)
    gains = gains[:TEAM] + gains[TEAM:]

    dq = exchange(dq_send)
    d_query = call(
        query_back_kernel,
        jax.ShapeDtypeStruct(query_rows.shape, BF16),
        (query_rows, query_gain_row, dq),
        size=2_000_000,
    )
    kv_back = call(
        combine_kernel,
        jax.ShapeDtypeStruct((TEAM, rows, 2 * KV_COLS), BF16),
        (d_own, back_near, back_far),
        size=1_200_000,
    )
    d_kv = exchange(kv_back)
    d_key, d_value = call(
        key_back_kernel,
        (
            jax.ShapeDtypeStruct(key_rows.shape, BF16),
            jax.ShapeDtypeStruct(value_rows.shape, BF16),
        ),
        (key_rows, key_gain_row, d_kv),
        size=700_000,
    )
    return (
        d_query[None],
        d_key[None],
        d_value[None],
        gains[:, :Q_COLS].reshape(-1),
        gains[:, Q_COLS:].reshape(-1),
    )


def solution(mesh):
    split = P("seq", "head", None)
    in_specs = (split, split, split, split, P(), P(), P())
    out_specs = (split, split, split, P(), P())
    return jax.shard_map(body, mesh=mesh, in_specs=in_specs, out_specs=out_specs, check_vma=False)
```

time: 435 us -> 125 us (0.29)
  the two profiles are of different devices: /device:TPU:1 before, /device:TPU:26 now
where the time goes in v1:
time: 125 us
  starting transfers between devices  51.8 us (41%)
  waiting for transfers between devices  34.3 us (27%)
  blocking collectives  17.5 us (14%)
  Pallas kernels  11.9 us (10%)
  local copies, waits for them, and re-layouts  8.07 us (6%)
    all_to_all x1, starting transfers between devices, body(): lax.all_to_all(jnp.broadcast_to(part, (seq_count, width)), 'seq', 0, 0, t...  22.2 us
    all_to_all x4, waiting for transfers between devices, exchange(): return lax.all_to_all(array, 'head', 0, 0, axis_index_groups=teams)  17.6 us
    all_to_all x1, blocking collectives, body(): lax.all_to_all(jnp.broadcast_to(part, (2 * TEAM, width)), 'head', 0, 0, t...  17.5 us
    ppermute x4, waiting for transfers between devices, sent(): return lax.ppermute(array, axes, pairs)  16.6 us
    ppermute x4, starting transfers between devices, sent(): return lax.ppermute(array, axes, pairs)  15.4 us
    all_to_all x4, starting transfers between devices, exchange(): return lax.all_to_all(array, 'head', 0, 0, axis_index_groups=teams)  14.2 us
    pallas_call x6, Pallas kernels, call(): pl.pallas_call(kernel, out_shape=out_shape, in_specs=[scalar] * smem + [w...  11.9 us
    unnamed x25, local copies, waits for them, and re-layouts  6.3 us
  transfers between devices with their start and end apart: 9, of which 7 were waited for; matrix products, arithmetic and copies ran while one was open for 1% of the time, Pallas kernels for 2%

profile of v1, /device:TPU:26, one launch (start us, length us, event | category | flops | bytes accessed | tf_op | source)
XLA Modules:
  0.0 124.6 jit_solution(2335338299110415208)
XLA Ops:
  0.7 1.0 copy-done.2
  1.6 0.9 copy-done.4
  3.2 0.8 shard_map.111
  4.0 3.6 %all-to-all-start.1 = ((bf16[4,64,512]{2,1,0:T(8,128)(2,1)}), bf16[4,64,512]{2,1,0:T(8,128)(2,1)S(1)}, u32[]{:S(2)}, u32[]{:S(2)}) async-start(bf16[4,64,512]{2,1,0:T(8,128)(2,1)} %shard_map.111), calls=%async_computation.1 | async-start | bytes 524288 | tf_op jit(solution)/shard_map/all_to_all | solution.py:273
  7.7 1.1 copy-done.1
  10.1 1.5 %shard_map.110 = (bf16[4,64,2560]{2,1,0:T(8,128)(2,1)}, s32[8,128]{1,0:T(8,128)S(1)}) custom-call(s32[1]{0:T(128)} %bitcast.2.segment_ref, bf16[64,5120]{1,0:T(8,128)(2,1)S(1)} %bitcast.21, bf16[64,5120]{1,0:T(8,128)(2,1)S(1)} %bitcast.24, f32[1,5120]{1,0:T(1,128)S(1)} %bitcast.30, s32[1,96]{1,0:T(1,128)S(1)} %bitcast.35), custom_call_target="tpu_custom_call" | custom-call | bytes 3000000 | tf_op jit(solution)/shard_map/pallas_call | solution.py:31
  11.6 2.1 %all-to-all-done.1 = bf16[4,64,512]{2,1,0:T(8,128)(2,1)S(1)} async-done(((bf16[4,64,512]{2,1,0:T(8,128)(2,1)}), bf16[4,64,512]{2,1,0:T(8,128)(2,1)S(1)}, u32[]{:S(2)}, u32[]{:S(2)}) %all-to-all-start.1) | async-done | bytes 262176 | tf_op jit(solution)/shard_map/all_to_all | solution.py:273
  13.7 3.7 %all-to-all-start = ((bf16[4,64,2560]{2,1,0:T(8,128)(2,1)}), bf16[4,64,2560]{2,1,0:T(8,128)(2,1)S(1)}, u32[]{:S(2)}, u32[]{:S(2)}) async-start(bf16[4,64,2560]{2,1,0:T(8,128)(2,1)} %get-tuple-element.15), calls=%async_computation | async-start | bytes 2621440 | tf_op jit(solution)/shard_map/all_to_all | solution.py:273
  17.4 3.4 %collective-permute-start = (bf16[256,512]{1,0:T(8,128)(2,1)S(1)}, bf16[256,512]{1,0:T(8,128)(2,1)S(1)}, u32[]{:S(2)}, u32[]{:S(2)}) collective-permute-start(bf16[256,512]{1,0:T(8,128)(2,1)S(1)} %bitcast.25), channel_id=1, source_target_pairs={{0,8},{1,9},{2,10},{3,11},{8,16},{9,17},{10,18},{11,19},{16,24},{1... | collective-permute-start | bytes 786440 | tf_op jit(solution)/shard_map/ppermute | solution.py:279
  20.8 5.2 %collective-permute-start.1 = (bf16[128,512]{1,0:T(8,128)(2,1)S(1)}, bf16[128,512]{1,0:T(8,128)(2,1)S(1)}, u32[]{:S(2)}, u32[]{:S(2)}) collective-permute-start(bf16[128,512]{1,0:T(8,128)(2,1)S(1)} %bitcast.37), channel_id=1, source_target_pairs={{0,16},{1,17},{2,18},{3,19},{8,24},{9,25},{10,26},{11,27},{16,32},... | collective-permute-start | bytes 393224 | tf_op jit(solution)/shard_map/ppermute | solution.py:279
  26.3 6.7 %collective-permute-done.1.far_ref = bf16[128,512]{1,0:T(8,128)(2,1)S(1)} collective-permute-done((bf16[128,512]{1,0:T(8,128)(2,1)S(1)}, bf16[128,512]{1,0:T(8,128)(2,1)S(1)}, u32[]{:S(2)}, u32[]{:S(2)}) %collective-permute-start.1) | collective-permute-done | bytes 131104 | tf_op jit(solution)/shard_map/ppermute | solution.py:279
  33.0 1.7 %all-to-all-done = bf16[4,64,2560]{2,1,0:T(8,128)(2,1)S(1)} async-done(((bf16[4,64,2560]{2,1,0:T(8,128)(2,1)}), bf16[4,64,2560]{2,1,0:T(8,128)(2,1)S(1)}, u32[]{:S(2)}, u32[]{:S(2)}) %all-to-all-start) | async-done | bytes 1310752 | tf_op jit(solution)/shard_map/all_to_all | solution.py:273
  34.6 6.6 %shard_map.112 = (bf16[4,64,1280]{2,1,0:T(8,128)(2,1)}, f32[256,512]{1,0:T(8,128)S(1)}, bf16[256,512]{1,0:T(8,128)(2,1)S(1)}, bf16[128,512]{1,0:T(8,128)(2,1)S(1...) custom-call(bf16[256,2560]{1,0:T(8,128)(2,1)S(1)} %bitcast.23, bf16[256,512]{1,0:T(8,128)(2,1)S(1)} %bitcast.26, ...), custom_call_target="tpu_custom_call" | custom-call | flops 1677721600 | bytes 5000000 | tf_op jit(solution)/shard_map/pallas_call | solution.py:31
  41.9 1.0 broadcast_in_dim.39
  42.9 22.2 %all-to-all-start.4 = ((f32[64,1,1536]{2,1,0:T(1,128)}), f32[64,1,1536]{2,1,0:T(1,128)S(1)}, u32[]{:S(2)}, u32[]{:S(2)}) async-start(f32[64,1,1536]{2,1,0:T(1,128)} %broadcast_in_dim.39), calls=%async_computation.4 | async-start | bytes 786432 | tf_op jit(solution)/shard_map/all_to_all | solution.py:330
  65.0 2.5 %collective-permute-start.2 = (bf16[256,512]{1,0:T(8,128)(2,1)S(1)}, bf16[256,512]{1,0:T(8,128)(2,1)S(1)}, u32[]{:S(2)}, u32[]{:S(2)}) collective-permute-start(bf16[256,512]{1,0:T(8,128)(2,1)S(1)} %get-tuple-element.19), channel_id=1, source_target_pairs={{8,0},{9,1},{10,2},{11,3},{16,8},{17,9},{18,10},{19,11},{24,16},{2... | collective-permute-start | bytes 786440 | tf_op jit(solution)/shard_map/ppermute | solution.py:279
  67.5 4.3 %collective-permute-start.3 = (bf16[128,512]{1,0:T(8,128)(2,1)}, bf16[128,512]{1,0:T(8,128)(2,1)S(1)}, u32[]{:S(2)}, u32[]{:S(2)}) collective-permute-start(bf16[128,512]{1,0:T(8,128)(2,1)} %copy-done.10), channel_id=1, source_target_pairs={{16,0},{17,1},{18,2},{19,3},{24,8},{25,9},{26,10},{27,11},{32,16},... | collective-permute-start | bytes 393224 | tf_op jit(solution)/shard_map/ppermute | solution.py:279
  71.8 9.9 %collective-permute-done.3.far_ref = bf16[128,512]{1,0:T(8,128)(2,1)S(1)} collective-permute-done((bf16[128,512]{1,0:T(8,128)(2,1)}, bf16[128,512]{1,0:T(8,128)(2,1)S(1)}, u32[]{:S(2)}, u32[]{:S(2)}) %collective-permute-start.3) | collective-permute-done | bytes 131104 | tf_op jit(solution)/shard_map/ppermute | solution.py:279
  82.5 3.4 %all-to-all-start.3 = ((bf16[4,64,512]{2,1,0:T(8,128)(2,1)}), bf16[4,64,512]{2,1,0:T(8,128)(2,1)S(1)}, u32[]{:S(2)}, u32[]{:S(2)}) async-start(bf16[4,64,512]{2,1,0:T(8,128)(2,1)} %shard_map.114), calls=%async_computation.3 | async-start | bytes 524288 | tf_op jit(solution)/shard_map/all_to_all | solution.py:273
  86.2 5.8 %all-to-all-done.3.grad_ref = bf16[4,64,512]{2,1,0:T(8,128)(2,1)S(1)} async-done(((bf16[4,64,512]{2,1,0:T(8,128)(2,1)}), bf16[4,64,512]{2,1,0:T(8,128)(2,1)S(1)}, u32[]{:S(2)}, u32[]{:S(2)}) %all-to-all-start.3) | async-done | bytes 262176 | tf_op jit(solution)/shard_map/all_to_all | solution.py:273
  92.0 17.5 %all_to_all.32 = f32[8,1,1536]{2,1,0:T(1,128)S(1)} all-to-all(f32[8,1,1536]{2,1,0:T(1,128)S(1)} %broadcast_in_dim.40), channel_id=1, replica_groups=mesh['seq'=64,'head'=8] {'head'}, dimensions={0} | all-to-all | bytes 98304 | tf_op jit(solution)/shard_map/all_to_all | solution.py:332
  109.5 3.5 %all-to-all-start.2 = ((bf16[4,64,1280]{2,1,0:T(8,128)(2,1)}), bf16[4,64,1280]{2,1,0:T(8,128)(2,1)S(1)}, u32[]{:S(2)}, u32[]{:S(2)}) async-start(bf16[4,64,1280]{2,1,0:T(8,128)(2,1)} %get-tuple-element.17), calls=%async_computation.2 | async-start | bytes 1310720 | tf_op jit(solution)/shard_map/all_to_all | solution.py:273
  115.0 8.1 %all-to-all-done.2.grad_ref = bf16[4,64,1280]{2,1,0:T(8,128)(2,1)S(1)} async-done(((bf16[4,64,1280]{2,1,0:T(8,128)(2,1)}), bf16[4,64,1280]{2,1,0:T(8,128)(2,1)S(1)}, u32[]{:S(2)}, u32[]{:S(2)}) %all-to-all-start.2) | async-done | bytes 655392 | tf_op jit(solution)/shard_map/all_to_all | solution.py:273
  123.2 1.4 %shard_map.113 = bf16[64,5120]{1,0:T(8,128)(2,1)} custom-call(bf16[64,5120]{1,0:T(8,128)(2,1)S(1)} %bitcast.22, f32[1,5120]{1,0:T(1,128)S(1)} %bitcast.31, bf16[4,64,1280]{2,1,0:T(8,128)(2,1)S(1)} %all-to-all-done.2.grad_ref), custom_call_target="tpu_custom_call" | custom-call | bytes 2000000 | tf_op jit(solution)/shard_map/pallas_call | solution.py:31
  (37 shorter events, 6.2 us)
Async XLA Ops:
  0.6 7.0 %copy-start = (bf16[1,64,5120]{2,1,0:T(8,128)(2,1)S(1)}, bf16[1,64,5120]{2,1,0:T(8,128)(2,1)}, u32[]{:S(2)}) copy-start(bf16[1,64,5120]{2,1,0:T(8,128)(2,1)} %param.7) | copy-start | bytes 1966084
  0.6 1.0 copy-start.2
  1.6 0.9 copy-start.4
  2.5 0.7 copy-start.7
  4.0 9.7 %all-to-all-start.1 = ((bf16[4,64,512]{2,1,0:T(8,128)(2,1)}), bf16[4,64,512]{2,1,0:T(8,128)(2,1)S(1)}, u32[]{:S(2)}, u32[]{:S(2)}) async-start(bf16[4,64,512]{2,1,0:T(8,128)(2,1)} %shard_map.111), calls=%async_computation.1 | async-start | bytes 524288 | tf_op jit(solution)/shard_map/all_to_all | solution.py:273
  7.7 1.1 copy-start.1
  8.8 0.7 copy-start.5
  9.5 0.7 copy-start.9
  13.7 12.4 %copy-start.8 = (f32[1024]{0:T(1024)S(1)}, f32[1024]{0:T(1024)}, u32[]{:S(2)}) copy-start(f32[1024]{0:T(1024)} %param.12) | copy-start | bytes 12292
  13.7 12.5 %copy-start.6 = (f32[5120]{0:T(1024)S(1)}, f32[5120]{0:T(1024)}, u32[]{:S(2)}) copy-start(f32[5120]{0:T(1024)} %param.11) | copy-start | bytes 61444
  13.7 20.9 %all-to-all-start = ((bf16[4,64,2560]{2,1,0:T(8,128)(2,1)}), bf16[4,64,2560]{2,1,0:T(8,128)(2,1)S(1)}, u32[]{:S(2)}, u32[]{:S(2)}) async-start(bf16[4,64,2560]{2,1,0:T(8,128)(2,1)} %get-tuple-element.15), calls=%async_computation | async-start | bytes 2621440 | tf_op jit(solution)/shard_map/all_to_all | solution.py:273
  17.4 15.6 %collective-permute-start = (bf16[256,512]{1,0:T(8,128)(2,1)S(1)}, bf16[256,512]{1,0:T(8,128)(2,1)S(1)}, u32[]{:S(2)}, u32[]{:S(2)}) collective-permute-start(bf16[256,512]{1,0:T(8,128)(2,1)S(1)} %bitcast.25), channel_id=1, source_target_pairs={{0,8},{1,9},{2,10},{3,11},{8,16},{9,17},{10,18},{11,19},{16,24},{1... | collective-permute-start | bytes 786440 | tf_op jit(solution)/shard_map/ppermute | solution.py:279
  20.8 12.2 %collective-permute-start.1 = (bf16[128,512]{1,0:T(8,128)(2,1)S(1)}, bf16[128,512]{1,0:T(8,128)(2,1)S(1)}, u32[]{:S(2)}, u32[]{:S(2)}) collective-permute-start(bf16[128,512]{1,0:T(8,128)(2,1)S(1)} %bitcast.37), channel_id=1, source_target_pairs={{0,16},{1,17},{2,18},{3,19},{8,24},{9,25},{10,26},{11,27},{16,32},... | collective-permute-start | bytes 393224 | tf_op jit(solution)/shard_map/ppermute | solution.py:279
  41.2 0.7 copy-start.10
  42.9 39.7 %all-to-all-start.4 = ((f32[64,1,1536]{2,1,0:T(1,128)}), f32[64,1,1536]{2,1,0:T(1,128)S(1)}, u32[]{:S(2)}, u32[]{:S(2)}) async-start(f32[64,1,1536]{2,1,0:T(1,128)} %broadcast_in_dim.39), calls=%async_computation.4 | async-start | bytes 786432 | tf_op jit(solution)/shard_map/all_to_all | solution.py:330
  65.0 16.6 %collective-permute-start.2 = (bf16[256,512]{1,0:T(8,128)(2,1)S(1)}, bf16[256,512]{1,0:T(8,128)(2,1)S(1)}, u32[]{:S(2)}, u32[]{:S(2)}) collective-permute-start(bf16[256,512]{1,0:T(8,128)(2,1)S(1)} %get-tuple-element.19), channel_id=1, source_target_pairs={{8,0},{9,1},{10,2},{11,3},{16,8},{17,9},{18,10},{19,11},{24,16},{2... | collective-permute-start | bytes 786440 | tf_op jit(solution)/shard_map/ppermute | solution.py:279
  67.5 14.1 %collective-permute-start.3 = (bf16[128,512]{1,0:T(8,128)(2,1)}, bf16[128,512]{1,0:T(8,128)(2,1)S(1)}, u32[]{:S(2)}, u32[]{:S(2)}) collective-permute-start(bf16[128,512]{1,0:T(8,128)(2,1)} %copy-done.10), channel_id=1, source_target_pairs={{16,0},{17,1},{18,2},{19,3},{24,8},{25,9},{26,10},{27,11},{32,16},... | collective-permute-start | bytes 393224 | tf_op jit(solution)/shard_map/ppermute | solution.py:279
  82.4 30.5 %copy-start.3 = (bf16[1,64,1024]{2,1,0:T(8,128)(2,1)S(1)}, bf16[1,64,1024]{2,1,0:T(8,128)(2,1)}, u32[]{:S(2)}) copy-start(bf16[1,64,1024]{2,1,0:T(8,128)(2,1)} %param.8) | copy-start | bytes 393220
  82.5 9.4 %all-to-all-start.3 = ((bf16[4,64,512]{2,1,0:T(8,128)(2,1)}), bf16[4,64,512]{2,1,0:T(8,128)(2,1)S(1)}, u32[]{:S(2)}, u32[]{:S(2)}) async-start(bf16[4,64,512]{2,1,0:T(8,128)(2,1)} %shard_map.114), calls=%async_computation.3 | async-start | bytes 524288 | tf_op jit(solution)/shard_map/all_to_all | solution.py:273
  109.5 13.7 %all-to-all-start.2 = ((bf16[4,64,1280]{2,1,0:T(8,128)(2,1)}), bf16[4,64,1280]{2,1,0:T(8,128)(2,1)S(1)}, u32[]{:S(2)}, u32[]{:S(2)}) async-start(bf16[4,64,1280]{2,1,0:T(8,128)(2,1)} %get-tuple-element.17), calls=%async_computation.2 | async-start | bytes 1310720 | tf_op jit(solution)/shard_map/all_to_all | solution.py:273

commit v2 on v1

v2 whole, which is shorter than its diff:
```python
import functools
import math

import jax
import jax.numpy as jnp
from jax import lax
from jax.experimental import pallas as pl
from jax.experimental.pallas import tpu as pltpu
from jax.sharding import PartitionSpec as P

GROUP = 5
HEAD_DIM = 128
BLOCK = 128
EPSILON = 1e-06
MASKED = -1e30
TEAM = 8
SPAN = 4
WINDOW = 2 * SPAN - 1
Q_COLS = GROUP * HEAD_DIM
KV_COLS = 2 * HEAD_DIM
BACK_COLS = Q_COLS + KV_COLS
SUM_COLS = Q_COLS + HEAD_DIM
SUM_ROWS = 16
SCALE = 1.0 / math.sqrt(HEAD_DIM)
LOG2E = math.log2(math.e)
F32 = jnp.float32
BF16 = jnp.bfloat16
VMEM_LIMIT = 32 * 1024 * 1024
VMEM_ALL = 63 * 1024 * 1024


def call(kernel, out_shape, args, smem=0, flops=0, size=1024, scratch=(), far=False):
    whole = pl.BlockSpec(memory_space=pltpu.VMEM)
    scalar = pl.BlockSpec(memory_space=pltpu.SMEM)
    given = pl.BlockSpec(memory_space=pltpu.HBM) if far else whole
    single = not isinstance(out_shape, (tuple, list))
    scratch = list(scratch)
    if far:
        arrays = args[smem:]
        scratch += [pltpu.VMEM(array.shape, array.dtype) for array in arrays]
        scratch += [pltpu.SemaphoreType.DMA((len(arrays),))]
    return pl.pallas_call(
        kernel,
        out_shape=out_shape,
        in_specs=[scalar] * smem + [given] * (len(args) - smem),
        out_specs=whole if single else [whole] * len(out_shape),
        scratch_shapes=scratch,
        compiler_params=pltpu.CompilerParams(vmem_limit_bytes=VMEM_ALL if far else VMEM_LIMIT),
        cost_estimate=pl.CostEstimate(flops=flops, bytes_accessed=size, transcendentals=0),
    )(*args)


def fetched(sources, targets, semaphores):
    copies = [
        pltpu.make_async_copy(source, target, semaphores.at[at])
        for at, (source, target) in enumerate(zip(sources, targets))
    ]
    for copy in copies:
        copy.start()
    for copy in copies:
        copy.wait()
    return targets


def inverse_rms(values):
    return lax.rsqrt(jnp.mean(values * values, axis=-1, keepdims=True) + EPSILON)


def key_norm_kernel(
    mask_ref, key_in, value_in, gain_in, out_ref, key_ref, value_ref, gain_ref, semaphores
):
    fetched((key_in, value_in, gain_in), (key_ref, value_ref, gain_ref), semaphores)
    values = key_ref[...].astype(F32)
    normed = (values * inverse_rms(values) * gain_ref[...]).astype(BF16)
    for head in range(TEAM):
        columns = slice(head * HEAD_DIM, (head + 1) * HEAD_DIM)
        slot = head ^ mask_ref[0]
        out_ref[slot, :, :HEAD_DIM] = normed[:, columns]
        out_ref[slot, :, HEAD_DIM:] = value_ref[:, columns]


def query_norm_kernel(mask_ref, span_ref, *refs):
    sources, (out_ref, flags_ref), targets, semaphores = refs[:4], refs[4:6], refs[6:10], refs[10]
    query_ref, grad_ref, gain_ref, docs_ref = fetched(sources, targets, semaphores)
    values = query_ref[...].astype(F32)
    normed = (values * inverse_rms(values) * gain_ref[...]).astype(BF16)
    for head in range(TEAM):
        columns = slice(head * Q_COLS, (head + 1) * Q_COLS)
        slot = head ^ mask_ref[0]
        out_ref[slot, :, :Q_COLS] = normed[:, columns]
        out_ref[slot, :, Q_COLS:] = grad_ref[:, columns]
    lengths = docs_ref[...]
    count = lengths.shape[1]
    earlier = lax.broadcasted_iota(jnp.int32, (count, count), 1) <= lax.broadcasted_iota(
        jnp.int32, (count, count), 0
    )
    ends = jnp.sum(jnp.where(earlier, lengths, 0), axis=1, keepdims=True)
    first = SPAN * (span_ref[0] - 1) + 1
    places = first + lax.broadcasted_iota(jnp.int32, (count, 128), 1)
    found = jnp.sum((ends <= places).astype(jnp.int32), axis=0, keepdims=True)
    found = jnp.where(places[:1] >= 0, found, -1)
    flags_ref[...] = jnp.zeros_like(flags_ref)
    for at in range(WINDOW):
        flags_ref[at : at + 1, :] = jnp.broadcast_to(found[:, at : at + 1], (1, 128))


def contract(left, right, dims):
    return lax.dot_general(left, right, (dims, ((), ())), preferred_element_type=F32)


def attention_kernel(
    qd_ref,
    own_ref,
    near_ref,
    flags_ref,
    query_gain_ref,
    key_gain_ref,
    dq_ref,
    d_own_ref,
    d_near_ref,
    part_ref,
    s_ref,
    g_ref,
    p_ref,
    ds_ref,
):
    def window(at, kind):
        columns = slice(kind * HEAD_DIM, (kind + 1) * HEAD_DIM)
        ref, row = (near_ref, at) if at < SPAN - 1 else (own_ref, at - SPAN + 1)
        return ref[row * BLOCK : (row + 1) * BLOCK, columns]

    causal = lax.broadcasted_iota(jnp.int32, (BLOCK, BLOCK), 0) <= lax.broadcasted_iota(
        jnp.int32, (BLOCK, BLOCK), 1
    )
    diagonal = jnp.where(causal, 0.0, MASKED)
    factor = SCALE * LOG2E
    half = BLOCK // 2
    copies = part_ref.shape[0]
    d_keys = [None] * WINDOW
    d_values = [None] * WINDOW
    q_part = [0.0] * GROUP
    for z in range(SPAN):
        rows = slice(z * BLOCK, (z + 1) * BLOCK)
        blocks = list(range(z, z + SPAN))

        def heads_of(kind):
            base = kind * Q_COLS
            return jnp.concatenate(
                [
                    qd_ref[rows, base + j * HEAD_DIM : base + (j + 1) * HEAD_DIM]
                    for j in range(GROUP)
                ],
                axis=0,
            )

        queries, grads = heads_of(0), heads_of(1)
        keys = jnp.concatenate([window(at, 0) for at in blocks], axis=0)
        values = jnp.concatenate([window(at, 1) for at in blocks], axis=0)
        s_ref[...] = contract(keys, queries, ((1,), (1,)))
        g_ref[...] = contract(values, grads, ((1,), (1,)))
        biases = []
        for place, at in enumerate(blocks):
            if place == SPAN - 1:
                biases.append(diagonal)
            else:
                mine = SPAN - 1 + z
                same = flags_ref[at : at + 1, :] == flags_ref[mine : mine + 1, :]
                biases.append(jnp.where(same, 0.0, MASKED))
        for j in range(GROUP):
            lanes = slice(j * HEAD_DIM, (j + 1) * HEAD_DIM)
            spans = [slice(place * BLOCK, (place + 1) * BLOCK) for place in range(SPAN)]
            tiles = [s_ref[span, lanes] * factor + bias for span, bias in zip(spans, biases)]
            highest = functools.reduce(
                jnp.maximum, [jnp.max(t, axis=0, keepdims=True) for t in tiles]
            )
            tiles = [jnp.exp2(t - highest) for t in tiles]
            total = functools.reduce(jnp.add, [jnp.sum(t, axis=0, keepdims=True) for t in tiles])
            recip = 1.0 / total
            delta = 0.0
            kept = []
            for tile, span in zip(tiles, spans):
                weights = tile * recip
                probs = weights.astype(BF16)
                p_ref[span, lanes] = probs
                kept.append(weights)
                delta = delta + jnp.sum(
                    probs.astype(F32) * g_ref[span, lanes], axis=0, keepdims=True
                )
            for weights, span in zip(kept, spans):
                ds_ref[span, lanes] = (weights * (g_ref[span, lanes] - delta)).astype(BF16)
        score_grads = ds_ref[...]
        d_key = contract(score_grads, queries, ((1,), (0,)))
        d_value = contract(p_ref[...], grads, ((1,), (0,)))
        for place, at in enumerate(blocks):
            span = slice(place * BLOCK, (place + 1) * BLOCK)
            first = d_keys[at] is None
            d_keys[at] = d_key[span] if first else d_keys[at] + d_key[span]
            d_values[at] = d_value[span] if first else d_values[at] + d_value[span]
        d_query = contract(jnp.transpose(keys), score_grads, ((1,), (0,)))
        for j in range(GROUP):
            lanes = slice(j * HEAD_DIM, (j + 1) * HEAD_DIM)
            grad = (jnp.transpose(d_query[:, lanes]) * SCALE).astype(BF16)
            dq_ref[2 * z, :, lanes] = grad[:half]
            dq_ref[2 * z + 1, :, lanes] = grad[half:]
            normed = qd_ref[rows, lanes].astype(F32)
            q_part[j] = q_part[j] + jnp.sum(grad.astype(F32) * normed, axis=0, keepdims=True)
    for j in range(GROUP):
        lanes = slice(j * HEAD_DIM, (j + 1) * HEAD_DIM)
        part_ref[:, lanes] = jnp.broadcast_to(
            q_part[j] / query_gain_ref[:, lanes], (copies, HEAD_DIM)
        )
    k_part = 0.0
    for at in range(WINDOW):
        grad = d_keys[at] * SCALE
        k_part = k_part + jnp.sum(grad * window(at, 0).astype(F32), axis=0, keepdims=True)
        target, row = (d_near_ref, at) if at < SPAN - 1 else (d_own_ref, at - SPAN + 1)
        span = slice(row * BLOCK, (row + 1) * BLOCK)
        target[span, :HEAD_DIM] = grad.astype(target.dtype)
        target[span, HEAD_DIM:] = d_values[at].astype(target.dtype)
    part_ref[:, Q_COLS:] = jnp.broadcast_to(k_part / key_gain_ref[...], (copies, HEAD_DIM))


def gather_kernel(own_ref, near_ref, dq_ref, sums_ref, out_ref):
    half = BLOCK // 2
    rest = jnp.sum(sums_ref[...], axis=0, keepdims=True)
    pieces = []
    for _ in range(3):
        pieces.append(rest.astype(BF16).astype(F32))
        rest = rest - pieces[-1]
    pieces.append(jnp.zeros((SUM_ROWS - 3, SUM_COLS), F32))
    sums = jnp.concatenate(pieces, axis=0).astype(BF16)
    for slot in range(TEAM):
        rows = slice(slot * half, (slot + 1) * half)
        total = own_ref[rows]
        if slot >= 2:
            total = total + near_ref[(slot - 2) * half : (slot - 1) * half].astype(F32)
        out_ref[slot, :half, :Q_COLS] = dq_ref[slot]
        out_ref[slot, :half, Q_COLS:] = total.astype(BF16)
        out_ref[slot, half:, :SUM_COLS] = sums
        out_ref[slot, half:, SUM_COLS:] = jnp.zeros((SUM_ROWS, BACK_COLS - SUM_COLS), BF16)


def norm_backward(rows, gain, grad):
    values = rows.astype(F32)
    inverse = inverse_rms(values)
    scaled = grad.astype(F32) * gain
    inner = jnp.mean(scaled * values, axis=-1, keepdims=True)
    return (inverse * scaled - values * (inverse * inverse * inverse * inner)).astype(BF16)


def final_kernel(
    mask_ref,
    query_ref,
    key_ref,
    query_gain_ref,
    key_gain_ref,
    back_ref,
    d_query_ref,
    d_key_ref,
    d_value_ref,
    d_query_gain_ref,
    d_key_gain_ref,
):
    half = BLOCK // 2
    slots = [head ^ mask_ref[0] for head in range(TEAM)]
    grad = jnp.concatenate([back_ref[slot, :half, :Q_COLS] for slot in slots], axis=1)
    d_query_ref[...] = norm_backward(query_ref[...], query_gain_ref[...], grad)
    keys = slice(Q_COLS, Q_COLS + HEAD_DIM)
    grad = jnp.concatenate([back_ref[slot, :half, keys] for slot in slots], axis=1)
    d_key_ref[...] = norm_backward(key_ref[...], key_gain_ref[...], grad)
    for head, slot in enumerate(slots):
        d_value_ref[:, head * HEAD_DIM : (head + 1) * HEAD_DIM] = back_ref[
            slot, :half, Q_COLS + HEAD_DIM :
        ]
        pieces = back_ref[slot, half:, :SUM_COLS].astype(F32)
        sums = pieces[0:1] + pieces[1:2] + pieces[2:3]
        d_query_gain_ref[:, head * Q_COLS : (head + 1) * Q_COLS] = sums[:, :Q_COLS]
        d_key_gain_ref[:, head * HEAD_DIM : (head + 1) * HEAD_DIM] = sums[:, Q_COLS:]


def team_of(seq_at, head_at, seq_count):
    upper = head_at // 4
    segment = seq_at + upper * (2 * seq_count - 1 - 2 * seq_at)
    slot = (segment % 2) * 4 + head_at % 4
    mask = ((seq_at // 2) % 2 ^ upper) * 4 + (seq_at // (seq_count // 2)) * 2
    return segment // 2, slot, mask


def layout(seq_count):
    spans = seq_count
    teams = [[None] * TEAM for _ in range(spans)]
    by_head = [[None] * spans for _ in range(TEAM)]
    for seq_at in range(seq_count):
        for head_at in range(TEAM):
            span, slot, mask = team_of(seq_at, head_at, seq_count)
            device = seq_at * TEAM + head_at
            teams[span][slot] = device
            by_head[slot ^ mask][span] = device
    return teams, by_head


def body(query_raw, key_raw, value_in, out_grad, query_gain, key_gain, doc_blocks):
    seq_count = lax.axis_size("seq")
    axes = ("seq", "head")
    teams, by_head = layout(seq_count)
    span, slot, mask = team_of(lax.axis_index("seq"), lax.axis_index("head"), seq_count)
    head = slot ^ mask
    mask_scalar = mask[None].astype(jnp.int32)
    span_scalar = span[None].astype(jnp.int32)
    rows = query_raw.shape[1]
    query_rows, key_rows, value_rows, grad_rows = (
        query_raw[0],
        key_raw[0],
        value_in[0],
        out_grad[0],
    )
    query_gain_row, key_gain_row = query_gain[None], key_gain[None]

    def exchange(array):
        return lax.all_to_all(array, axes, 0, 0, axis_index_groups=teams, tiled=True)

    onward = [(line[at], line[at + 1]) for line in by_head for at in range(len(line) - 1)]
    onward.sort()
    backward = sorted((target, source) for source, target in onward)

    kv_send = call(
        key_norm_kernel,
        jax.ShapeDtypeStruct((TEAM, rows, KV_COLS), BF16),
        (mask_scalar, key_rows, value_rows, key_gain_row),
        smem=1,
        far=True,
    )
    own = exchange(kv_send).reshape(TEAM * rows, KV_COLS)
    near = lax.ppermute(own[BLOCK:], axes, onward)
    qd_send, flags = call(
        query_norm_kernel,
        (
            jax.ShapeDtypeStruct((TEAM, rows, 2 * Q_COLS), BF16),
            jax.ShapeDtypeStruct((8, 128), jnp.int32),
        ),
        (mask_scalar, span_scalar, query_rows, grad_rows, query_gain_row, doc_blocks[None]),
        smem=2,
        far=True,
    )
    qd = exchange(qd_send).reshape(TEAM * rows, 2 * Q_COLS)
    my_query_gain = lax.dynamic_slice_in_dim(query_gain_row, head * Q_COLS, Q_COLS, 1)
    my_key_gain = lax.dynamic_slice_in_dim(key_gain_row, head * HEAD_DIM, HEAD_DIM, 1)
    window = SPAN * BLOCK
    dq, d_own, d_near, part = call(
        attention_kernel,
        (
            jax.ShapeDtypeStruct((TEAM, rows, Q_COLS), BF16),
            jax.ShapeDtypeStruct((window, KV_COLS), F32),
            jax.ShapeDtypeStruct((window - BLOCK, KV_COLS), BF16),
            jax.ShapeDtypeStruct((seq_count, SUM_COLS), F32),
        ),
        (qd, own, near, flags, my_query_gain, my_key_gain),
        scratch=[
            pltpu.VMEM((window, Q_COLS), F32),
            pltpu.VMEM((window, Q_COLS), F32),
            pltpu.VMEM((window, Q_COLS), BF16),
            pltpu.VMEM((window, Q_COLS), BF16),
        ],
    )
    back_near = lax.ppermute(d_near, axes, backward)

    def by_exchange(part):
        return lax.all_to_all(part, axes, 0, 0, axis_index_groups=by_head, tiled=True)

    def by_gather(part):
        return lax.all_gather(part[0], axes, axis_index_groups=by_head)

    sums = lax.cond(doc_blocks[0] >= 0, by_exchange, by_gather, part)
    back_send = call(
        gather_kernel,
        jax.ShapeDtypeStruct((TEAM, rows + SUM_ROWS, BACK_COLS), BF16),
        (d_own, back_near, dq, sums),
    )
    back = exchange(back_send)
    d_query, d_key, d_value, d_query_gain, d_key_gain = call(
        final_kernel,
        (
            jax.ShapeDtypeStruct(query_rows.shape, BF16),
            jax.ShapeDtypeStruct(key_rows.shape, BF16),
            jax.ShapeDtypeStruct(value_rows.shape, BF16),
            jax.ShapeDtypeStruct(query_gain_row.shape, F32),
            jax.ShapeDtypeStruct(key_gain_row.shape, F32),
        ),
        (mask_scalar, query_rows, key_rows, query_gain_row, key_gain_row, back),
        smem=1,
    )
    return d_query[None], d_key[None], d_value[None], d_query_gain[0], d_key_gain[0]


def solution(mesh):
    split = P("seq", "head", None)
    in_specs = (split, split, split, split, P(), P(), P())
    out_specs = (split, split, split, P(), P())
    return jax.shard_map(body, mesh=mesh, in_specs=in_specs, out_specs=out_specs, check_vma=False)
```

time: 125 us -> 99.3 us (0.79)
  the two profiles are of different devices: /device:TPU:26 before, /device:TPU:1 now
where the time goes in v2:
time: 99.3 us; the launch traced here: 98.8 us
  blocking collectives  51.6 us (52%)
  starting transfers between devices  17.7 us (18%)
  waiting for transfers between devices  16 us (16%)
  Pallas kernels  12.2 us (12%)
    all_to_all x1, blocking collectives, by_exchange(): lax.all_to_all(part, axes, 0, 0, axis_index_groups=by_head, tiled=True)  29.2 us
    all_to_all x1, blocking collectives, exchange(): lax.all_to_all(array, axes, 0, 0, axis_index_groups=teams, tiled=True)  22.4 us
    all_to_all x2, starting transfers between devices, exchange(): lax.all_to_all(array, axes, 0, 0, axis_index_groups=teams, tiled=True)  15.1 us
    pallas_call x5, Pallas kernels, call(): pl.pallas_call(kernel, out_shape=out_shape, in_specs=[scalar] * smem + [g...  12.2 us
    all_to_all x2, waiting for transfers between devices, exchange(): lax.all_to_all(array, axes, 0, 0, axis_index_groups=teams, tiled=True)  11.8 us
    ppermute x1, waiting for transfers between devices, body(): near = lax.ppermute(own[BLOCK:], axes, onward)  4.18 us
  transfers between devices with their start and end apart: 4, of which 3 were waited for; matrix products, arithmetic and copies ran while one was open for 0% of the time, Pallas kernels for 3%

profile of v2, /device:TPU:1, one launch (start us, length us, event | category | flops | bytes accessed | tf_op | source)
XLA Modules:
  0.0 98.8 jit_solution(13184232557936521631)
XLA Ops:
  0.7 1.8 %shard_map.111 = bf16[8,64,256]{2,1,0:T(8,128)(2,1)} custom-call(s32[1]{0:T(128)} %bitcast.1.mask_ref, bf16[64,1024]{1,0:T(8,128)(2,1)} %bitcast.33, bf16[64,1024]{1,0:T(8,128)(2,1)} %bitcast.43, f32[1,1024]{1,0:T(1,128)} %bitcast.37), custom_call_target="tpu_custom_call" | custom-call | bytes 1024 | tf_op jit(solution)/shard_map/pallas_call | solution.py:42
  2.5 10.2 %all-to-all-start.2 = ((bf16[8,64,256]{2,1,0:T(8,128)(2,1)}), bf16[8,64,256]{2,1,0:T(8,128)(2,1)S(1)}, u32[]{:S(2)}, u32[]{:S(2)}) async-start(bf16[8,64,256]{2,1,0:T(8,128)(2,1)} %shard_map.111), calls=%async_computation.2 | async-start | bytes 524288 | tf_op jit(solution)/shard_map/all_to_all | solution.py:320
  12.7 2.8 %shard_map.110 = (bf16[8,64,1280]{2,1,0:T(8,128)(2,1)}, s32[8,128]{1,0:T(8,128)}) custom-call(s32[1]{0:T(128)} %bitcast.1.mask_ref, s32[1]{0:T(128)} %bitcast.6.span_ref, bf16[64,5120]{1,0:T(8,128)(2,1)} %bitcast.30, bf16[64,5120]{1,0:T(8,128)(2,1)} %bitcast.41, f32[1,5120]{1,0:T(1,128)} %bitcast.35, s32[1,96]{1,0:T(1,128)} %bitcast.44), custom_call_target="tpu_custom_call" | custom-call | bytes 1024 | tf_op jit(solution)/shard_map/pallas_call | solution.py:42
  15.6 2.8 %all-to-all-done.2 = bf16[8,64,256]{2,1,0:T(8,128)(2,1)S(1)} async-done(((bf16[8,64,256]{2,1,0:T(8,128)(2,1)}), bf16[8,64,256]{2,1,0:T(8,128)(2,1)S(1)}, u32[]{:S(2)}, u32[]{:S(2)}) %all-to-all-start.2) | async-done | bytes 262176 | tf_op jit(solution)/shard_map/all_to_all | solution.py:320
  18.4 4.9 %all-to-all-start.1 = ((bf16[8,64,1280]{2,1,0:T(8,128)(2,1)}), bf16[8,64,1280]{2,1,0:T(8,128)(2,1)S(1)}, u32[]{:S(2)}, u32[]{:S(2)}) async-start(bf16[8,64,1280]{2,1,0:T(8,128)(2,1)} %get-tuple-element.21), calls=%async_computation.1 | async-start | bytes 2621440 | tf_op jit(solution)/shard_map/all_to_all | solution.py:320
  23.3 1.3 %collective-permute-start = (bf16[384,256]{1,0:T(8,128)(2,1)S(1)}, bf16[384,256]{1,0:T(8,128)(2,1)S(1)}, u32[]{:S(2)}, u32[]{:S(2)}) collective-permute-start(bf16[384,256]{1,0:T(8,128)(2,1)S(1)} %bitcast.42), channel_id=1, source_target_pairs={{0,24},{1,25},{2,26},{3,27},{8,16},{9,17},{10,18},{11,19},{16,40},... | collective-permute-start | bytes 589832 | tf_op jit(solution)/shard_map/ppermute | solution.py:334
  24.7 0.0 copy-done.2
  24.7 0.1 dynamic-slice.6
  24.8 0.0 copy-done.3
  24.8 0.1 dynamic-slice_bitcast_fusion.key_gain_ref
  24.9 4.2 %collective-permute-done.near_ref = bf16[384,256]{1,0:T(8,128)(2,1)S(1)} collective-permute-done((bf16[384,256]{1,0:T(8,128)(2,1)S(1)}, bf16[384,256]{1,0:T(8,128)(2,1)S(1)}, u32[]{:S(2)}, u32[]{:S(2)}) %collective-permute-start) | collective-permute-done | bytes 196640 | tf_op jit(solution)/shard_map/ppermute | solution.py:334
  29.0 9.0 %all-to-all-done.1 = bf16[8,64,1280]{2,1,0:T(8,128)(2,1)S(1)} async-done(((bf16[8,64,1280]{2,1,0:T(8,128)(2,1)}), bf16[8,64,1280]{2,1,0:T(8,128)(2,1)S(1)}, u32[]{:S(2)}, u32[]{:S(2)}) %all-to-all-start.1) | async-done | bytes 1310752 | tf_op jit(solution)/shard_map/all_to_all | solution.py:320
  38.0 5.8 %shard_map.112 = (bf16[8,64,640]{2,1,0:T(8,128)(2,1)S(1)}, f32[512,256]{1,0:T(8,128)S(1)}, bf16[384,256]{1,0:T(8,128)(2,1)S(1)}, f32[64,768]{1,0:T(8,128)S(1)}) custom-call(bf16[512,1280]{1,0:T(8,128)(2,1)S(1)} %bitcast.29, bf16[512,256]{1,0:T(8,128)(2,1)S(1)} %bitcast.32, bf16[384,256]{1,0:T(8,128)(2,1)S(1)} %collective-permute-done.near_ref, ...), custom_call_target="tpu_custom_call" | custom-call | bytes 1024 | tf_op jit(solution)/shard_map/pallas_call | solution.py:42
  43.8 1.3 %collective-permute-start.1 = (bf16[384,256]{1,0:T(8,128)(2,1)S(1)}, bf16[384,256]{1,0:T(8,128)(2,1)S(1)}, u32[]{:S(2)}, u32[]{:S(2)}) collective-permute-start(bf16[384,256]{1,0:T(8,128)(2,1)S(1)} %get-tuple-element.24), channel_id=1, source_target_pairs={{4,28},{5,29},{6,30},{7,31},{12,20},{13,21},{14,22},{15,23},{16,8}... | collective-permute-start | bytes 589832 | tf_op jit(solution)/shard_map/ppermute | solution.py:365
  45.2 29.4 %conditional.1 = (f32[64,768]{1,0:T(8,128)S(1)}) conditional(s32[]{:T(128)} %bitcast.14, f32[64,768]{1,0:T(8,128)S(1)} %get-tuple-element.26, f32[64,768]{1,0:T(8,128)S(1)} %get-tuple-element.26), branch_computations={%region_0.1_spmd, %region_1.2_spmd} | conditional | bytes 1179656 | solution.py:373
  45.2 0.1 all_to_all.8
  45.3 29.2 %all_to_all.24 = f32[64,1,768]{2,1,0:T(1,128)S(1)} all-to-all(f32[64,1,768]{2,1,0:T(1,128)S(1)} %all_to_all.8), channel_id=1, replica_groups={{0,24,32,56,64,88,96,120,128,152,160,184,192,216,224,248,258,282,290,31..., dimensions={0} | all-to-all | bytes 393216 | tf_op jit(solution)/shard_map/cond/branch_1_fun/all_to_all | solution.py:368
  74.6 0.0 collective-permute-done.1.near_ref
  74.6 0.1 shard_map.113
  74.7 0.0 copy-start
  74.7 0.0 copy-start.1
  74.8 22.4 %all_to_all.25.back_ref = bf16[8,80,896]{2,1,0:T(8,128)(2,1)S(1)} all-to-all(bf16[8,80,896]{2,1,0:T(8,128)(2,1)S(1)} %shard_map.113), channel_id=1, replica_groups={{0,1,2,3,8,9,10,11},{16,17,18,19,24,25,26,27},{32,33,34,35,40,41,42,43}..., dimensions={0} | all-to-all | bytes 2293760 | tf_op jit(solution)/shard_map/all_to_all | solution.py:320
  97.2 0.0 copy-done.1
  97.2 1.7 %shard_map.114 = (bf16[64,5120]{1,0:T(8,128)(2,1)}, bf16[64,1024]{1,0:T(8,128)(2,1)}, bf16[64,1024]{1,0:T(8,128)(2,1)}, f32[1,5120]{1,0:T(1,128)}, f32[1,1024]{1,0:T(1,128)}) custom-call(s32[1]{0:T(128)} %bitcast.1.mask_ref, bf16[64,5120]{1,0:T(8,128)(2,1)S(1)} %bitcast.31, bf16[64,1024]{1,0:T(8,128)(2,1)S(1)} %bitcast.34, f32[1,5120]{1,0:T(1,128)S(1)} %bitcast.36, ...), custom_call_target="tpu_custom_call" | custom-call | bytes 1024 | tf_op jit(solution)/shard_map/pallas_call | solution.py:42
  (10 shorter events, 0.0 us)
Async XLA Ops:
  2.5 15.8 %all-to-all-start.2 = ((bf16[8,64,256]{2,1,0:T(8,128)(2,1)}), bf16[8,64,256]{2,1,0:T(8,128)(2,1)S(1)}, u32[]{:S(2)}, u32[]{:S(2)}) async-start(bf16[8,64,256]{2,1,0:T(8,128)(2,1)} %shard_map.111), calls=%async_computation.2 | async-start | bytes 524288 | tf_op jit(solution)/shard_map/all_to_all | solution.py:320
  18.4 6.3 %copy-start.2 = (f32[5120]{0:T(1024)S(1)}, f32[5120]{0:T(1024)}, u32[]{:S(2)}) copy-start(f32[5120]{0:T(1024)} %param.13) | copy-start | bytes 61444
  18.4 6.4 %copy-start.3 = (f32[1024]{0:T(1024)S(1)}, f32[1024]{0:T(1024)}, u32[]{:S(2)}) copy-start(f32[1024]{0:T(1024)} %param.14) | copy-start | bytes 12292
  18.4 19.7 %copy-start.4 = (s32[8,128]{1,0:T(8,128)S(1)}, s32[8,128]{1,0:T(8,128)}, u32[]{:S(2)}) copy-start(s32[8,128]{1,0:T(8,128)} %get-tuple-element.22.flags_ref) | copy-start | bytes 12292
  18.4 19.6 %all-to-all-start.1 = ((bf16[8,64,1280]{2,1,0:T(8,128)(2,1)}), bf16[8,64,1280]{2,1,0:T(8,128)(2,1)S(1)}, u32[]{:S(2)}, u32[]{:S(2)}) async-start(bf16[8,64,1280]{2,1,0:T(8,128)(2,1)} %get-tuple-element.21), calls=%async_computation.1 | async-start | bytes 2621440 | tf_op jit(solution)/shard_map/all_to_all | solution.py:320
  23.3 21.8 %copy-start.5 = (s32[96]{0:T(128)S(1)}, s32[96]{0:T(128)}, u32[]{:S(2)}) copy-start(s32[96]{0:T(128)} %param.15) | copy-start | bytes 1156
  23.3 5.7 %collective-permute-start = (bf16[384,256]{1,0:T(8,128)(2,1)S(1)}, bf16[384,256]{1,0:T(8,128)(2,1)S(1)}, u32[]{:S(2)}, u32[]{:S(2)}) collective-permute-start(bf16[384,256]{1,0:T(8,128)(2,1)S(1)} %bitcast.42), channel_id=1, source_target_pairs={{0,24},{1,25},{2,26},{3,27},{8,16},{9,17},{10,18},{11,19},{16,40},... | collective-permute-start | bytes 589832 | tf_op jit(solution)/shard_map/ppermute | solution.py:334
  43.8 30.8 %collective-permute-start.1 = (bf16[384,256]{1,0:T(8,128)(2,1)S(1)}, bf16[384,256]{1,0:T(8,128)(2,1)S(1)}, u32[]{:S(2)}, u32[]{:S(2)}) collective-permute-start(bf16[384,256]{1,0:T(8,128)(2,1)S(1)} %get-tuple-element.24), channel_id=1, source_target_pairs={{4,28},{5,29},{6,30},{7,31},{12,20},{13,21},{14,22},{15,23},{16,8}... | collective-permute-start | bytes 589832 | tf_op jit(solution)/shard_map/ppermute | solution.py:365
  74.7 22.4 %copy-start = (bf16[1,64,5120]{2,1,0:T(8,128)(2,1)S(1)}, bf16[1,64,5120]{2,1,0:T(8,128)(2,1)}, u32[]{:S(2)}) copy-start(bf16[1,64,5120]{2,1,0:T(8,128)(2,1)} %param.9) | copy-start | bytes 1966084
  74.7 22.4 %copy-start.1 = (bf16[1,64,1024]{2,1,0:T(8,128)(2,1)S(1)}, bf16[1,64,1024]{2,1,0:T(8,128)(2,1)}, u32[]{:S(2)}) copy-start(bf16[1,64,1024]{2,1,0:T(8,128)(2,1)} %param.10) | copy-start | bytes 393220

commit v3 on v2

--- a/solution.py
+++ b/solution.py
@@ -18,8 +18,7 @@
 WINDOW = 2 * SPAN - 1
 Q_COLS = GROUP * HEAD_DIM
 KV_COLS = 2 * HEAD_DIM
-BACK_COLS = Q_COLS + KV_COLS
-SUM_COLS = Q_COLS + HEAD_DIM
+TILES = GROUP + 2
 SUM_ROWS = 16
 SCALE = 1.0 / math.sqrt(HEAD_DIM)
 LOG2E = math.log2(math.e)
@@ -113,8 +112,6 @@
     own_ref,
     near_ref,
     flags_ref,
-    query_gain_ref,
-    key_gain_ref,
     dq_ref,
     d_own_ref,
     d_near_ref,
@@ -156,8 +153,8 @@
         queries, grads = heads_of(0), heads_of(1)
         keys = jnp.concatenate([window(at, 0) for at in blocks], axis=0)
         values = jnp.concatenate([window(at, 1) for at in blocks], axis=0)
-        s_ref[...] = contract(keys, queries, ((1,), (1,)))
-        g_ref[...] = contract(values, grads, ((1,), (1,)))
+        s_ref[z] = contract(keys, queries, ((1,), (1,)))
+        g_ref[z] = contract(values, grads, ((1,), (1,)))
         biases = []
         for place, at in enumerate(blocks):
             if place == SPAN - 1:
@@ -169,7 +166,7 @@
         for j in range(GROUP):
             lanes = slice(j * HEAD_DIM, (j + 1) * HEAD_DIM)
             spans = [slice(place * BLOCK, (place + 1) * BLOCK) for place in range(SPAN)]
-            tiles = [s_ref[span, lanes] * factor + bias for span, bias in zip(spans, biases)]
+            tiles = [s_ref[z, span, lanes] * factor + bias for span, bias in zip(spans, biases)]
             highest = functools.reduce(
                 jnp.maximum, [jnp.max(t, axis=0, keepdims=True) for t in tiles]
             )
@@ -181,16 +178,16 @@
             for tile, span in zip(tiles, spans):
                 weights = tile * recip
                 probs = weights.astype(BF16)
-                p_ref[span, lanes] = probs
+                p_ref[z, span, lanes] = probs
                 kept.append(weights)
                 delta = delta + jnp.sum(
-                    probs.astype(F32) * g_ref[span, lanes], axis=0, keepdims=True
+                    probs.astype(F32) * g_ref[z, span, lanes], axis=0, keepdims=True
                 )
             for weights, span in zip(kept, spans):
-                ds_ref[span, lanes] = (weights * (g_ref[span, lanes] - delta)).astype(BF16)
-        score_grads = ds_ref[...]
+                ds_ref[z, span, lanes] = (weights * (g_ref[z, span, lanes] - delta)).astype(BF16)
+        score_grads = ds_ref[z]
         d_key = contract(score_grads, queries, ((1,), (0,)))
-        d_value = contract(p_ref[...], grads, ((1,), (0,)))
+        d_value = contract(p_ref[z], grads, ((1,), (0,)))
         for place, at in enumerate(blocks):
             span = slice(place * BLOCK, (place + 1) * BLOCK)
             first = d_keys[at] is None
@@ -199,45 +196,44 @@
         d_query = contract(jnp.transpose(keys), score_grads, ((1,), (0,)))
         for j in range(GROUP):
             lanes = slice(j * HEAD_DIM, (j + 1) * HEAD_DIM)
-            grad = (jnp.transpose(d_query[:, lanes]) * SCALE).astype(BF16)
+            grad = jnp.transpose(d_query[:, lanes]) * SCALE
+            normed = qd_ref[rows, lanes].astype(F32)
+            q_part[j] = q_part[j] + jnp.sum(grad * normed, axis=0, keepdims=True)
+            grad = grad.astype(BF16)
             dq_ref[2 * z, :, lanes] = grad[:half]
             dq_ref[2 * z + 1, :, lanes] = grad[half:]
-            normed = qd_ref[rows, lanes].astype(F32)
-            q_part[j] = q_part[j] + jnp.sum(grad.astype(F32) * normed, axis=0, keepdims=True)
     for j in range(GROUP):
         lanes = slice(j * HEAD_DIM, (j + 1) * HEAD_DIM)
-        part_ref[:, lanes] = jnp.broadcast_to(
-            q_part[j] / query_gain_ref[:, lanes], (copies, HEAD_DIM)
-        )
-    k_part = 0.0
+        part_ref[:, :, lanes] = jnp.broadcast_to(q_part[j][None], (copies, 1, HEAD_DIM))
     for at in range(WINDOW):
         grad = d_keys[at] * SCALE
-        k_part = k_part + jnp.sum(grad * window(at, 0).astype(F32), axis=0, keepdims=True)
         target, row = (d_near_ref, at) if at < SPAN - 1 else (d_own_ref, at - SPAN + 1)
         span = slice(row * BLOCK, (row + 1) * BLOCK)
         target[span, :HEAD_DIM] = grad.astype(target.dtype)
         target[span, HEAD_DIM:] = d_values[at].astype(target.dtype)
-    part_ref[:, Q_COLS:] = jnp.broadcast_to(k_part / key_gain_ref[...], (copies, HEAD_DIM))
 
 
 def gather_kernel(own_ref, near_ref, dq_ref, sums_ref, out_ref):
     half = BLOCK // 2
-    rest = jnp.sum(sums_ref[...], axis=0, keepdims=True)
+    rest = jnp.sum(sums_ref[...], axis=0)
     pieces = []
     for _ in range(3):
-        pieces.append(rest.astype(BF16).astype(F32))
-        rest = rest - pieces[-1]
-    pieces.append(jnp.zeros((SUM_ROWS - 3, SUM_COLS), F32))
+        piece = rest.astype(BF16).astype(F32)
+        pieces += [piece[:, at : at + HEAD_DIM] for at in range(0, Q_COLS, HEAD_DIM)]
+        rest = rest - piece
+    pieces.append(jnp.zeros((SUM_ROWS - len(pieces), HEAD_DIM), F32))
     sums = jnp.concatenate(pieces, axis=0).astype(BF16)
     for slot in range(TEAM):
         rows = slice(slot * half, (slot + 1) * half)
         total = own_ref[rows]
         if slot >= 2:
             total = total + near_ref[(slot - 2) * half : (slot - 1) * half].astype(F32)
-        out_ref[slot, :half, :Q_COLS] = dq_ref[slot]
-        out_ref[slot, :half, Q_COLS:] = total.astype(BF16)
-        out_ref[slot, half:, :SUM_COLS] = sums
-        out_ref[slot, half:, SUM_COLS:] = jnp.zeros((SUM_ROWS, BACK_COLS - SUM_COLS), BF16)
+        total = total.astype(BF16)
+        tiles = [dq_ref[slot, :, j * HEAD_DIM : (j + 1) * HEAD_DIM] for j in range(GROUP)]
+        tiles += [total[:, :HEAD_DIM], total[:, HEAD_DIM:]]
+        for at, tile in enumerate(tiles):
+            out_ref[slot, at * half : (at + 1) * half] = tile
+        out_ref[slot, TILES * half :] = sums
 
 
 def norm_backward(rows, gain, grad):
@@ -263,19 +259,25 @@
 ):
     half = BLOCK // 2
     slots = [head ^ mask_ref[0] for head in range(TEAM)]
-    grad = jnp.concatenate([back_ref[slot, :half, :Q_COLS] for slot in slots], axis=1)
+
+    def tile(slot, at):
+        return back_ref[slot, at * half : (at + 1) * half]
+
+    grad = jnp.concatenate([tile(slot, at) for slot in slots for at in range(GROUP)], axis=1)
     d_query_ref[...] = norm_backward(query_ref[...], query_gain_ref[...], grad)
-    keys = slice(Q_COLS, Q_COLS + HEAD_DIM)
-    grad = jnp.concatenate([back_ref[slot, :half, keys] for slot in slots], axis=1)
+    grad = jnp.concatenate([tile(slot, GROUP) for slot in slots], axis=1)
     d_key_ref[...] = norm_backward(key_ref[...], key_gain_ref[...], grad)
+    count = Q_COLS // HEAD_DIM
     for head, slot in enumerate(slots):
-        d_value_ref[:, head * HEAD_DIM : (head + 1) * HEAD_DIM] = back_ref[
-            slot, :half, Q_COLS + HEAD_DIM :
-        ]
-        pieces = back_ref[slot, half:, :SUM_COLS].astype(F32)
-        sums = pieces[0:1] + pieces[1:2] + pieces[2:3]
-        d_query_gain_ref[:, head * Q_COLS : (head + 1) * Q_COLS] = sums[:, :Q_COLS]
-        d_key_gain_ref[:, head * HEAD_DIM : (head + 1) * HEAD_DIM] = sums[:, Q_COLS:]
+        columns = slice(head * HEAD_DIM, (head + 1) * HEAD_DIM)
+        d_value_ref[:, columns] = tile(slot, GROUP + 1)
+        pieces = back_ref[slot, TILES * half :].astype(F32)
+        sums = pieces[:count] + pieces[count : 2 * count] + pieces[2 * count : 3 * count]
+        for j in range(GROUP):
+            at = slice((head * GROUP + j) * HEAD_DIM, (head * GROUP + j + 1) * HEAD_DIM)
+            d_query_gain_ref[:, at] = sums[j : j + 1] / query_gain_ref[:, at]
+        whole = jnp.sum(sums, axis=0, keepdims=True)
+        d_key_gain_ref[:, columns] = whole / key_gain_ref[:, columns]
 
 
 def team_of(seq_at, head_at, seq_count):
@@ -304,7 +306,6 @@
     axes = ("seq", "head")
     teams, by_head = layout(seq_count)
     span, slot, mask = team_of(lax.axis_index("seq"), lax.axis_index("head"), seq_count)
-    head = slot ^ mask
     mask_scalar = mask[None].astype(jnp.int32)
     span_scalar = span[None].astype(jnp.int32)
     rows = query_raw.shape[1]
@@ -343,8 +344,6 @@
         far=True,
     )
     qd = exchange(qd_send).reshape(TEAM * rows, 2 * Q_COLS)
-    my_query_gain = lax.dynamic_slice_in_dim(query_gain_row, head * Q_COLS, Q_COLS, 1)
-    my_key_gain = lax.dynamic_slice_in_dim(key_gain_row, head * HEAD_DIM, HEAD_DIM, 1)
     window = SPAN * BLOCK
     dq, d_own, d_near, part = call(
         attention_kernel,
@@ -352,28 +351,22 @@
             jax.ShapeDtypeStruct((TEAM, rows, Q_COLS), BF16),
             jax.ShapeDtypeStruct((window, KV_COLS), F32),
             jax.ShapeDtypeStruct((window - BLOCK, KV_COLS), BF16),
-            jax.ShapeDtypeStruct((seq_count, SUM_COLS), F32),
+            jax.ShapeDtypeStruct((seq_count, 1, Q_COLS), F32),
         ),
-        (qd, own, near, flags, my_query_gain, my_key_gain),
+        (qd, own, near, flags),
         scratch=[
-            pltpu.VMEM((window, Q_COLS), F32),
-            pltpu.VMEM((window, Q_COLS), F32),
-            pltpu.VMEM((window, Q_COLS), BF16),
-            pltpu.VMEM((window, Q_COLS), BF16),
+            pltpu.VMEM((SPAN, window, Q_COLS), F32),
+            pltpu.VMEM((SPAN, window, Q_COLS), F32),
+            pltpu.VMEM((SPAN, window, Q_COLS), BF16),
+            pltpu.VMEM((SPAN, window, Q_COLS), BF16),
         ],
     )
     back_near = lax.ppermute(d_near, axes, backward)
 
-    def by_exchange(part):
-        return lax.all_to_all(part, axes, 0, 0, axis_index_groups=by_head, tiled=True)
-
-    def by_gather(part):
-        return lax.all_gather(part[0], axes, axis_index_groups=by_head)
-
-    sums = lax.cond(doc_blocks[0] >= 0, by_exchange, by_gather, part)
+    sums = lax.all_to_all(part, axes, 0, 0, axis_index_groups=by_head, tiled=True)
     back_send = call(
         gather_kernel,
-        jax.ShapeDtypeStruct((TEAM, rows + SUM_ROWS, BACK_COLS), BF16),
+        jax.ShapeDtypeStruct((TEAM, TILES * rows + SUM_ROWS, HEAD_DIM), BF16),
         (d_own, back_near, dq, sums),
     )
     back = exchange(back_send)

time: 99.3 us -> 94.9 us (0.956)
  blocking collectives: 51.6 us -> 20 us
  starting transfers between devices: 17.7 us -> 33 us
  waiting for transfers between devices: 16 us -> 27.7 us
    all_to_all x1 -> x0, blocking collectives: 29.2 us -> none  [by_exchange(): lax.all_to_all(part, axes, 0, 0, axis_index_groups=by_head, tiled=True)]
    all_to_all x0 -> x1, starting transfers between devices: none -> 15.3 us  [body(): lax.all_to_all(part, axes, 0, 0, axis_index_groups=by_head, tiled=True)]
    ppermute x1, waiting for transfers between devices: 0.01 us -> 7.63 us  [body(): back_near = lax.ppermute(d_near, axes, backward)]
    all_to_all x0 -> x1, waiting for transfers between devices: none -> 3.84 us  [body(): lax.all_to_all(part, axes, 0, 0, axis_index_groups=by_head, tiled=True)]
    all_to_all x1, blocking collectives: 22.4 us -> 20 us  [exchange(): lax.all_to_all(array, axes, 0, 0, axis_index_groups=teams, tiled=True)]
  transfers between devices with their start and end apart: 4 -> 5, of which waited for: 3 -> 5; matrix products, arithmetic and copies ran while one was open for 0% -> 0% of each run, Pallas kernels for 3% -> 3%
where the time goes in v3:
time: 94.9 us; the launch traced here: 94.4 us
  starting transfers between devices  33 us (35%)
  waiting for transfers between devices  27.7 us (29%)
  blocking collectives  20 us (21%)
  Pallas kernels  13 us (14%)
    all_to_all x1, blocking collectives, exchange(): lax.all_to_all(array, axes, 0, 0, axis_index_groups=teams, tiled=True)  20 us
    all_to_all x1, starting transfers between devices, body(): lax.all_to_all(part, axes, 0, 0, axis_index_groups=by_head, tiled=True)  15.3 us
    all_to_all x2, starting transfers between devices, exchange(): lax.all_to_all(array, axes, 0, 0, axis_index_groups=teams, tiled=True)  15.1 us
    pallas_call x5, Pallas kernels, call(): pl.pallas_call(kernel, out_shape=out_shape, in_specs=[scalar] * smem + [g...  13 us
    all_to_all x2, waiting for transfers between devices, exchange(): lax.all_to_all(array, axes, 0, 0, axis_index_groups=teams, tiled=True)  11.8 us
    ppermute x1, waiting for transfers between devices, body(): back_near = lax.ppermute(d_near, axes, backward)  7.63 us
    ppermute x1, waiting for transfers between devices, body(): near = lax.ppermute(own[BLOCK:], axes, onward)  4.4 us
    all_to_all x1, waiting for transfers between devices, body(): lax.all_to_all(part, axes, 0, 0, axis_index_groups=by_head, tiled=True)  3.84 us
  transfers between devices with their start and end apart: 5, of which 5 were waited for; matrix products, arithmetic and copies ran while one was open for 0% of the time, Pallas kernels for 3%

profile of v3, /device:TPU:1, one launch (start us, length us, event | category | flops | bytes accessed | tf_op | source)
XLA Modules:
  0.0 94.4 jit_solution(535574854617619195)
XLA Ops:
  0.7 1.8 %shard_map.111 = bf16[8,64,256]{2,1,0:T(8,128)(2,1)} custom-call(s32[1]{0:T(128)} %bitcast.mask_ref, bf16[64,1024]{1,0:T(8,128)(2,1)} %bitcast.21, bf16[64,1024]{1,0:T(8,128)(2,1)} %bitcast.29, f32[1,1024]{1,0:T(1,128)} %bitcast.25), custom_call_target="tpu_custom_call" | custom-call | bytes 1024 | tf_op jit(solution)/shard_map/pallas_call | solution.py:41
  2.5 10.2 %all-to-all-start.1 = ((bf16[8,64,256]{2,1,0:T(8,128)(2,1)}), bf16[8,64,256]{2,1,0:T(8,128)(2,1)S(1)}, u32[]{:S(2)}, u32[]{:S(2)}) async-start(bf16[8,64,256]{2,1,0:T(8,128)(2,1)} %shard_map.111), calls=%async_computation.1 | async-start | bytes 524288 | tf_op jit(solution)/shard_map/all_to_all | solution.py:321
  12.7 2.8 %shard_map.110 = (bf16[8,64,1280]{2,1,0:T(8,128)(2,1)}, s32[8,128]{1,0:T(8,128)}) custom-call(s32[1]{0:T(128)} %bitcast.mask_ref, s32[1]{0:T(128)} %bitcast.5.span_ref, bf16[64,5120]{1,0:T(8,128)(2,1)} %bitcast.18, bf16[64,5120]{1,0:T(8,128)(2,1)} %bitcast.27, f32[1,5120]{1,0:T(1,128)} %bitcast.23, s32[1,96]{1,0:T(1,128)} %bitcast.30), custom_call_target="tpu_custom_call" | custom-call | bytes 1024 | tf_op jit(solution)/shard_map/pallas_call | solution.py:41
  15.6 2.8 %all-to-all-done.1 = bf16[8,64,256]{2,1,0:T(8,128)(2,1)S(1)} async-done(((bf16[8,64,256]{2,1,0:T(8,128)(2,1)}), bf16[8,64,256]{2,1,0:T(8,128)(2,1)S(1)}, u32[]{:S(2)}, u32[]{:S(2)}) %all-to-all-start.1) | async-done | bytes 262176 | tf_op jit(solution)/shard_map/all_to_all | solution.py:321
  18.4 4.9 %all-to-all-start = ((bf16[8,64,1280]{2,1,0:T(8,128)(2,1)}), bf16[8,64,1280]{2,1,0:T(8,128)(2,1)S(1)}, u32[]{:S(2)}, u32[]{:S(2)}) async-start(bf16[8,64,1280]{2,1,0:T(8,128)(2,1)} %get-tuple-element.16), calls=%async_computation | async-start | bytes 2621440 | tf_op jit(solution)/shard_map/all_to_all | solution.py:321
  23.3 1.3 %collective-permute-start = (bf16[384,256]{1,0:T(8,128)(2,1)S(1)}, bf16[384,256]{1,0:T(8,128)(2,1)S(1)}, u32[]{:S(2)}, u32[]{:S(2)}) collective-permute-start(bf16[384,256]{1,0:T(8,128)(2,1)S(1)} %bitcast.28), channel_id=1, source_target_pairs={{0,24},{1,25},{2,26},{3,27},{8,16},{9,17},{10,18},{11,19},{16,40},... | collective-permute-start | bytes 589832 | tf_op jit(solution)/shard_map/ppermute | solution.py:335
  24.6 4.4 %collective-permute-done.near_ref = bf16[384,256]{1,0:T(8,128)(2,1)S(1)} collective-permute-done((bf16[384,256]{1,0:T(8,128)(2,1)S(1)}, bf16[384,256]{1,0:T(8,128)(2,1)S(1)}, u32[]{:S(2)}, u32[]{:S(2)}) %collective-permute-start) | collective-permute-done | bytes 196640 | tf_op jit(solution)/shard_map/ppermute | solution.py:335
  29.0 9.0 %all-to-all-done = bf16[8,64,1280]{2,1,0:T(8,128)(2,1)S(1)} async-done(((bf16[8,64,1280]{2,1,0:T(8,128)(2,1)}), bf16[8,64,1280]{2,1,0:T(8,128)(2,1)S(1)}, u32[]{:S(2)}, u32[]{:S(2)}) %all-to-all-start) | async-done | bytes 1310752 | tf_op jit(solution)/shard_map/all_to_all | solution.py:321
  38.0 0.0 copy-done.4
  38.0 6.4 %shard_map.112 = (bf16[8,64,640]{2,1,0:T(8,128)(2,1)S(1)}, f32[512,256]{1,0:T(8,128)S(1)}, bf16[384,256]{1,0:T(8,128)(2,1)S(1)}, f32[64,1,640]{2,1,0:T(1,128)}) custom-call(bf16[512,1280]{1,0:T(8,128)(2,1)S(1)} %bitcast.17, bf16[512,256]{1,0:T(8,128)(2,1)S(1)} %bitcast.20, bf16[384,256]{1,0:T(8,128)(2,1)S(1)} %collective-permute-done.near_ref, ...), custom_call_target="tpu_custom_call" | custom-call | bytes 1024 | tf_op jit(solution)/shard_map/pallas_call | solution.py:41
  44.4 15.3 %all-to-all-start.2 = ((f32[64,1,640]{2,1,0:T(1,128)}), f32[64,1,640]{2,1,0:T(1,128)S(1)}, u32[]{:S(2)}, u32[]{:S(2)}) async-start(f32[64,1,640]{2,1,0:T(1,128)} %get-tuple-element.21), calls=%async_computation.2 | async-start | bytes 327680 | tf_op jit(solution)/shard_map/all_to_all | solution.py:366
  59.7 1.3 %collective-permute-start.1 = (bf16[384,256]{1,0:T(8,128)(2,1)S(1)}, bf16[384,256]{1,0:T(8,128)(2,1)S(1)}, u32[]{:S(2)}, u32[]{:S(2)}) collective-permute-start(bf16[384,256]{1,0:T(8,128)(2,1)S(1)} %get-tuple-element.19), channel_id=1, source_target_pairs={{4,28},{5,29},{6,30},{7,31},{12,20},{13,21},{14,22},{15,23},{16,8}... | collective-permute-start | bytes 589832 | tf_op jit(solution)/shard_map/ppermute | solution.py:364
  61.0 7.6 %collective-permute-done.1.near_ref = bf16[384,256]{1,0:T(8,128)(2,1)S(1)} collective-permute-done((bf16[384,256]{1,0:T(8,128)(2,1)S(1)}, bf16[384,256]{1,0:T(8,128)(2,1)S(1)}, u32[]{:S(2)}, u32[]{:S(2)}) %collective-permute-start.1) | collective-permute-done | bytes 196640 | tf_op jit(solution)/shard_map/ppermute | solution.py:364
  68.6 3.8 %all-to-all-done.2.sums_ref = f32[64,1,640]{2,1,0:T(1,128)S(1)} async-done(((f32[64,1,640]{2,1,0:T(1,128)}), f32[64,1,640]{2,1,0:T(1,128)S(1)}, u32[]{:S(2)}, u32[]{:S(2)}) %all-to-all-start.2) | async-done | bytes 163872 | tf_op jit(solution)/shard_map/all_to_all | solution.py:366
  72.5 0.3 shard_map.113
  72.7 0.0 copy-start
  72.7 0.0 copy-start.1
  72.7 0.0 copy-start.2
  72.8 0.0 copy-start.3
  72.8 20.0 %all_to_all.20.back_ref = bf16[8,464,128]{2,1,0:T(8,128)(2,1)S(1)} all-to-all(bf16[8,464,128]{2,1,0:T(8,128)(2,1)S(1)} %shard_map.113), channel_id=1, replica_groups={{0,1,2,3,8,9,10,11},{16,17,18,19,24,25,26,27},{32,33,34,35,40,41,42,43}..., dimensions={0} | all-to-all | bytes 1900544 | tf_op jit(solution)/shard_map/all_to_all | solution.py:321
  92.7 0.0 copy-done
  92.7 0.0 copy-done.1
  92.7 0.0 copy-done.2
  92.8 1.7 %shard_map.114 = (bf16[64,5120]{1,0:T(8,128)(2,1)}, bf16[64,1024]{1,0:T(8,128)(2,1)}, bf16[64,1024]{1,0:T(8,128)(2,1)}, f32[1,5120]{1,0:T(1,128)}, f32[1,1024]{1,0:T(1,128)}) custom-call(s32[1]{0:T(128)} %bitcast.mask_ref, bf16[64,5120]{1,0:T(8,128)(2,1)S(1)} %bitcast.19, bf16[64,1024]{1,0:T(8,128)(2,1)S(1)} %bitcast.22, f32[1,5120]{1,0:T(1,128)S(1)} %bitcast.24, ...), custom_call_target="tpu_custom_call" | custom-call | bytes 1024 | tf_op jit(solution)/shard_map/pallas_call | solution.py:41
  (3 shorter events, 0.0 us)
Async XLA Ops:
  2.5 15.8 %all-to-all-start.1 = ((bf16[8,64,256]{2,1,0:T(8,128)(2,1)}), bf16[8,64,256]{2,1,0:T(8,128)(2,1)S(1)}, u32[]{:S(2)}, u32[]{:S(2)}) async-start(bf16[8,64,256]{2,1,0:T(8,128)(2,1)} %shard_map.111), calls=%async_computation.1 | async-start | bytes 524288 | tf_op jit(solution)/shard_map/all_to_all | solution.py:321
  18.4 19.7 %copy-start.4 = (s32[8,128]{1,0:T(8,128)S(1)}, s32[8,128]{1,0:T(8,128)}, u32[]{:S(2)}) copy-start(s32[8,128]{1,0:T(8,128)} %get-tuple-element.17.flags_ref) | copy-start | bytes 12292
  18.4 19.6 %all-to-all-start = ((bf16[8,64,1280]{2,1,0:T(8,128)(2,1)}), bf16[8,64,1280]{2,1,0:T(8,128)(2,1)S(1)}, u32[]{:S(2)}, u32[]{:S(2)}) async-start(bf16[8,64,1280]{2,1,0:T(8,128)(2,1)} %get-tuple-element.16), calls=%async_computation | async-start | bytes 2621440 | tf_op jit(solution)/shard_map/all_to_all | solution.py:321
  23.3 5.7 %collective-permute-start = (bf16[384,256]{1,0:T(8,128)(2,1)S(1)}, bf16[384,256]{1,0:T(8,128)(2,1)S(1)}, u32[]{:S(2)}, u32[]{:S(2)}) collective-permute-start(bf16[384,256]{1,0:T(8,128)(2,1)S(1)} %bitcast.28), channel_id=1, source_target_pairs={{0,24},{1,25},{2,26},{3,27},{8,16},{9,17},{10,18},{11,19},{16,40},... | collective-permute-start | bytes 589832 | tf_op jit(solution)/shard_map/ppermute | solution.py:335
  44.4 28.0 %all-to-all-start.2 = ((f32[64,1,640]{2,1,0:T(1,128)}), f32[64,1,640]{2,1,0:T(1,128)S(1)}, u32[]{:S(2)}, u32[]{:S(2)}) async-start(f32[64,1,640]{2,1,0:T(1,128)} %get-tuple-element.21), calls=%async_computation.2 | async-start | bytes 327680 | tf_op jit(solution)/shard_map/all_to_all | solution.py:366
  59.7 8.9 %collective-permute-start.1 = (bf16[384,256]{1,0:T(8,128)(2,1)S(1)}, bf16[384,256]{1,0:T(8,128)(2,1)S(1)}, u32[]{:S(2)}, u32[]{:S(2)}) collective-permute-start(bf16[384,256]{1,0:T(8,128)(2,1)S(1)} %get-tuple-element.19), channel_id=1, source_target_pairs={{4,28},{5,29},{6,30},{7,31},{12,20},{13,21},{14,22},{15,23},{16,8}... | collective-permute-start | bytes 589832 | tf_op jit(solution)/shard_map/ppermute | solution.py:364
  72.7 20.0 %copy-start = (bf16[1,64,5120]{2,1,0:T(8,128)(2,1)S(1)}, bf16[1,64,5120]{2,1,0:T(8,128)(2,1)}, u32[]{:S(2)}) copy-start(bf16[1,64,5120]{2,1,0:T(8,128)(2,1)} %param.7) | copy-start | bytes 1966084
  72.7 20.0 %copy-start.1 = (bf16[1,64,1024]{2,1,0:T(8,128)(2,1)S(1)}, bf16[1,64,1024]{2,1,0:T(8,128)(2,1)}, u32[]{:S(2)}) copy-start(bf16[1,64,1024]{2,1,0:T(8,128)(2,1)} %param.8) | copy-start | bytes 393220
  72.7 20.0 %copy-start.2 = (f32[5120]{0:T(1024)S(1)}, f32[5120]{0:T(1024)}, u32[]{:S(2)}) copy-start(f32[5120]{0:T(1024)} %param.11) | copy-start | bytes 61444
  72.8 20.0 %copy-start.3 = (f32[1024]{0:T(1024)S(1)}, f32[1024]{0:T(1024)}, u32[]{:S(2)}) copy-start(f32[1024]{0:T(1024)} %param.12) | copy-start | bytes 12292

commit v4 on v3

--- a/solution.py
+++ b/solution.py
@@ -18,7 +18,7 @@
 WINDOW = 2 * SPAN - 1
 Q_COLS = GROUP * HEAD_DIM
 KV_COLS = 2 * HEAD_DIM
-TILES = GROUP + 2
+CHIPS = TEAM // 2
 SUM_ROWS = 16
 SCALE = 1.0 / math.sqrt(HEAD_DIM)
 LOG2E = math.log2(math.e)
@@ -108,18 +108,23 @@
 
 
 def attention_kernel(
+    slot_ref,
     qd_ref,
     own_ref,
     near_ref,
     flags_ref,
-    dq_ref,
     d_own_ref,
     d_near_ref,
     part_ref,
+    dq_0_ref,
+    dq_1_ref,
+    dq_2_ref,
+    dq_3_ref,
     s_ref,
     g_ref,
     p_ref,
     ds_ref,
+    dq_ref,
 ):
     def window(at, kind):
         columns = slice(kind * HEAD_DIM, (kind + 1) * HEAD_DIM)
@@ -205,6 +210,9 @@
     for j in range(GROUP):
         lanes = slice(j * HEAD_DIM, (j + 1) * HEAD_DIM)
         part_ref[:, :, lanes] = jnp.broadcast_to(q_part[j][None], (copies, 1, HEAD_DIM))
+    for apart, out_ref in enumerate((dq_0_ref, dq_1_ref, dq_2_ref, dq_3_ref)):
+        for core in range(2):
+            out_ref[core] = dq_ref[2 * ((slot_ref[0] // 2) ^ apart) + core]
     for at in range(WINDOW):
         grad = d_keys[at] * SCALE
         target, row = (d_near_ref, at) if at < SPAN - 1 else (d_own_ref, at - SPAN + 1)
@@ -213,7 +221,9 @@
         target[span, HEAD_DIM:] = d_values[at].astype(target.dtype)
 
 
-def gather_kernel(own_ref, near_ref, dq_ref, sums_ref, out_ref):
+def gather_kernel(
+    slot_ref, own_ref, near_ref, sums_ref, dq_0_ref, dq_1_ref, dq_2_ref, dq_3_ref, out_ref, keep_ref, give_ref
+):
     half = BLOCK // 2
     rest = jnp.sum(sums_ref[...], axis=0)
     pieces = []
@@ -229,11 +239,13 @@
         if slot >= 2:
             total = total + near_ref[(slot - 2) * half : (slot - 1) * half].astype(F32)
         total = total.astype(BF16)
-        tiles = [dq_ref[slot, :, j * HEAD_DIM : (j + 1) * HEAD_DIM] for j in range(GROUP)]
-        tiles += [total[:, :HEAD_DIM], total[:, HEAD_DIM:]]
-        for at, tile in enumerate(tiles):
-            out_ref[slot, at * half : (at + 1) * half] = tile
-        out_ref[slot, TILES * half :] = sums
+        out_ref[slot, :half] = total[:, :HEAD_DIM]
+        out_ref[slot, half:BLOCK] = total[:, HEAD_DIM:]
+        out_ref[slot, BLOCK:] = sums
+    core = slot_ref[0] % 2
+    for apart, dq_ref in enumerate((dq_0_ref, dq_1_ref, dq_2_ref, dq_3_ref)):
+        keep_ref[apart] = dq_ref[core]
+        give_ref[apart] = dq_ref[1 - core]
 
 
 def norm_backward(rows, gain, grad):
@@ -244,14 +256,20 @@
     return (inverse * scaled - values * (inverse * inverse * inverse * inner)).astype(BF16)
 
 
-def final_kernel(
+def query_back_kernel(head_ref, query_ref, gain_ref, kept_ref, given_ref, out_ref, grad_ref):
+    for apart in range(CHIPS):
+        for other, source in enumerate((kept_ref, given_ref)):
+            head = head_ref[0] ^ (2 * apart + other)
+            grad_ref[:, pl.ds(pl.multiple_of(head * Q_COLS, Q_COLS), Q_COLS)] = source[apart]
+    out_ref[...] = norm_backward(query_ref[...], gain_ref[...], grad_ref[...])
+
+
+def key_back_kernel(
     mask_ref,
-    query_ref,
     key_ref,
     query_gain_ref,
     key_gain_ref,
     back_ref,
-    d_query_ref,
     d_key_ref,
     d_value_ref,
     d_query_gain_ref,
@@ -259,20 +277,13 @@
 ):
     half = BLOCK // 2
     slots = [head ^ mask_ref[0] for head in range(TEAM)]
-
-    def tile(slot, at):
-        return back_ref[slot, at * half : (at + 1) * half]
-
-    grad = jnp.concatenate([tile(slot, at) for slot in slots for at in range(GROUP)], axis=1)
-    d_query_ref[...] = norm_backward(query_ref[...], query_gain_ref[...], grad)
-    grad = jnp.concatenate([tile(slot, GROUP) for slot in slots], axis=1)
+    grad = jnp.concatenate([back_ref[slot, :half] for slot in slots], axis=1)
     d_key_ref[...] = norm_backward(key_ref[...], key_gain_ref[...], grad)
-    count = Q_COLS // HEAD_DIM
     for head, slot in enumerate(slots):
         columns = slice(head * HEAD_DIM, (head + 1) * HEAD_DIM)
-        d_value_ref[:, columns] = tile(slot, GROUP + 1)
-        pieces = back_ref[slot, TILES * half :].astype(F32)
-        sums = pieces[:count] + pieces[count : 2 * count] + pieces[2 * count : 3 * count]
+        d_value_ref[:, columns] = back_ref[slot, half:BLOCK]
+        pieces = back_ref[slot, BLOCK:].astype(F32)
+        sums = pieces[:GROUP] + pieces[GROUP : 2 * GROUP] + pieces[2 * GROUP : 3 * GROUP]
         for j in range(GROUP):
             at = slice((head * GROUP + j) * HEAD_DIM, (head * GROUP + j + 1) * HEAD_DIM)
             d_query_gain_ref[:, at] = sums[j : j + 1] / query_gain_ref[:, at]
@@ -307,6 +318,8 @@
     teams, by_head = layout(seq_count)
     span, slot, mask = team_of(lax.axis_index("seq"), lax.axis_index("head"), seq_count)
     mask_scalar = mask[None].astype(jnp.int32)
+    slot_scalar = slot[None].astype(jnp.int32)
+    head_scalar = (slot ^ mask)[None].astype(jnp.int32)
     span_scalar = span[None].astype(jnp.int32)
     rows = query_raw.shape[1]
     query_rows, key_rows, value_rows, grad_rows = (
@@ -345,41 +358,60 @@
     )
     qd = exchange(qd_send).reshape(TEAM * rows, 2 * Q_COLS)
     window = SPAN * BLOCK
-    dq, d_own, d_near, part = call(
+    d_own, d_near, part, *dq = call(
         attention_kernel,
         (
-            jax.ShapeDtypeStruct((TEAM, rows, Q_COLS), BF16),
             jax.ShapeDtypeStruct((window, KV_COLS), F32),
             jax.ShapeDtypeStruct((window - BLOCK, KV_COLS), BF16),
             jax.ShapeDtypeStruct((seq_count, 1, Q_COLS), F32),
-        ),
-        (qd, own, near, flags),
+        )
+        + (jax.ShapeDtypeStruct((2, rows, Q_COLS), BF16),) * CHIPS,
+        (slot_scalar, qd, own, near, flags),
+        smem=1,
         scratch=[
             pltpu.VMEM((SPAN, window, Q_COLS), F32),
             pltpu.VMEM((SPAN, window, Q_COLS), F32),
             pltpu.VMEM((SPAN, window, Q_COLS), BF16),
             pltpu.VMEM((SPAN, window, Q_COLS), BF16),
+            pltpu.VMEM((TEAM, rows, Q_COLS), BF16),
         ],
     )
+
+    def within(array, apart):
+        pairs = [(team[at], team[at ^ apart]) for team in teams for at in range(TEAM)]
+        return lax.ppermute(array, axes, sorted(pairs))
+
     back_near = lax.ppermute(d_near, axes, backward)
-
     sums = lax.all_to_all(part, axes, 0, 0, axis_index_groups=by_head, tiled=True)
-    back_send = call(
+    dq = [dq[0]] + [within(dq[apart], 2 * apart) for apart in range(1, CHIPS)]
+    back_send, keep, give = call(
         gather_kernel,
-        jax.ShapeDtypeStruct((TEAM, TILES * rows + SUM_ROWS, HEAD_DIM), BF16),
-        (d_own, back_near, dq, sums),
+        (
+            jax.ShapeDtypeStruct((TEAM, 2 * rows + SUM_ROWS, HEAD_DIM), BF16),
+            jax.ShapeDtypeStruct((CHIPS, rows, Q_COLS), BF16),
+            jax.ShapeDtypeStruct((CHIPS, rows, Q_COLS), BF16),
+        ),
+        (slot_scalar, d_own, back_near, sums, *dq),
+        smem=1,
     )
     back = exchange(back_send)
-    d_query, d_key, d_value, d_query_gain, d_key_gain = call(
-        final_kernel,
+    given = within(give, 1)
+    d_query = call(
+        query_back_kernel,
+        jax.ShapeDtypeStruct(query_rows.shape, BF16),
+        (head_scalar, query_rows, query_gain_row, keep, given),
+        smem=1,
+        scratch=[pltpu.VMEM(query_rows.shape, BF16)],
+    )
+    d_key, d_value, d_query_gain, d_key_gain = call(
+        key_back_kernel,
         (
-            jax.ShapeDtypeStruct(query_rows.shape, BF16),
             jax.ShapeDtypeStruct(key_rows.shape, BF16),
             jax.ShapeDtypeStruct(value_rows.shape, BF16),
             jax.ShapeDtypeStruct(query_gain_row.shape, F32),
             jax.ShapeDtypeStruct(key_gain_row.shape, F32),
         ),
-        (mask_scalar, query_rows, key_rows, query_gain_row, key_gain_row, back),
+        (mask_scalar, key_rows, query_gain_row, key_gain_row, back),
         smem=1,
     )
     return d_query[None], d_key[None], d_value[None], d_query_gain[0], d_key_gain[0]

time: 94.9 us -> 92.8 us (0.978)
  the two profiles are of different devices: /device:TPU:1 before, /device:TPU:40 now
where the time goes in v4:
time: 92.8 us; the launch traced here: 92.2 us
  starting transfers between devices  51 us (55%)
  waiting for transfers between devices  25.9 us (28%)
  Pallas kernels  14.4 us (16%)
    all_to_all x1, starting transfers between devices, body(): lax.all_to_all(part, axes, 0, 0, axis_index_groups=by_head, tiled=True)  17 us
    pallas_call x6, Pallas kernels, call(): pl.pallas_call(kernel, out_shape=out_shape, in_specs=[scalar] * smem + [g...  14.4 us
    all_to_all x3, waiting for transfers between devices, exchange(): lax.all_to_all(array, axes, 0, 0, axis_index_groups=teams, tiled=True)  13.2 us
    all_to_all x3, starting transfers between devices, exchange(): lax.all_to_all(array, axes, 0, 0, axis_index_groups=teams, tiled=True)  11.8 us
    ppermute x4, starting transfers between devices, within(): return lax.ppermute(array, axes, sorted(pairs))  11.5 us
    ppermute x4, waiting for transfers between devices, within(): return lax.ppermute(array, axes, sorted(pairs))  6.64 us
    ppermute x1, waiting for transfers between devices, body(): near = lax.ppermute(own[BLOCK:], axes, onward)  6.09 us
    ppermute x1, starting transfers between devices, body(): back_near = lax.ppermute(d_near, axes, backward)  5.48 us
  transfers between devices with their start and end apart: 10, of which 6 were waited for; matrix products, arithmetic and copies ran while one was open for 0% of the time, Pallas kernels for 5%

profile of v4, /device:TPU:40, one launch (start us, length us, event | category | flops | bytes accessed | tf_op | source)
XLA Modules:
  0.0 92.2 jit_solution(4469265555398529813)
XLA Ops:
  0.7 1.8 %shard_map.111 = bf16[8,64,256]{2,1,0:T(8,128)(2,1)} custom-call(s32[1]{0:T(128)} %bitcast.4.mask_ref, bf16[64,1024]{1,0:T(8,128)(2,1)} %bitcast.23, bf16[64,1024]{1,0:T(8,128)(2,1)} %bitcast.33, f32[1,1024]{1,0:T(1,128)} %bitcast.28), custom_call_target="tpu_custom_call" | custom-call | bytes 1024 | tf_op jit(solution)/shard_map/pallas_call | solution.py:41
  2.5 4.6 %all-to-all-start.1 = ((bf16[8,64,256]{2,1,0:T(8,128)(2,1)}), bf16[8,64,256]{2,1,0:T(8,128)(2,1)S(1)}, u32[]{:S(2)}, u32[]{:S(2)}) async-start(bf16[8,64,256]{2,1,0:T(8,128)(2,1)} %shard_map.111), calls=%async_computation.1 | async-start | bytes 524288 | tf_op jit(solution)/shard_map/all_to_all | solution.py:334
  7.1 2.8 %shard_map.110 = (bf16[8,64,1280]{2,1,0:T(8,128)(2,1)}, s32[8,128]{1,0:T(8,128)}) custom-call(s32[1]{0:T(128)} %bitcast.4.mask_ref, s32[1]{0:T(128)} %bitcast.5.span_ref, bf16[64,5120]{1,0:T(8,128)(2,1)} %bitcast.20, bf16[64,5120]{1,0:T(8,128)(2,1)} %bitcast.30, f32[1,5120]{1,0:T(1,128)} %bitcast.25, s32[1,96]{1,0:T(1,128)} %bitcast.34), custom_call_target="tpu_custom_call" | custom-call | bytes 1024 | tf_op jit(solution)/shard_map/pallas_call | solution.py:41
  10.0 4.1 %all-to-all-done.1 = bf16[8,64,256]{2,1,0:T(8,128)(2,1)S(1)} async-done(((bf16[8,64,256]{2,1,0:T(8,128)(2,1)}), bf16[8,64,256]{2,1,0:T(8,128)(2,1)S(1)}, u32[]{:S(2)}, u32[]{:S(2)}) %all-to-all-start.1) | async-done | bytes 262176 | tf_op jit(solution)/shard_map/all_to_all | solution.py:334
  14.1 3.7 %all-to-all-start = ((bf16[8,64,1280]{2,1,0:T(8,128)(2,1)}), bf16[8,64,1280]{2,1,0:T(8,128)(2,1)S(1)}, u32[]{:S(2)}, u32[]{:S(2)}) async-start(bf16[8,64,1280]{2,1,0:T(8,128)(2,1)} %get-tuple-element.21), calls=%async_computation | async-start | bytes 2621440 | tf_op jit(solution)/shard_map/all_to_all | solution.py:334
  17.8 5.1 %collective-permute-start = (bf16[384,256]{1,0:T(8,128)(2,1)S(1)}, bf16[384,256]{1,0:T(8,128)(2,1)S(1)}, u32[]{:S(2)}, u32[]{:S(2)}) collective-permute-start(bf16[384,256]{1,0:T(8,128)(2,1)S(1)} %bitcast.32), channel_id=1, source_target_pairs={{0,24},{1,25},{2,26},{3,27},{8,16},{9,17},{10,18},{11,19},{16,40},... | collective-permute-start | bytes 589832 | tf_op jit(solution)/shard_map/ppermute | solution.py:348
  22.9 6.1 %collective-permute-done.near_ref = bf16[384,256]{1,0:T(8,128)(2,1)S(1)} collective-permute-done((bf16[384,256]{1,0:T(8,128)(2,1)S(1)}, bf16[384,256]{1,0:T(8,128)(2,1)S(1)}, u32[]{:S(2)}, u32[]{:S(2)}) %collective-permute-start) | collective-permute-done | bytes 196640 | tf_op jit(solution)/shard_map/ppermute | solution.py:348
  29.0 6.9 %all-to-all-done = bf16[8,64,1280]{2,1,0:T(8,128)(2,1)S(1)} async-done(((bf16[8,64,1280]{2,1,0:T(8,128)(2,1)}), bf16[8,64,1280]{2,1,0:T(8,128)(2,1)S(1)}, u32[]{:S(2)}, u32[]{:S(2)}) %all-to-all-start) | async-done | bytes 1310752 | tf_op jit(solution)/shard_map/all_to_all | solution.py:334
  35.9 6.5 %shard_map.112 = (f32[512,256]{1,0:T(8,128)S(1)}, bf16[384,256]{1,0:T(8,128)(2,1)S(1)}, f32[64,1,640]{2,1,0:T(1,128)}, bf16[2,64,640]{2,1,0:T(8,128)(2,1)S(1)}, ...) custom-call(s32[1]{0:T(128)} %bitcast.3.slot_ref, ...), custom_call_target="tpu_custom_call" | custom-call | bytes 1024 | tf_op jit(solution)/shard_map/pallas_call | solution.py:41
  42.4 17.0 %all-to-all-start.2 = ((f32[64,1,640]{2,1,0:T(1,128)}), f32[64,1,640]{2,1,0:T(1,128)S(1)}, u32[]{:S(2)}, u32[]{:S(2)}) async-start(f32[64,1,640]{2,1,0:T(1,128)} %get-tuple-element.25), calls=%async_computation.2 | async-start | bytes 327680 | tf_op jit(solution)/shard_map/all_to_all | solution.py:385
  59.5 5.5 %collective-permute-start.1 = (bf16[384,256]{1,0:T(8,128)(2,1)S(1)}, bf16[384,256]{1,0:T(8,128)(2,1)S(1)}, u32[]{:S(2)}, u32[]{:S(2)}) collective-permute-start(bf16[384,256]{1,0:T(8,128)(2,1)S(1)} %get-tuple-element.24), channel_id=1, source_target_pairs={{4,28},{5,29},{6,30},{7,31},{12,20},{13,21},{14,22},{15,23},{16,8}... | collective-permute-start | bytes 589832 | tf_op jit(solution)/shard_map/ppermute | solution.py:384
  64.9 3.9 %collective-permute-start.2 = (bf16[2,64,640]{2,1,0:T(8,128)(2,1)S(1)}, bf16[2,64,640]{2,1,0:T(8,128)(2,1)S(1)}, u32[]{:S(2)}, u32[]{:S(2)}) collective-permute-start(bf16[2,64,640]{2,1,0:T(8,128)(2,1)S(1)} %get-tuple-element.27), channel_id=1, source_target_pairs={{0,2},{1,3},{2,0},{3,1},{4,6},{5,7},{6,4},{7,5},{8,10},{9,11},{10,... | collective-permute-start | bytes 491528 | tf_op jit(solution)/shard_map/ppermute | solution.py:382
  68.9 1.9 %collective-permute-start.3 = (bf16[2,64,640]{2,1,0:T(8,128)(2,1)S(1)}, bf16[2,64,640]{2,1,0:T(8,128)(2,1)S(1)}, u32[]{:S(2)}, u32[]{:S(2)}) collective-permute-start(bf16[2,64,640]{2,1,0:T(8,128)(2,1)S(1)} %get-tuple-element.28), channel_id=1, source_target_pairs={{0,8},{1,9},{2,10},{3,11},{4,12},{5,13},{6,14},{7,15},{8,0},{9,1},... | collective-permute-start | bytes 491528 | tf_op jit(solution)/shard_map/ppermute | solution.py:382
  70.8 3.4 %collective-permute-start.4 = (bf16[2,64,640]{2,1,0:T(8,128)(2,1)S(1)}, bf16[2,64,640]{2,1,0:T(8,128)(2,1)S(1)}, u32[]{:S(2)}, u32[]{:S(2)}) collective-permute-start(bf16[2,64,640]{2,1,0:T(8,128)(2,1)S(1)} %get-tuple-element.29), channel_id=1, source_target_pairs={{0,10},{1,11},{2,8},{3,9},{4,14},{5,15},{6,12},{7,13},{8,2},{9,3},... | collective-permute-start | bytes 491528 | tf_op jit(solution)/shard_map/ppermute | solution.py:382
  74.2 0.0 collective-permute-done.2.dq_1_ref
  74.2 5.4 %collective-permute-done.3.dq_2_ref = bf16[2,64,640]{2,1,0:T(8,128)(2,1)S(1)} collective-permute-done((bf16[2,64,640]{2,1,0:T(8,128)(2,1)S(1)}, bf16[2,64,640]{2,1,0:T(8,128)(2,1)S(1)}, u32[]{:S(2)}, u32[]{:S(2)}) %collective-permute-start.3) | collective-permute-done | bytes 163872 | tf_op jit(solution)/shard_map/ppermute | solution.py:382
  79.6 0.0 collective-permute-done.1.near_ref
  79.6 0.9 %shard_map.113 = (bf16[8,144,128]{2,1,0:T(8,128)(2,1)}, bf16[4,64,640]{2,1,0:T(8,128)(2,1)S(1)}, bf16[4,64,640]{2,1,0:T(8,128)(2,1)S(1)}) custom-call(s32[1]{0:T(128)} %bitcast.3.slot_ref, f32[512,256]{1,0:T(8,128)S(1)} %get-tuple-element.23.own_ref, bf16[384,256]{1,0:T(8,128)(2,1)S(1)} %collective-permute-done.1.near_ref, ...), custom_call_target="tpu_custom_call" | custom-call | bytes 1024 | tf_op jit(solution)/shard_map/pallas_call | solution.py:41
  80.6 3.6 %all-to-all-start.3 = ((bf16[8,144,128]{2,1,0:T(8,128)(2,1)}), bf16[8,144,128]{2,1,0:T(8,128)(2,1)S(1)}, u32[]{:S(2)}, u32[]{:S(2)}) async-start(bf16[8,144,128]{2,1,0:T(8,128)(2,1)} %get-tuple-element.32), calls=%async_computation.3 | async-start | bytes 589824 | tf_op jit(solution)/shard_map/all_to_all | solution.py:334
  84.1 2.3 %collective-permute-start.5 = (bf16[4,64,640]{2,1,0:T(8,128)(2,1)S(1)}, bf16[4,64,640]{2,1,0:T(8,128)(2,1)S(1)}, u32[]{:S(2)}, u32[]{:S(2)}) collective-permute-start(bf16[4,64,640]{2,1,0:T(8,128)(2,1)S(1)} %get-tuple-element.31), channel_id=1, source_target_pairs={{0,1},{1,0},{2,3},{3,2},{4,5},{5,4},{6,7},{7,6},{8,9},{9,8},{10,11... | collective-permute-start | bytes 983048 | tf_op jit(solution)/shard_map/ppermute | solution.py:382
  86.4 1.2 %collective-permute-done.5.given_ref = bf16[4,64,640]{2,1,0:T(8,128)(2,1)S(1)} collective-permute-done((bf16[4,64,640]{2,1,0:T(8,128)(2,1)S(1)}, bf16[4,64,640]{2,1,0:T(8,128)(2,1)S(1)}, u32[]{:S(2)}, u32[]{:S(2)}) %collective-permute-start.5) | collective-permute-done | bytes 327712 | tf_op jit(solution)/shard_map/ppermute | solution.py:382
  87.7 1.5 %shard_map.114 = bf16[64,5120]{1,0:T(8,128)(2,1)} custom-call(s32[1]{0:T(128)} %bitcast.head_ref, bf16[64,5120]{1,0:T(8,128)(2,1)S(1)} %bitcast.21, f32[1,5120]{1,0:T(1,128)S(1)} %bitcast.26, bf16[4,64,640]{2,1,0:T(8,128)(2,1)S(1)} %get-tuple-element.30.kept_ref, bf16[4,64,640]{2,1,0:T(8,128)(2,1)S(1)} %collective-permute-done.5.given_ref), custom_call_target="tpu_custom_call" | custom-call | bytes 1024 | tf_op jit(solution)/shard_map/pallas_call | solution.py:41
  89.1 2.2 %all-to-all-done.3.back_ref = bf16[8,144,128]{2,1,0:T(8,128)(2,1)S(1)} async-done(((bf16[8,144,128]{2,1,0:T(8,128)(2,1)}), bf16[8,144,128]{2,1,0:T(8,128)(2,1)S(1)}, u32[]{:S(2)}, u32[]{:S(2)}) %all-to-all-start.3) | async-done | bytes 294944 | tf_op jit(solution)/shard_map/all_to_all | solution.py:334
  91.3 0.9 shard_map.115
  (13 shorter events, 0.0 us)
Async XLA Ops:
  2.5 11.5 %all-to-all-start.1 = ((bf16[8,64,256]{2,1,0:T(8,128)(2,1)}), bf16[8,64,256]{2,1,0:T(8,128)(2,1)S(1)}, u32[]{:S(2)}, u32[]{:S(2)}) async-start(bf16[8,64,256]{2,1,0:T(8,128)(2,1)} %shard_map.111), calls=%async_computation.1 | async-start | bytes 524288 | tf_op jit(solution)/shard_map/all_to_all | solution.py:334
  14.1 21.9 %copy-start.4 = (s32[8,128]{1,0:T(8,128)S(1)}, s32[8,128]{1,0:T(8,128)}, u32[]{:S(2)}) copy-start(s32[8,128]{1,0:T(8,128)} %get-tuple-element.22.flags_ref) | copy-start | bytes 12292
  14.1 21.9 %all-to-all-start = ((bf16[8,64,1280]{2,1,0:T(8,128)(2,1)}), bf16[8,64,1280]{2,1,0:T(8,128)(2,1)S(1)}, u32[]{:S(2)}, u32[]{:S(2)}) async-start(bf16[8,64,1280]{2,1,0:T(8,128)(2,1)} %get-tuple-element.21), calls=%async_computation | async-start | bytes 2621440 | tf_op jit(solution)/shard_map/all_to_all | solution.py:334
  17.8 11.2 %collective-permute-start = (bf16[384,256]{1,0:T(8,128)(2,1)S(1)}, bf16[384,256]{1,0:T(8,128)(2,1)S(1)}, u32[]{:S(2)}, u32[]{:S(2)}) collective-permute-start(bf16[384,256]{1,0:T(8,128)(2,1)S(1)} %bitcast.32), channel_id=1, source_target_pairs={{0,24},{1,25},{2,26},{3,27},{8,16},{9,17},{10,18},{11,19},{16,40},... | collective-permute-start | bytes 589832 | tf_op jit(solution)/shard_map/ppermute | solution.py:348
  42.4 45.3 %copy-start = (bf16[1,64,5120]{2,1,0:T(8,128)(2,1)S(1)}, bf16[1,64,5120]{2,1,0:T(8,128)(2,1)}, u32[]{:S(2)}) copy-start(bf16[1,64,5120]{2,1,0:T(8,128)(2,1)} %param.7) | copy-start | bytes 1966084
  42.4 45.3 %copy-start.2 = (f32[5120]{0:T(1024)S(1)}, f32[5120]{0:T(1024)}, u32[]{:S(2)}) copy-start(f32[5120]{0:T(1024)} %param.11) | copy-start | bytes 61444
  42.4 37.2 %all-to-all-start.2 = ((f32[64,1,640]{2,1,0:T(1,128)}), f32[64,1,640]{2,1,0:T(1,128)S(1)}, u32[]{:S(2)}, u32[]{:S(2)}) async-start(f32[64,1,640]{2,1,0:T(1,128)} %get-tuple-element.25), calls=%async_computation.2 | async-start | bytes 327680 | tf_op jit(solution)/shard_map/all_to_all | solution.py:385
  59.5 20.1 %collective-permute-start.1 = (bf16[384,256]{1,0:T(8,128)(2,1)S(1)}, bf16[384,256]{1,0:T(8,128)(2,1)S(1)}, u32[]{:S(2)}, u32[]{:S(2)}) collective-permute-start(bf16[384,256]{1,0:T(8,128)(2,1)S(1)} %get-tuple-element.24), channel_id=1, source_target_pairs={{4,28},{5,29},{6,30},{7,31},{12,20},{13,21},{14,22},{15,23},{16,8}... | collective-permute-start | bytes 589832 | tf_op jit(solution)/shard_map/ppermute | solution.py:384
  64.9 9.2 %collective-permute-start.2 = (bf16[2,64,640]{2,1,0:T(8,128)(2,1)S(1)}, bf16[2,64,640]{2,1,0:T(8,128)(2,1)S(1)}, u32[]{:S(2)}, u32[]{:S(2)}) collective-permute-start(bf16[2,64,640]{2,1,0:T(8,128)(2,1)S(1)} %get-tuple-element.27), channel_id=1, source_target_pairs={{0,2},{1,3},{2,0},{3,1},{4,6},{5,7},{6,4},{7,5},{8,10},{9,11},{10,... | collective-permute-start | bytes 491528 | tf_op jit(solution)/shard_map/ppermute | solution.py:382
  68.9 10.7 %collective-permute-start.3 = (bf16[2,64,640]{2,1,0:T(8,128)(2,1)S(1)}, bf16[2,64,640]{2,1,0:T(8,128)(2,1)S(1)}, u32[]{:S(2)}, u32[]{:S(2)}) collective-permute-start(bf16[2,64,640]{2,1,0:T(8,128)(2,1)S(1)} %get-tuple-element.28), channel_id=1, source_target_pairs={{0,8},{1,9},{2,10},{3,11},{4,12},{5,13},{6,14},{7,15},{8,0},{9,1},... | collective-permute-start | bytes 491528 | tf_op jit(solution)/shard_map/ppermute | solution.py:382
  70.8 8.8 %collective-permute-start.4 = (bf16[2,64,640]{2,1,0:T(8,128)(2,1)S(1)}, bf16[2,64,640]{2,1,0:T(8,128)(2,1)S(1)}, u32[]{:S(2)}, u32[]{:S(2)}) collective-permute-start(bf16[2,64,640]{2,1,0:T(8,128)(2,1)S(1)} %get-tuple-element.29), channel_id=1, source_target_pairs={{0,10},{1,11},{2,8},{3,9},{4,14},{5,15},{6,12},{7,13},{8,2},{9,3},... | collective-permute-start | bytes 491528 | tf_op jit(solution)/shard_map/ppermute | solution.py:382
  80.6 10.8 %copy-start.1 = (bf16[1,64,1024]{2,1,0:T(8,128)(2,1)S(1)}, bf16[1,64,1024]{2,1,0:T(8,128)(2,1)}, u32[]{:S(2)}) copy-start(bf16[1,64,1024]{2,1,0:T(8,128)(2,1)} %param.8) | copy-start | bytes 393220
  80.6 10.8 %copy-start.3 = (f32[1024]{0:T(1024)S(1)}, f32[1024]{0:T(1024)}, u32[]{:S(2)}) copy-start(f32[1024]{0:T(1024)} %param.12) | copy-start | bytes 12292
  80.6 10.8 %all-to-all-start.3 = ((bf16[8,144,128]{2,1,0:T(8,128)(2,1)}), bf16[8,144,128]{2,1,0:T(8,128)(2,1)S(1)}, u32[]{:S(2)}, u32[]{:S(2)}) async-start(bf16[8,144,128]{2,1,0:T(8,128)(2,1)} %get-tuple-element.32), calls=%async_computation.3 | async-start | bytes 589824 | tf_op jit(solution)/shard_map/all_to_all | solution.py:334
  84.1 3.5 %collective-permute-start.5 = (bf16[4,64,640]{2,1,0:T(8,128)(2,1)S(1)}, bf16[4,64,640]{2,1,0:T(8,128)(2,1)S(1)}, u32[]{:S(2)}, u32[]{:S(2)}) collective-permute-start(bf16[4,64,640]{2,1,0:T(8,128)(2,1)S(1)} %get-tuple-element.31), channel_id=1, source_target_pairs={{0,1},{1,0},{2,3},{3,2},{4,5},{5,4},{6,7},{7,6},{8,9},{9,8},{10,11... | collective-permute-start | bytes 983048 | tf_op jit(solution)/shard_map/ppermute | solution.py:382

commit v5 on v4

--- a/solution.py
+++ b/solution.py
@@ -24,11 +24,11 @@
 LOG2E = math.log2(math.e)
 F32 = jnp.float32
 BF16 = jnp.bfloat16
-VMEM_LIMIT = 32 * 1024 * 1024
+VMEM_LIMIT = 14 * 1024 * 1024
 VMEM_ALL = 63 * 1024 * 1024
 
 
-def call(kernel, out_shape, args, smem=0, flops=0, size=1024, scratch=(), far=False):
+def call(kernel, out_shape, args, smem=0, smem_out=0, flops=0, size=1024, scratch=(), far=False):
     whole = pl.BlockSpec(memory_space=pltpu.VMEM)
     scalar = pl.BlockSpec(memory_space=pltpu.SMEM)
     given = pl.BlockSpec(memory_space=pltpu.HBM) if far else whole
@@ -42,7 +42,9 @@
         kernel,
         out_shape=out_shape,
         in_specs=[scalar] * smem + [given] * (len(args) - smem),
-        out_specs=whole if single else [whole] * len(out_shape),
+        out_specs=whole
+        if single
+        else [whole] * (len(out_shape) - smem_out) + [scalar] * smem_out,
         scratch_shapes=scratch,
         compiler_params=pltpu.CompilerParams(vmem_limit_bytes=VMEM_ALL if far else VMEM_LIMIT),
         cost_estimate=pl.CostEstimate(flops=flops, bytes_accessed=size, transcendentals=0),
@@ -79,7 +81,7 @@
 
 
 def query_norm_kernel(mask_ref, span_ref, *refs):
-    sources, (out_ref, flags_ref), targets, semaphores = refs[:4], refs[4:6], refs[6:10], refs[10]
+    sources, (out_ref, counts_ref), targets, semaphores = refs[:4], refs[4:6], refs[6:10], refs[10]
     query_ref, grad_ref, gain_ref, docs_ref = fetched(sources, targets, semaphores)
     values = query_ref[...].astype(F32)
     normed = (values * inverse_rms(values) * gain_ref[...]).astype(BF16)
@@ -98,9 +100,11 @@
     places = first + lax.broadcasted_iota(jnp.int32, (count, 128), 1)
     found = jnp.sum((ends <= places).astype(jnp.int32), axis=0, keepdims=True)
     found = jnp.where(places[:1] >= 0, found, -1)
-    flags_ref[...] = jnp.zeros_like(flags_ref)
-    for at in range(WINDOW):
-        flags_ref[at : at + 1, :] = jnp.broadcast_to(found[:, at : at + 1], (1, 128))
+    lane = lax.broadcasted_iota(jnp.int32, found.shape, 1)
+    for z in range(SPAN):
+        mine = found[:, SPAN - 1 + z : SPAN + z]
+        near = (lane >= z) & (lane < z + SPAN)
+        counts_ref[z] = jnp.sum(((found == mine) & near).astype(jnp.int32))
 
 
 def contract(left, right, dims):
@@ -109,10 +113,10 @@
 
 def attention_kernel(
     slot_ref,
+    counts_ref,
     qd_ref,
     own_ref,
     near_ref,
-    flags_ref,
     d_own_ref,
     d_near_ref,
     part_ref,
@@ -125,53 +129,40 @@
     p_ref,
     ds_ref,
     dq_ref,
+    kv_ref,
+    d_kv_ref,
+    sums_ref,
 ):
-    def window(at, kind):
-        columns = slice(kind * HEAD_DIM, (kind + 1) * HEAD_DIM)
-        ref, row = (near_ref, at) if at < SPAN - 1 else (own_ref, at - SPAN + 1)
-        return ref[row * BLOCK : (row + 1) * BLOCK, columns]
-
+    border = (SPAN - 1) * BLOCK
+    kv_ref[:border] = near_ref[...]
+    kv_ref[border:] = own_ref[...]
+    d_kv_ref[...] = jnp.zeros_like(d_kv_ref)
+    sums_ref[...] = jnp.zeros_like(sums_ref)
     causal = lax.broadcasted_iota(jnp.int32, (BLOCK, BLOCK), 0) <= lax.broadcasted_iota(
         jnp.int32, (BLOCK, BLOCK), 1
     )
     diagonal = jnp.where(causal, 0.0, MASKED)
     factor = SCALE * LOG2E
     half = BLOCK // 2
-    copies = part_ref.shape[0]
-    d_keys = [None] * WINDOW
-    d_values = [None] * WINDOW
-    q_part = [0.0] * GROUP
-    for z in range(SPAN):
-        rows = slice(z * BLOCK, (z + 1) * BLOCK)
-        blocks = list(range(z, z + SPAN))
-
-        def heads_of(kind):
-            base = kind * Q_COLS
-            return jnp.concatenate(
-                [
-                    qd_ref[rows, base + j * HEAD_DIM : base + (j + 1) * HEAD_DIM]
-                    for j in range(GROUP)
-                ],
-                axis=0,
-            )
-
-        queries, grads = heads_of(0), heads_of(1)
-        keys = jnp.concatenate([window(at, 0) for at in blocks], axis=0)
-        values = jnp.concatenate([window(at, 1) for at in blocks], axis=0)
-        s_ref[z] = contract(keys, queries, ((1,), (1,)))
-        g_ref[z] = contract(values, grads, ((1,), (1,)))
-        biases = []
-        for place, at in enumerate(blocks):
-            if place == SPAN - 1:
-                biases.append(diagonal)
-            else:
-                mine = SPAN - 1 + z
-                same = flags_ref[at : at + 1, :] == flags_ref[mine : mine + 1, :]
-                biases.append(jnp.where(same, 0.0, MASKED))
-        for j in range(GROUP):
-            lanes = slice(j * HEAD_DIM, (j + 1) * HEAD_DIM)
-            spans = [slice(place * BLOCK, (place + 1) * BLOCK) for place in range(SPAN)]
-            tiles = [s_ref[z, span, lanes] * factor + bias for span, bias in zip(spans, biases)]
+
+    def attend(z, count):
+        rows = pl.ds(pl.multiple_of(z * BLOCK, BLOCK), BLOCK)
+        window = pl.ds(pl.multiple_of((z + SPAN - count) * BLOCK, BLOCK), count * BLOCK)
+        spans = [slice(place * BLOCK, (place + 1) * BLOCK) for place in range(count)]
+        used = slice(0, count * BLOCK)
+        heads = [slice(j * HEAD_DIM, (j + 1) * HEAD_DIM) for j in range(GROUP)]
+        queries = jnp.concatenate([qd_ref[rows, lanes] for lanes in heads], axis=0)
+        grads = jnp.concatenate(
+            [qd_ref[rows, Q_COLS + j * HEAD_DIM : Q_COLS + (j + 1) * HEAD_DIM] for j in range(GROUP)],
+            axis=0,
+        )
+        keys = kv_ref[window, :HEAD_DIM]
+        values = kv_ref[window, HEAD_DIM:]
+        s_ref[used] = contract(keys, queries, ((1,), (1,)))
+        g_ref[used] = contract(values, grads, ((1,), (1,)))
+        for lanes in heads:
+            tiles = [s_ref[span, lanes] * factor for span in spans]
+            tiles[-1] = tiles[-1] + diagonal
             highest = functools.reduce(
                 jnp.maximum, [jnp.max(t, axis=0, keepdims=True) for t in tiles]
             )
@@ -183,46 +174,42 @@
             for tile, span in zip(tiles, spans):
                 weights = tile * recip
                 probs = weights.astype(BF16)
-                p_ref[z, span, lanes] = probs
+                p_ref[span, lanes] = probs
                 kept.append(weights)
                 delta = delta + jnp.sum(
-                    probs.astype(F32) * g_ref[z, span, lanes], axis=0, keepdims=True
+                    probs.astype(F32) * g_ref[span, lanes], axis=0, keepdims=True
                 )
             for weights, span in zip(kept, spans):
-                ds_ref[z, span, lanes] = (weights * (g_ref[z, span, lanes] - delta)).astype(BF16)
-        score_grads = ds_ref[z]
-        d_key = contract(score_grads, queries, ((1,), (0,)))
-        d_value = contract(p_ref[z], grads, ((1,), (0,)))
-        for place, at in enumerate(blocks):
-            span = slice(place * BLOCK, (place + 1) * BLOCK)
-            first = d_keys[at] is None
-            d_keys[at] = d_key[span] if first else d_keys[at] + d_key[span]
-            d_values[at] = d_value[span] if first else d_values[at] + d_value[span]
+                ds_ref[span, lanes] = (weights * (g_ref[span, lanes] - delta)).astype(BF16)
+        score_grads = ds_ref[used]
+        d_kv_ref[window, :HEAD_DIM] += contract(score_grads, queries, ((1,), (0,)))
+        d_kv_ref[window, HEAD_DIM:] += contract(p_ref[used], grads, ((1,), (0,)))
         d_query = contract(jnp.transpose(keys), score_grads, ((1,), (0,)))
-        for j in range(GROUP):
-            lanes = slice(j * HEAD_DIM, (j + 1) * HEAD_DIM)
-            grad = jnp.transpose(d_query[:, lanes]) * SCALE
-            normed = qd_ref[rows, lanes].astype(F32)
-            q_part[j] = q_part[j] + jnp.sum(grad * normed, axis=0, keepdims=True)
-            grad = grad.astype(BF16)
+        d_query = (d_query * SCALE).astype(BF16)
+        for lanes in heads:
+            grad = jnp.transpose(d_query[:, lanes])
             dq_ref[2 * z, :, lanes] = grad[:half]
             dq_ref[2 * z + 1, :, lanes] = grad[half:]
-    for j in range(GROUP):
-        lanes = slice(j * HEAD_DIM, (j + 1) * HEAD_DIM)
-        part_ref[:, :, lanes] = jnp.broadcast_to(q_part[j][None], (copies, 1, HEAD_DIM))
+            normed = qd_ref[rows, lanes].astype(F32)
+            sums_ref[:1, lanes] += jnp.sum(grad.astype(F32) * normed, axis=0, keepdims=True)
+
+    @pl.loop(0, SPAN)
+    def _(z):
+        for count in range(1, SPAN + 1):
+            pl.when(counts_ref[z] == count)(functools.partial(attend, z, count))
+
+    part_ref[...] = jnp.broadcast_to(sums_ref[:1][None], part_ref.shape)
     for apart, out_ref in enumerate((dq_0_ref, dq_1_ref, dq_2_ref, dq_3_ref)):
         for core in range(2):
             out_ref[core] = dq_ref[2 * ((slot_ref[0] // 2) ^ apart) + core]
-    for at in range(WINDOW):
-        grad = d_keys[at] * SCALE
-        target, row = (d_near_ref, at) if at < SPAN - 1 else (d_own_ref, at - SPAN + 1)
-        span = slice(row * BLOCK, (row + 1) * BLOCK)
-        target[span, :HEAD_DIM] = grad.astype(target.dtype)
-        target[span, HEAD_DIM:] = d_values[at].astype(target.dtype)
+    d_near_ref[:, :HEAD_DIM] = (d_kv_ref[:border, :HEAD_DIM] * SCALE).astype(BF16)
+    d_near_ref[:, HEAD_DIM:] = d_kv_ref[:border, HEAD_DIM:].astype(BF16)
+    d_own_ref[:, :HEAD_DIM] = d_kv_ref[border:, :HEAD_DIM] * SCALE
+    d_own_ref[:, HEAD_DIM:] = d_kv_ref[border:, HEAD_DIM:]
 
 
 def gather_kernel(
-    slot_ref, own_ref, near_ref, sums_ref, dq_0_ref, dq_1_ref, dq_2_ref, dq_3_ref, out_ref, keep_ref, give_ref
+    slot_ref, own_ref, near_ref, sums_ref, dq_0_ref, dq_3_ref, dq_2_ref, dq_1_ref, out_ref, keep_ref, give_ref
 ):
     half = BLOCK // 2
     rest = jnp.sum(sums_ref[...], axis=0)
@@ -346,14 +333,15 @@
     )
     own = exchange(kv_send).reshape(TEAM * rows, KV_COLS)
     near = lax.ppermute(own[BLOCK:], axes, onward)
-    qd_send, flags = call(
+    qd_send, counts = call(
         query_norm_kernel,
         (
             jax.ShapeDtypeStruct((TEAM, rows, 2 * Q_COLS), BF16),
-            jax.ShapeDtypeStruct((8, 128), jnp.int32),
+            jax.ShapeDtypeStruct((SPAN,), jnp.int32),
         ),
         (mask_scalar, span_scalar, query_rows, grad_rows, query_gain_row, doc_blocks[None]),
         smem=2,
+        smem_out=1,
         far=True,
     )
     qd = exchange(qd_send).reshape(TEAM * rows, 2 * Q_COLS)
@@ -366,14 +354,17 @@
             jax.ShapeDtypeStruct((seq_count, 1, Q_COLS), F32),
         )
         + (jax.ShapeDtypeStruct((2, rows, Q_COLS), BF16),) * CHIPS,
-        (slot_scalar, qd, own, near, flags),
-        smem=1,
+        (slot_scalar, counts, qd, own, near),
+        smem=2,
         scratch=[
-            pltpu.VMEM((SPAN, window, Q_COLS), F32),
-            pltpu.VMEM((SPAN, window, Q_COLS), F32),
-            pltpu.VMEM((SPAN, window, Q_COLS), BF16),
-            pltpu.VMEM((SPAN, window, Q_COLS), BF16),
+            pltpu.VMEM((window, Q_COLS), F32),
+            pltpu.VMEM((window, Q_COLS), F32),
+            pltpu.VMEM((window, Q_COLS), BF16),
+            pltpu.VMEM((window, Q_COLS), BF16),
             pltpu.VMEM((TEAM, rows, Q_COLS), BF16),
+            pltpu.VMEM((WINDOW * BLOCK, KV_COLS), BF16),
+            pltpu.VMEM((WINDOW * BLOCK, KV_COLS), F32),
+            pltpu.VMEM((8, Q_COLS), F32),
         ],
     )
 
@@ -383,7 +374,8 @@
 
     back_near = lax.ppermute(d_near, axes, backward)
     sums = lax.all_to_all(part, axes, 0, 0, axis_index_groups=by_head, tiled=True)
-    dq = [dq[0]] + [within(dq[apart], 2 * apart) for apart in range(1, CHIPS)]
+    moved = {apart: within(dq[apart], 2 * apart) for apart in (3, 2, 1)}
+    dq = [dq[0]] + [moved[apart] for apart in range(1, CHIPS)]
     back_send, keep, give = call(
         gather_kernel,
         (
@@ -391,7 +383,7 @@
             jax.ShapeDtypeStruct((CHIPS, rows, Q_COLS), BF16),
             jax.ShapeDtypeStruct((CHIPS, rows, Q_COLS), BF16),
         ),
-        (slot_scalar, d_own, back_near, sums, *dq),
+        (slot_scalar, d_own, back_near, sums, dq[0], dq[3], dq[2], dq[1]),
         smem=1,
     )
     back = exchange(back_send)

time: 92.8 us -> 91.7 us (0.988)
  Pallas kernels: 14.4 us -> 13.3 us
    pallas_call x6, Pallas kernels: 14.4 us -> 13.3 us  [call(): pl.pallas_call(kernel, out_shape=out_shape, in_specs=[scalar] * smem + [g...]
  transfers between devices with their start and end apart: 10 -> 10, of which waited for: 6 -> 7; matrix products, arithmetic and copies ran while one was open for 0% -> 0% of each run, Pallas kernels for 5% -> 5%
where the time goes in v5:
time: 91.7 us; the launch traced here: 91.1 us
  starting transfers between devices  51.3 us (56%)
  waiting for transfers between devices  25.7 us (28%)
  Pallas kernels  13.3 us (15%)
    all_to_all x1, starting transfers between devices, body(): lax.all_to_all(part, axes, 0, 0, axis_index_groups=by_head, tiled=True)  17.3 us
    pallas_call x6, Pallas kernels, call(): pl.pallas_call(kernel, out_shape=out_shape, in_specs=[scalar] * smem + [g...  13.3 us
    all_to_all x3, waiting for transfers between devices, exchange(): lax.all_to_all(array, axes, 0, 0, axis_index_groups=teams, tiled=True)  13.1 us
    all_to_all x3, starting transfers between devices, exchange(): lax.all_to_all(array, axes, 0, 0, axis_index_groups=teams, tiled=True)  11.8 us
    ppermute x4, starting transfers between devices, within(): return lax.ppermute(array, axes, sorted(pairs))  11.5 us
    ppermute x4, waiting for transfers between devices, within(): return lax.ppermute(array, axes, sorted(pairs))  6.51 us
    ppermute x1, waiting for transfers between devices, body(): near = lax.ppermute(own[BLOCK:], axes, onward)  6.09 us
    ppermute x1, starting transfers between devices, body(): back_near = lax.ppermute(d_near, axes, backward)  5.48 us
  transfers between devices with their start and end apart: 10, of which 7 were waited for; matrix products, arithmetic and copies ran while one was open for 0% of the time, Pallas kernels for 5%

profile of v5, /device:TPU:40, one launch (start us, length us, event | category | flops | bytes accessed | tf_op | source)
XLA Modules:
  0.0 91.1 jit_solution(3054190140904680122)
XLA Ops:
  0.7 1.8 %shard_map.111 = bf16[8,64,256]{2,1,0:T(8,128)(2,1)} custom-call(s32[1]{0:T(128)} %bitcast.4.mask_ref, bf16[64,1024]{1,0:T(8,128)(2,1)} %bitcast.23, bf16[64,1024]{1,0:T(8,128)(2,1)} %bitcast.33, f32[1,1024]{1,0:T(1,128)} %bitcast.28), custom_call_target="tpu_custom_call" | custom-call | bytes 1024 | tf_op jit(solution)/shard_map/pallas_call | solution.py:41
  2.5 4.6 %all-to-all-start.1 = ((bf16[8,64,256]{2,1,0:T(8,128)(2,1)}), bf16[8,64,256]{2,1,0:T(8,128)(2,1)S(1)}, u32[]{:S(2)}, u32[]{:S(2)}) async-start(bf16[8,64,256]{2,1,0:T(8,128)(2,1)} %shard_map.111), calls=%async_computation.1 | async-start | bytes 524288 | tf_op jit(solution)/shard_map/all_to_all | solution.py:321
  7.1 2.9 %shard_map.110 = (bf16[8,64,1280]{2,1,0:T(8,128)(2,1)}, s32[4]{0:T(128)}) custom-call(s32[1]{0:T(128)} %bitcast.4.mask_ref, s32[1]{0:T(128)} %bitcast.5.span_ref, bf16[64,5120]{1,0:T(8,128)(2,1)} %bitcast.20, bf16[64,5120]{1,0:T(8,128)(2,1)} %bitcast.30, f32[1,5120]{1,0:T(1,128)} %bitcast.25, s32[1,96]{1,0:T(1,128)} %bitcast.34), custom_call_target="tpu_custom_call" | custom-call | bytes 1024 | tf_op jit(solution)/shard_map/pallas_call | solution.py:41
  10.1 4.0 %all-to-all-done.1 = bf16[8,64,256]{2,1,0:T(8,128)(2,1)S(1)} async-done(((bf16[8,64,256]{2,1,0:T(8,128)(2,1)}), bf16[8,64,256]{2,1,0:T(8,128)(2,1)S(1)}, u32[]{:S(2)}, u32[]{:S(2)}) %all-to-all-start.1) | async-done | bytes 262176 | tf_op jit(solution)/shard_map/all_to_all | solution.py:321
  14.1 3.7 %all-to-all-start = ((bf16[8,64,1280]{2,1,0:T(8,128)(2,1)}), bf16[8,64,1280]{2,1,0:T(8,128)(2,1)S(1)}, u32[]{:S(2)}, u32[]{:S(2)}) async-start(bf16[8,64,1280]{2,1,0:T(8,128)(2,1)} %get-tuple-element.22), calls=%async_computation | async-start | bytes 2621440 | tf_op jit(solution)/shard_map/all_to_all | solution.py:321
  17.8 5.1 %collective-permute-start = (bf16[384,256]{1,0:T(8,128)(2,1)S(1)}, bf16[384,256]{1,0:T(8,128)(2,1)S(1)}, u32[]{:S(2)}, u32[]{:S(2)}) collective-permute-start(bf16[384,256]{1,0:T(8,128)(2,1)S(1)} %bitcast.32), channel_id=1, source_target_pairs={{0,24},{1,25},{2,26},{3,27},{8,16},{9,17},{10,18},{11,19},{16,40},... | collective-permute-start | bytes 589832 | tf_op jit(solution)/shard_map/ppermute | solution.py:335
  22.9 6.1 %collective-permute-done.near_ref = bf16[384,256]{1,0:T(8,128)(2,1)S(1)} collective-permute-done((bf16[384,256]{1,0:T(8,128)(2,1)S(1)}, bf16[384,256]{1,0:T(8,128)(2,1)S(1)}, u32[]{:S(2)}, u32[]{:S(2)}) %collective-permute-start) | collective-permute-done | bytes 196640 | tf_op jit(solution)/shard_map/ppermute | solution.py:335
  29.0 6.9 %all-to-all-done = bf16[8,64,1280]{2,1,0:T(8,128)(2,1)S(1)} async-done(((bf16[8,64,1280]{2,1,0:T(8,128)(2,1)}), bf16[8,64,1280]{2,1,0:T(8,128)(2,1)S(1)}, u32[]{:S(2)}, u32[]{:S(2)}) %all-to-all-start) | async-done | bytes 1310752 | tf_op jit(solution)/shard_map/all_to_all | solution.py:321
  35.9 5.2 %shard_map.112 = (f32[512,256]{1,0:T(8,128)S(1)}, bf16[384,256]{1,0:T(8,128)(2,1)S(1)}, f32[64,1,640]{2,1,0:T(1,128)}, bf16[2,64,640]{2,1,0:T(8,128)(2,1)S(1)}, ...) custom-call(s32[1]{0:T(128)} %bitcast.3.slot_ref, ...), custom_call_target="tpu_custom_call" | custom-call | bytes 1024 | tf_op jit(solution)/shard_map/pallas_call | solution.py:41
  41.1 17.3 %all-to-all-start.2 = ((f32[64,1,640]{2,1,0:T(1,128)}), f32[64,1,640]{2,1,0:T(1,128)S(1)}, u32[]{:S(2)}, u32[]{:S(2)}) async-start(f32[64,1,640]{2,1,0:T(1,128)} %get-tuple-element.25), calls=%async_computation.2 | async-start | bytes 327680 | tf_op jit(solution)/shard_map/all_to_all | solution.py:376
  58.5 5.5 %collective-permute-start.1 = (bf16[384,256]{1,0:T(8,128)(2,1)S(1)}, bf16[384,256]{1,0:T(8,128)(2,1)S(1)}, u32[]{:S(2)}, u32[]{:S(2)}) collective-permute-start(bf16[384,256]{1,0:T(8,128)(2,1)S(1)} %get-tuple-element.24), channel_id=1, source_target_pairs={{4,28},{5,29},{6,30},{7,31},{12,20},{13,21},{14,22},{15,23},{16,8}... | collective-permute-start | bytes 589832 | tf_op jit(solution)/shard_map/ppermute | solution.py:375
  64.0 2.0 %collective-permute-start.2 = (bf16[2,64,640]{2,1,0:T(8,128)(2,1)S(1)}, bf16[2,64,640]{2,1,0:T(8,128)(2,1)S(1)}, u32[]{:S(2)}, u32[]{:S(2)}) collective-permute-start(bf16[2,64,640]{2,1,0:T(8,128)(2,1)S(1)} %get-tuple-element.27), channel_id=1, source_target_pairs={{0,10},{1,11},{2,8},{3,9},{4,14},{5,15},{6,12},{7,13},{8,2},{9,3},... | collective-permute-start | bytes 491528 | tf_op jit(solution)/shard_map/ppermute | solution.py:373
  66.0 5.3 %collective-permute-start.3 = (bf16[2,64,640]{2,1,0:T(8,128)(2,1)S(1)}, bf16[2,64,640]{2,1,0:T(8,128)(2,1)S(1)}, u32[]{:S(2)}, u32[]{:S(2)}) collective-permute-start(bf16[2,64,640]{2,1,0:T(8,128)(2,1)S(1)} %get-tuple-element.28), channel_id=1, source_target_pairs={{0,8},{1,9},{2,10},{3,11},{4,12},{5,13},{6,14},{7,15},{8,0},{9,1},... | collective-permute-start | bytes 491528 | tf_op jit(solution)/shard_map/ppermute | solution.py:373
  71.3 1.9 %collective-permute-start.4 = (bf16[2,64,640]{2,1,0:T(8,128)(2,1)S(1)}, bf16[2,64,640]{2,1,0:T(8,128)(2,1)S(1)}, u32[]{:S(2)}, u32[]{:S(2)}) collective-permute-start(bf16[2,64,640]{2,1,0:T(8,128)(2,1)S(1)} %get-tuple-element.29), channel_id=1, source_target_pairs={{0,2},{1,3},{2,0},{3,1},{4,6},{5,7},{6,4},{7,5},{8,10},{9,11},{10,... | collective-permute-start | bytes 491528 | tf_op jit(solution)/shard_map/ppermute | solution.py:373
  73.2 2.4 %collective-permute-done.3.dq_2_ref = bf16[2,64,640]{2,1,0:T(8,128)(2,1)S(1)} collective-permute-done((bf16[2,64,640]{2,1,0:T(8,128)(2,1)S(1)}, bf16[2,64,640]{2,1,0:T(8,128)(2,1)S(1)}, u32[]{:S(2)}, u32[]{:S(2)}) %collective-permute-start.3) | collective-permute-done | bytes 163872 | tf_op jit(solution)/shard_map/ppermute | solution.py:373
  75.6 2.9 %collective-permute-done.4.dq_1_ref = bf16[2,64,640]{2,1,0:T(8,128)(2,1)S(1)} collective-permute-done((bf16[2,64,640]{2,1,0:T(8,128)(2,1)S(1)}, bf16[2,64,640]{2,1,0:T(8,128)(2,1)S(1)}, u32[]{:S(2)}, u32[]{:S(2)}) %collective-permute-start.4) | collective-permute-done | bytes 163872 | tf_op jit(solution)/shard_map/ppermute | solution.py:373
  78.5 0.0 collective-permute-done.1.near_ref
  78.5 0.9 %shard_map.113 = (bf16[8,144,128]{2,1,0:T(8,128)(2,1)}, bf16[4,64,640]{2,1,0:T(8,128)(2,1)S(1)}, bf16[4,64,640]{2,1,0:T(8,128)(2,1)S(1)}) custom-call(s32[1]{0:T(128)} %bitcast.3.slot_ref, f32[512,256]{1,0:T(8,128)S(1)} %get-tuple-element.23.own_ref, bf16[384,256]{1,0:T(8,128)(2,1)S(1)} %collective-permute-done.1.near_ref, ...), custom_call_target="tpu_custom_call" | custom-call | bytes 1024 | tf_op jit(solution)/shard_map/pallas_call | solution.py:41
  79.4 3.6 %all-to-all-start.3 = ((bf16[8,144,128]{2,1,0:T(8,128)(2,1)}), bf16[8,144,128]{2,1,0:T(8,128)(2,1)S(1)}, u32[]{:S(2)}, u32[]{:S(2)}) async-start(bf16[8,144,128]{2,1,0:T(8,128)(2,1)} %get-tuple-element.32), calls=%async_computation.3 | async-start | bytes 589824 | tf_op jit(solution)/shard_map/all_to_all | solution.py:321
  83.0 2.3 %collective-permute-start.5 = (bf16[4,64,640]{2,1,0:T(8,128)(2,1)S(1)}, bf16[4,64,640]{2,1,0:T(8,128)(2,1)S(1)}, u32[]{:S(2)}, u32[]{:S(2)}) collective-permute-start(bf16[4,64,640]{2,1,0:T(8,128)(2,1)S(1)} %get-tuple-element.31), channel_id=1, source_target_pairs={{0,1},{1,0},{2,3},{3,2},{4,5},{5,4},{6,7},{7,6},{8,9},{9,8},{10,11... | collective-permute-start | bytes 983048 | tf_op jit(solution)/shard_map/ppermute | solution.py:373
  85.3 1.2 %collective-permute-done.5.given_ref = bf16[4,64,640]{2,1,0:T(8,128)(2,1)S(1)} collective-permute-done((bf16[4,64,640]{2,1,0:T(8,128)(2,1)S(1)}, bf16[4,64,640]{2,1,0:T(8,128)(2,1)S(1)}, u32[]{:S(2)}, u32[]{:S(2)}) %collective-permute-start.5) | collective-permute-done | bytes 327712 | tf_op jit(solution)/shard_map/ppermute | solution.py:373
  86.5 1.5 %shard_map.114 = bf16[64,5120]{1,0:T(8,128)(2,1)} custom-call(s32[1]{0:T(128)} %bitcast.head_ref, bf16[64,5120]{1,0:T(8,128)(2,1)S(1)} %bitcast.21, f32[1,5120]{1,0:T(1,128)S(1)} %bitcast.26, bf16[4,64,640]{2,1,0:T(8,128)(2,1)S(1)} %get-tuple-element.30.kept_ref, bf16[4,64,640]{2,1,0:T(8,128)(2,1)S(1)} %collective-permute-done.5.given_ref), custom_call_target="tpu_custom_call" | custom-call | bytes 1024 | tf_op jit(solution)/shard_map/pallas_call | solution.py:41
  88.0 2.2 %all-to-all-done.3.back_ref = bf16[8,144,128]{2,1,0:T(8,128)(2,1)S(1)} async-done(((bf16[8,144,128]{2,1,0:T(8,128)(2,1)}), bf16[8,144,128]{2,1,0:T(8,128)(2,1)S(1)}, u32[]{:S(2)}, u32[]{:S(2)}) %all-to-all-start.3) | async-done | bytes 294944 | tf_op jit(solution)/shard_map/all_to_all | solution.py:321
  90.2 0.9 shard_map.115
  (13 shorter events, 0.0 us)
Async XLA Ops:
  2.5 11.5 %all-to-all-start.1 = ((bf16[8,64,256]{2,1,0:T(8,128)(2,1)}), bf16[8,64,256]{2,1,0:T(8,128)(2,1)S(1)}, u32[]{:S(2)}, u32[]{:S(2)}) async-start(bf16[8,64,256]{2,1,0:T(8,128)(2,1)} %shard_map.111), calls=%async_computation.1 | async-start | bytes 524288 | tf_op jit(solution)/shard_map/all_to_all | solution.py:321
  14.1 21.9 %copy-start.4 = (s32[4]{0:T(128)S(1)}, s32[4]{0:T(128)}, u32[]{:S(2)}) copy-start(s32[4]{0:T(128)} %get-tuple-element.21.counts_ref) | copy-start | bytes 52
  14.1 21.9 %all-to-all-start = ((bf16[8,64,1280]{2,1,0:T(8,128)(2,1)}), bf16[8,64,1280]{2,1,0:T(8,128)(2,1)S(1)}, u32[]{:S(2)}, u32[]{:S(2)}) async-start(bf16[8,64,1280]{2,1,0:T(8,128)(2,1)} %get-tuple-element.22), calls=%async_computation | async-start | bytes 2621440 | tf_op jit(solution)/shard_map/all_to_all | solution.py:321
  17.8 11.2 %collective-permute-start = (bf16[384,256]{1,0:T(8,128)(2,1)S(1)}, bf16[384,256]{1,0:T(8,128)(2,1)S(1)}, u32[]{:S(2)}, u32[]{:S(2)}) collective-permute-start(bf16[384,256]{1,0:T(8,128)(2,1)S(1)} %bitcast.32), channel_id=1, source_target_pairs={{0,24},{1,25},{2,26},{3,27},{8,16},{9,17},{10,18},{11,19},{16,40},... | collective-permute-start | bytes 589832 | tf_op jit(solution)/shard_map/ppermute | solution.py:335
  41.1 45.4 %copy-start = (bf16[1,64,5120]{2,1,0:T(8,128)(2,1)S(1)}, bf16[1,64,5120]{2,1,0:T(8,128)(2,1)}, u32[]{:S(2)}) copy-start(bf16[1,64,5120]{2,1,0:T(8,128)(2,1)} %param.7) | copy-start | bytes 1966084
  41.1 45.4 %copy-start.2 = (f32[5120]{0:T(1024)S(1)}, f32[5120]{0:T(1024)}, u32[]{:S(2)}) copy-start(f32[5120]{0:T(1024)} %param.11) | copy-start | bytes 61444
  41.1 37.4 %all-to-all-start.2 = ((f32[64,1,640]{2,1,0:T(1,128)}), f32[64,1,640]{2,1,0:T(1,128)S(1)}, u32[]{:S(2)}, u32[]{:S(2)}) async-start(f32[64,1,640]{2,1,0:T(1,128)} %get-tuple-element.25), calls=%async_computation.2 | async-start | bytes 327680 | tf_op jit(solution)/shard_map/all_to_all | solution.py:376
  58.5 20.0 %collective-permute-start.1 = (bf16[384,256]{1,0:T(8,128)(2,1)S(1)}, bf16[384,256]{1,0:T(8,128)(2,1)S(1)}, u32[]{:S(2)}, u32[]{:S(2)}) collective-permute-start(bf16[384,256]{1,0:T(8,128)(2,1)S(1)} %get-tuple-element.24), channel_id=1, source_target_pairs={{4,28},{5,29},{6,30},{7,31},{12,20},{13,21},{14,22},{15,23},{16,8}... | collective-permute-start | bytes 589832 | tf_op jit(solution)/shard_map/ppermute | solution.py:375
  64.0 9.2 %collective-permute-start.2 = (bf16[2,64,640]{2,1,0:T(8,128)(2,1)S(1)}, bf16[2,64,640]{2,1,0:T(8,128)(2,1)S(1)}, u32[]{:S(2)}, u32[]{:S(2)}) collective-permute-start(bf16[2,64,640]{2,1,0:T(8,128)(2,1)S(1)} %get-tuple-element.27), channel_id=1, source_target_pairs={{0,10},{1,11},{2,8},{3,9},{4,14},{5,15},{6,12},{7,13},{8,2},{9,3},... | collective-permute-start | bytes 491528 | tf_op jit(solution)/shard_map/ppermute | solution.py:373
  66.0 9.6 %collective-permute-start.3 = (bf16[2,64,640]{2,1,0:T(8,128)(2,1)S(1)}, bf16[2,64,640]{2,1,0:T(8,128)(2,1)S(1)}, u32[]{:S(2)}, u32[]{:S(2)}) collective-permute-start(bf16[2,64,640]{2,1,0:T(8,128)(2,1)S(1)} %get-tuple-element.28), channel_id=1, source_target_pairs={{0,8},{1,9},{2,10},{3,11},{4,12},{5,13},{6,14},{7,15},{8,0},{9,1},... | collective-permute-start | bytes 491528 | tf_op jit(solution)/shard_map/ppermute | solution.py:373
  71.3 7.2 %collective-permute-start.4 = (bf16[2,64,640]{2,1,0:T(8,128)(2,1)S(1)}, bf16[2,64,640]{2,1,0:T(8,128)(2,1)S(1)}, u32[]{:S(2)}, u32[]{:S(2)}) collective-permute-start(bf16[2,64,640]{2,1,0:T(8,128)(2,1)S(1)} %get-tuple-element.29), channel_id=1, source_target_pairs={{0,2},{1,3},{2,0},{3,1},{4,6},{5,7},{6,4},{7,5},{8,10},{9,11},{10,... | collective-permute-start | bytes 491528 | tf_op jit(solution)/shard_map/ppermute | solution.py:373
  79.4 10.8 %copy-start.1 = (bf16[1,64,1024]{2,1,0:T(8,128)(2,1)S(1)}, bf16[1,64,1024]{2,1,0:T(8,128)(2,1)}, u32[]{:S(2)}) copy-start(bf16[1,64,1024]{2,1,0:T(8,128)(2,1)} %param.8) | copy-start | bytes 393220
  79.4 10.8 %copy-start.3 = (f32[1024]{0:T(1024)S(1)}, f32[1024]{0:T(1024)}, u32[]{:S(2)}) copy-start(f32[1024]{0:T(1024)} %param.12) | copy-start | bytes 12292
  79.4 10.8 %all-to-all-start.3 = ((bf16[8,144,128]{2,1,0:T(8,128)(2,1)}), bf16[8,144,128]{2,1,0:T(8,128)(2,1)S(1)}, u32[]{:S(2)}, u32[]{:S(2)}) async-start(bf16[8,144,128]{2,1,0:T(8,128)(2,1)} %get-tuple-element.32), calls=%async_computation.3 | async-start | bytes 589824 | tf_op jit(solution)/shard_map/all_to_all | solution.py:321
  83.0 3.5 %collective-permute-start.5 = (bf16[4,64,640]{2,1,0:T(8,128)(2,1)S(1)}, bf16[4,64,640]{2,1,0:T(8,128)(2,1)S(1)}, u32[]{:S(2)}, u32[]{:S(2)}) collective-permute-start(bf16[4,64,640]{2,1,0:T(8,128)(2,1)S(1)} %get-tuple-element.31), channel_id=1, source_target_pairs={{0,1},{1,0},{2,3},{3,2},{4,5},{5,4},{6,7},{7,6},{8,9},{9,8},{10,11... | collective-permute-start | bytes 983048 | tf_op jit(solution)/shard_map/ppermute | solution.py:373

commit v6 on v5

--- a/solution.py
+++ b/solution.py
@@ -81,10 +81,13 @@
 
 
 def query_norm_kernel(mask_ref, span_ref, *refs):
-    sources, (out_ref, counts_ref), targets, semaphores = refs[:4], refs[4:6], refs[6:10], refs[10]
+    sources, (out_ref, inverse_ref, counts_ref) = refs[:4], refs[4:7]
+    targets, semaphores = refs[7:11], refs[11]
     query_ref, grad_ref, gain_ref, docs_ref = fetched(sources, targets, semaphores)
     values = query_ref[...].astype(F32)
-    normed = (values * inverse_rms(values) * gain_ref[...]).astype(BF16)
+    inverse = inverse_rms(values)
+    inverse_ref[...] = jnp.broadcast_to(inverse, inverse_ref.shape)
+    normed = (values * inverse * gain_ref[...]).astype(BF16)
     for head in range(TEAM):
         columns = slice(head * Q_COLS, (head + 1) * Q_COLS)
         slot = head ^ mask_ref[0]
@@ -235,20 +238,24 @@
         give_ref[apart] = dq_ref[1 - core]
 
 
-def norm_backward(rows, gain, grad):
+def norm_backward(rows, gain, grad, inverse=None):
     values = rows.astype(F32)
-    inverse = inverse_rms(values)
+    inverse = inverse_rms(values) if inverse is None else inverse
     scaled = grad.astype(F32) * gain
     inner = jnp.mean(scaled * values, axis=-1, keepdims=True)
     return (inverse * scaled - values * (inverse * inverse * inverse * inner)).astype(BF16)
 
 
-def query_back_kernel(head_ref, query_ref, gain_ref, kept_ref, given_ref, out_ref, grad_ref):
+def query_back_kernel(
+    head_ref, query_ref, gain_ref, inverse_ref, kept_ref, given_ref, out_ref, grad_ref
+):
     for apart in range(CHIPS):
         for other, source in enumerate((kept_ref, given_ref)):
             head = head_ref[0] ^ (2 * apart + other)
             grad_ref[:, pl.ds(pl.multiple_of(head * Q_COLS, Q_COLS), Q_COLS)] = source[apart]
-    out_ref[...] = norm_backward(query_ref[...], gain_ref[...], grad_ref[...])
+    out_ref[...] = norm_backward(
+        query_ref[...], gain_ref[...], grad_ref[...], inverse_ref[:, :1]
+    )
 
 
 def key_back_kernel(
@@ -333,10 +340,11 @@
     )
     own = exchange(kv_send).reshape(TEAM * rows, KV_COLS)
     near = lax.ppermute(own[BLOCK:], axes, onward)
-    qd_send, counts = call(
+    qd_send, inverse, counts = call(
         query_norm_kernel,
         (
             jax.ShapeDtypeStruct((TEAM, rows, 2 * Q_COLS), BF16),
+            jax.ShapeDtypeStruct((rows, 128), F32),
             jax.ShapeDtypeStruct((SPAN,), jnp.int32),
         ),
         (mask_scalar, span_scalar, query_rows, grad_rows, query_gain_row, doc_blocks[None]),
@@ -391,7 +399,7 @@
     d_query = call(
         query_back_kernel,
         jax.ShapeDtypeStruct(query_rows.shape, BF16),
-        (head_scalar, query_rows, query_gain_row, keep, given),
+        (head_scalar, query_rows, query_gain_row, inverse, keep, given),
         smem=1,
         scratch=[pltpu.VMEM(query_rows.shape, BF16)],
     )

time: 91.7 us -> 92 us (level)
  Pallas kernels: 13.3 us -> 14.3 us
  starting transfers between devices: 51.3 us -> 50.3 us
    all_to_all x1, starting transfers between devices: 17.3 us -> 16 us  [body(): lax.all_to_all(part, axes, 0, 0, axis_index_groups=by_head, tiled=True)]
    pallas_call x6, Pallas kernels: 13.3 us -> 14.3 us  [call(): pl.pallas_call(kernel, out_shape=out_shape, in_specs=[scalar] * smem + [g...]
where the time goes in v6:
time: 92 us; the launch traced here: 91.1 us
  starting transfers between devices  50.3 us (55%)
  waiting for transfers between devices  25.6 us (28%)
  Pallas kernels  14.3 us (16%)
    all_to_all x1, starting transfers between devices, body(): lax.all_to_all(part, axes, 0, 0, axis_index_groups=by_head, tiled=True)  16 us
    pallas_call x6, Pallas kernels, call(): pl.pallas_call(kernel, out_shape=out_shape, in_specs=[scalar] * smem + [g...  14.3 us
    all_to_all x3, waiting for transfers between devices, exchange(): lax.all_to_all(array, axes, 0, 0, axis_index_groups=teams, tiled=True)  13 us
    ppermute x4, starting transfers between devices, within(): return lax.ppermute(array, axes, sorted(pairs))  11.9 us
    all_to_all x3, starting transfers between devices, exchange(): lax.all_to_all(array, axes, 0, 0, axis_index_groups=teams, tiled=True)  11.8 us
    ppermute x4, waiting for transfers between devices, within(): return lax.ppermute(array, axes, sorted(pairs))  6.51 us
    ppermute x1, waiting for transfers between devices, body(): near = lax.ppermute(own[BLOCK:], axes, onward)  6.09 us
    ppermute x1, starting transfers between devices, body(): back_near = lax.ppermute(d_near, axes, backward)  5.48 us
  transfers between devices with their start and end apart: 10, of which 7 were waited for; matrix products, arithmetic and copies ran while one was open for 0% of the time, Pallas kernels for 5%

profile of v6, /device:TPU:40, one launch (start us, length us, event | category | flops | bytes accessed | tf_op | source)
XLA Modules:
  0.0 91.1 jit_solution(9632937704113579802)
XLA Ops:
  0.7 1.8 %shard_map.111 = bf16[8,64,256]{2,1,0:T(8,128)(2,1)} custom-call(s32[1]{0:T(128)} %bitcast.3.mask_ref, bf16[64,1024]{1,0:T(8,128)(2,1)} %bitcast.23, bf16[64,1024]{1,0:T(8,128)(2,1)} %bitcast.33, f32[1,1024]{1,0:T(1,128)} %bitcast.28), custom_call_target="tpu_custom_call" | custom-call | bytes 1024 | tf_op jit(solution)/shard_map/pallas_call | solution.py:41
  2.5 4.6 %all-to-all-start.1 = ((bf16[8,64,256]{2,1,0:T(8,128)(2,1)}), bf16[8,64,256]{2,1,0:T(8,128)(2,1)S(1)}, u32[]{:S(2)}, u32[]{:S(2)}) async-start(bf16[8,64,256]{2,1,0:T(8,128)(2,1)} %shard_map.111), calls=%async_computation.1 | async-start | bytes 524288 | tf_op jit(solution)/shard_map/all_to_all | solution.py:328
  7.1 3.0 %shard_map.110 = (bf16[8,64,1280]{2,1,0:T(8,128)(2,1)}, f32[64,128]{1,0:T(8,128)}, s32[4]{0:T(128)}) custom-call(s32[1]{0:T(128)} %bitcast.3.mask_ref, s32[1]{0:T(128)} %bitcast.4.span_ref, bf16[64,5120]{1,0:T(8,128)(2,1)} %bitcast.20, bf16[64,5120]{1,0:T(8,128)(2,1)} %bitcast.30, f32[1,5120]{1,0:T(1,128)} %bitcast.25, s32[1,96]{1,0:T(1,128)} %bitcast.34), custom_call_target="tpu_custom_call" | custom-call | bytes 1024 | tf_op jit(solution)/shard_map/pallas_call | solution.py:41
  10.1 4.0 %all-to-all-done.1 = bf16[8,64,256]{2,1,0:T(8,128)(2,1)S(1)} async-done(((bf16[8,64,256]{2,1,0:T(8,128)(2,1)}), bf16[8,64,256]{2,1,0:T(8,128)(2,1)S(1)}, u32[]{:S(2)}, u32[]{:S(2)}) %all-to-all-start.1) | async-done | bytes 262176 | tf_op jit(solution)/shard_map/all_to_all | solution.py:328
  14.1 3.7 %all-to-all-start = ((bf16[8,64,1280]{2,1,0:T(8,128)(2,1)}), bf16[8,64,1280]{2,1,0:T(8,128)(2,1)S(1)}, u32[]{:S(2)}, u32[]{:S(2)}) async-start(bf16[8,64,1280]{2,1,0:T(8,128)(2,1)} %get-tuple-element.24), calls=%async_computation | async-start | bytes 2621440 | tf_op jit(solution)/shard_map/all_to_all | solution.py:328
  17.8 5.1 %collective-permute-start = (bf16[384,256]{1,0:T(8,128)(2,1)S(1)}, bf16[384,256]{1,0:T(8,128)(2,1)S(1)}, u32[]{:S(2)}, u32[]{:S(2)}) collective-permute-start(bf16[384,256]{1,0:T(8,128)(2,1)S(1)} %bitcast.32), channel_id=1, source_target_pairs={{0,24},{1,25},{2,26},{3,27},{8,16},{9,17},{10,18},{11,19},{16,40},... | collective-permute-start | bytes 589832 | tf_op jit(solution)/shard_map/ppermute | solution.py:342
  22.9 6.1 %collective-permute-done.near_ref = bf16[384,256]{1,0:T(8,128)(2,1)S(1)} collective-permute-done((bf16[384,256]{1,0:T(8,128)(2,1)S(1)}, bf16[384,256]{1,0:T(8,128)(2,1)S(1)}, u32[]{:S(2)}, u32[]{:S(2)}) %collective-permute-start) | collective-permute-done | bytes 196640 | tf_op jit(solution)/shard_map/ppermute | solution.py:342
  29.0 6.9 %all-to-all-done = bf16[8,64,1280]{2,1,0:T(8,128)(2,1)S(1)} async-done(((bf16[8,64,1280]{2,1,0:T(8,128)(2,1)}), bf16[8,64,1280]{2,1,0:T(8,128)(2,1)S(1)}, u32[]{:S(2)}, u32[]{:S(2)}) %all-to-all-start) | async-done | bytes 1310752 | tf_op jit(solution)/shard_map/all_to_all | solution.py:328
  35.9 6.1 %shard_map.112 = (f32[512,256]{1,0:T(8,128)S(1)}, bf16[384,256]{1,0:T(8,128)(2,1)S(1)}, f32[64,1,640]{2,1,0:T(1,128)}, bf16[2,64,640]{2,1,0:T(8,128)(2,1)S(1)}, ...) custom-call(s32[1]{0:T(128)} %bitcast.7.slot_ref, ...), custom_call_target="tpu_custom_call" | custom-call | bytes 1024 | tf_op jit(solution)/shard_map/pallas_call | solution.py:41
  42.1 16.0 %all-to-all-start.2 = ((f32[64,1,640]{2,1,0:T(1,128)}), f32[64,1,640]{2,1,0:T(1,128)S(1)}, u32[]{:S(2)}, u32[]{:S(2)}) async-start(f32[64,1,640]{2,1,0:T(1,128)} %get-tuple-element.27), calls=%async_computation.2 | async-start | bytes 327680 | tf_op jit(solution)/shard_map/all_to_all | solution.py:384
  58.0 5.5 %collective-permute-start.1 = (bf16[384,256]{1,0:T(8,128)(2,1)S(1)}, bf16[384,256]{1,0:T(8,128)(2,1)S(1)}, u32[]{:S(2)}, u32[]{:S(2)}) collective-permute-start(bf16[384,256]{1,0:T(8,128)(2,1)S(1)} %get-tuple-element.26), channel_id=1, source_target_pairs={{4,28},{5,29},{6,30},{7,31},{12,20},{13,21},{14,22},{15,23},{16,8}... | collective-permute-start | bytes 589832 | tf_op jit(solution)/shard_map/ppermute | solution.py:383
  63.5 2.5 %collective-permute-start.2 = (bf16[2,64,640]{2,1,0:T(8,128)(2,1)S(1)}, bf16[2,64,640]{2,1,0:T(8,128)(2,1)S(1)}, u32[]{:S(2)}, u32[]{:S(2)}) collective-permute-start(bf16[2,64,640]{2,1,0:T(8,128)(2,1)S(1)} %get-tuple-element.29), channel_id=1, source_target_pairs={{0,10},{1,11},{2,8},{3,9},{4,14},{5,15},{6,12},{7,13},{8,2},{9,3},... | collective-permute-start | bytes 491528 | tf_op jit(solution)/shard_map/ppermute | solution.py:381
  66.0 5.2 %collective-permute-start.3 = (bf16[2,64,640]{2,1,0:T(8,128)(2,1)S(1)}, bf16[2,64,640]{2,1,0:T(8,128)(2,1)S(1)}, u32[]{:S(2)}, u32[]{:S(2)}) collective-permute-start(bf16[2,64,640]{2,1,0:T(8,128)(2,1)S(1)} %get-tuple-element.30), channel_id=1, source_target_pairs={{0,8},{1,9},{2,10},{3,11},{4,12},{5,13},{6,14},{7,15},{8,0},{9,1},... | collective-permute-start | bytes 491528 | tf_op jit(solution)/shard_map/ppermute | solution.py:381
  71.3 1.9 %collective-permute-start.4 = (bf16[2,64,640]{2,1,0:T(8,128)(2,1)S(1)}, bf16[2,64,640]{2,1,0:T(8,128)(2,1)S(1)}, u32[]{:S(2)}, u32[]{:S(2)}) collective-permute-start(bf16[2,64,640]{2,1,0:T(8,128)(2,1)S(1)} %get-tuple-element.31), channel_id=1, source_target_pairs={{0,2},{1,3},{2,0},{3,1},{4,6},{5,7},{6,4},{7,5},{8,10},{9,11},{10,... | collective-permute-start | bytes 491528 | tf_op jit(solution)/shard_map/ppermute | solution.py:381
  73.2 2.0 %collective-permute-done.3.dq_2_ref = bf16[2,64,640]{2,1,0:T(8,128)(2,1)S(1)} collective-permute-done((bf16[2,64,640]{2,1,0:T(8,128)(2,1)S(1)}, bf16[2,64,640]{2,1,0:T(8,128)(2,1)S(1)}, u32[]{:S(2)}, u32[]{:S(2)}) %collective-permute-start.3) | collective-permute-done | bytes 163872 | tf_op jit(solution)/shard_map/ppermute | solution.py:381
  75.2 3.3 %collective-permute-done.4.dq_1_ref = bf16[2,64,640]{2,1,0:T(8,128)(2,1)S(1)} collective-permute-done((bf16[2,64,640]{2,1,0:T(8,128)(2,1)S(1)}, bf16[2,64,640]{2,1,0:T(8,128)(2,1)S(1)}, u32[]{:S(2)}, u32[]{:S(2)}) %collective-permute-start.4) | collective-permute-done | bytes 163872 | tf_op jit(solution)/shard_map/ppermute | solution.py:381
  78.5 0.0 all-to-all-done.2.sums_ref
  78.5 0.9 %shard_map.113 = (bf16[8,144,128]{2,1,0:T(8,128)(2,1)}, bf16[4,64,640]{2,1,0:T(8,128)(2,1)S(1)}, bf16[4,64,640]{2,1,0:T(8,128)(2,1)S(1)}) custom-call(s32[1]{0:T(128)} %bitcast.7.slot_ref, f32[512,256]{1,0:T(8,128)S(1)} %get-tuple-element.25.own_ref, bf16[384,256]{1,0:T(8,128)(2,1)S(1)} %collective-permute-done.1.near_ref, ...), custom_call_target="tpu_custom_call" | custom-call | bytes 1024 | tf_op jit(solution)/shard_map/pallas_call | solution.py:41
  79.4 3.6 %all-to-all-start.3 = ((bf16[8,144,128]{2,1,0:T(8,128)(2,1)}), bf16[8,144,128]{2,1,0:T(8,128)(2,1)S(1)}, u32[]{:S(2)}, u32[]{:S(2)}) async-start(bf16[8,144,128]{2,1,0:T(8,128)(2,1)} %get-tuple-element.34), calls=%async_computation.3 | async-start | bytes 589824 | tf_op jit(solution)/shard_map/all_to_all | solution.py:328
  83.0 2.3 %collective-permute-start.5 = (bf16[4,64,640]{2,1,0:T(8,128)(2,1)S(1)}, bf16[4,64,640]{2,1,0:T(8,128)(2,1)S(1)}, u32[]{:S(2)}, u32[]{:S(2)}) collective-permute-start(bf16[4,64,640]{2,1,0:T(8,128)(2,1)S(1)} %get-tuple-element.33), channel_id=1, source_target_pairs={{0,1},{1,0},{2,3},{3,2},{4,5},{5,4},{6,7},{7,6},{8,9},{9,8},{10,11... | collective-permute-start | bytes 983048 | tf_op jit(solution)/shard_map/ppermute | solution.py:381
  85.3 1.2 %collective-permute-done.5.given_ref = bf16[4,64,640]{2,1,0:T(8,128)(2,1)S(1)} collective-permute-done((bf16[4,64,640]{2,1,0:T(8,128)(2,1)S(1)}, bf16[4,64,640]{2,1,0:T(8,128)(2,1)S(1)}, u32[]{:S(2)}, u32[]{:S(2)}) %collective-permute-start.5) | collective-permute-done | bytes 327712 | tf_op jit(solution)/shard_map/ppermute | solution.py:381
  86.5 1.5 %shard_map.114 = bf16[64,5120]{1,0:T(8,128)(2,1)} custom-call(s32[1]{0:T(128)} %bitcast.head_ref, bf16[64,5120]{1,0:T(8,128)(2,1)S(1)} %bitcast.21, f32[1,5120]{1,0:T(1,128)S(1)} %bitcast.26, f32[64,128]{1,0:T(8,128)S(1)} %copy-done.3, bf16[4,64,640]{2,1,0:T(8,128)(2,1)S(1)} %get-tuple-element.32.kept_ref, ...), custom_call_target="tpu_custom_call" | custom-call | bytes 1024 | tf_op jit(solution)/shard_map/pallas_call | solution.py:41
  88.1 2.1 %all-to-all-done.3.back_ref = bf16[8,144,128]{2,1,0:T(8,128)(2,1)S(1)} async-done(((bf16[8,144,128]{2,1,0:T(8,128)(2,1)}), bf16[8,144,128]{2,1,0:T(8,128)(2,1)S(1)}, u32[]{:S(2)}, u32[]{:S(2)}) %all-to-all-start.3) | async-done | bytes 294944 | tf_op jit(solution)/shard_map/all_to_all | solution.py:328
  90.2 0.9 shard_map.115
  (15 shorter events, 0.0 us)
Async XLA Ops:
  2.5 11.5 %all-to-all-start.1 = ((bf16[8,64,256]{2,1,0:T(8,128)(2,1)}), bf16[8,64,256]{2,1,0:T(8,128)(2,1)S(1)}, u32[]{:S(2)}, u32[]{:S(2)}) async-start(bf16[8,64,256]{2,1,0:T(8,128)(2,1)} %shard_map.111), calls=%async_computation.1 | async-start | bytes 524288 | tf_op jit(solution)/shard_map/all_to_all | solution.py:328
  14.1 21.9 %copy-start.5 = (s32[4]{0:T(128)S(1)}, s32[4]{0:T(128)}, u32[]{:S(2)}) copy-start(s32[4]{0:T(128)} %get-tuple-element.23.counts_ref) | copy-start | bytes 52
  14.1 21.9 %all-to-all-start = ((bf16[8,64,1280]{2,1,0:T(8,128)(2,1)}), bf16[8,64,1280]{2,1,0:T(8,128)(2,1)S(1)}, u32[]{:S(2)}, u32[]{:S(2)}) async-start(bf16[8,64,1280]{2,1,0:T(8,128)(2,1)} %get-tuple-element.24), calls=%async_computation | async-start | bytes 2621440 | tf_op jit(solution)/shard_map/all_to_all | solution.py:328
  17.8 11.2 %collective-permute-start = (bf16[384,256]{1,0:T(8,128)(2,1)S(1)}, bf16[384,256]{1,0:T(8,128)(2,1)S(1)}, u32[]{:S(2)}, u32[]{:S(2)}) collective-permute-start(bf16[384,256]{1,0:T(8,128)(2,1)S(1)} %bitcast.32), channel_id=1, source_target_pairs={{0,24},{1,25},{2,26},{3,27},{8,16},{9,17},{10,18},{11,19},{16,40},... | collective-permute-start | bytes 589832 | tf_op jit(solution)/shard_map/ppermute | solution.py:342
  42.1 44.5 %copy-start = (bf16[1,64,5120]{2,1,0:T(8,128)(2,1)S(1)}, bf16[1,64,5120]{2,1,0:T(8,128)(2,1)}, u32[]{:S(2)}) copy-start(bf16[1,64,5120]{2,1,0:T(8,128)(2,1)} %param.7) | copy-start | bytes 1966084
  42.1 44.5 %copy-start.2 = (f32[5120]{0:T(1024)S(1)}, f32[5120]{0:T(1024)}, u32[]{:S(2)}) copy-start(f32[5120]{0:T(1024)} %param.11) | copy-start | bytes 61444
  42.1 44.5 %copy-start.3 = (f32[64,128]{1,0:T(8,128)S(1)}, f32[64,128]{1,0:T(8,128)}, u32[]{:S(2)}) copy-start(f32[64,128]{1,0:T(8,128)} %get-tuple-element.22.inverse_ref) | copy-start | bytes 98308
  42.1 36.4 %all-to-all-start.2 = ((f32[64,1,640]{2,1,0:T(1,128)}), f32[64,1,640]{2,1,0:T(1,128)S(1)}, u32[]{:S(2)}, u32[]{:S(2)}) async-start(f32[64,1,640]{2,1,0:T(1,128)} %get-tuple-element.27), calls=%async_computation.2 | async-start | bytes 327680 | tf_op jit(solution)/shard_map/all_to_all | solution.py:384
  58.0 20.4 %collective-permute-start.1 = (bf16[384,256]{1,0:T(8,128)(2,1)S(1)}, bf16[384,256]{1,0:T(8,128)(2,1)S(1)}, u32[]{:S(2)}, u32[]{:S(2)}) collective-permute-start(bf16[384,256]{1,0:T(8,128)(2,1)S(1)} %get-tuple-element.26), channel_id=1, source_target_pairs={{4,28},{5,29},{6,30},{7,31},{12,20},{13,21},{14,22},{15,23},{16,8}... | collective-permute-start | bytes 589832 | tf_op jit(solution)/shard_map/ppermute | solution.py:383
  63.5 9.7 %collective-permute-start.2 = (bf16[2,64,640]{2,1,0:T(8,128)(2,1)S(1)}, bf16[2,64,640]{2,1,0:T(8,128)(2,1)S(1)}, u32[]{:S(2)}, u32[]{:S(2)}) collective-permute-start(bf16[2,64,640]{2,1,0:T(8,128)(2,1)S(1)} %get-tuple-element.29), channel_id=1, source_target_pairs={{0,10},{1,11},{2,8},{3,9},{4,14},{5,15},{6,12},{7,13},{8,2},{9,3},... | collective-permute-start | bytes 491528 | tf_op jit(solution)/shard_map/ppermute | solution.py:381
  66.0 9.1 %collective-permute-start.3 = (bf16[2,64,640]{2,1,0:T(8,128)(2,1)S(1)}, bf16[2,64,640]{2,1,0:T(8,128)(2,1)S(1)}, u32[]{:S(2)}, u32[]{:S(2)}) collective-permute-start(bf16[2,64,640]{2,1,0:T(8,128)(2,1)S(1)} %get-tuple-element.30), channel_id=1, source_target_pairs={{0,8},{1,9},{2,10},{3,11},{4,12},{5,13},{6,14},{7,15},{8,0},{9,1},... | collective-permute-start | bytes 491528 | tf_op jit(solution)/shard_map/ppermute | solution.py:381
  71.3 7.2 %collective-permute-start.4 = (bf16[2,64,640]{2,1,0:T(8,128)(2,1)S(1)}, bf16[2,64,640]{2,1,0:T(8,128)(2,1)S(1)}, u32[]{:S(2)}, u32[]{:S(2)}) collective-permute-start(bf16[2,64,640]{2,1,0:T(8,128)(2,1)S(1)} %get-tuple-element.31), channel_id=1, source_target_pairs={{0,2},{1,3},{2,0},{3,1},{4,6},{5,7},{6,4},{7,5},{8,10},{9,11},{10,... | collective-permute-start | bytes 491528 | tf_op jit(solution)/shard_map/ppermute | solution.py:381
  79.4 10.8 %copy-start.1 = (bf16[1,64,1024]{2,1,0:T(8,128)(2,1)S(1)}, bf16[1,64,1024]{2,1,0:T(8,128)(2,1)}, u32[]{:S(2)}) copy-start(bf16[1,64,1024]{2,1,0:T(8,128)(2,1)} %param.8) | copy-start | bytes 393220
  79.4 10.8 %copy-start.4 = (f32[1024]{0:T(1024)S(1)}, f32[1024]{0:T(1024)}, u32[]{:S(2)}) copy-start(f32[1024]{0:T(1024)} %param.12) | copy-start | bytes 12292
  79.4 10.8 %all-to-all-start.3 = ((bf16[8,144,128]{2,1,0:T(8,128)(2,1)}), bf16[8,144,128]{2,1,0:T(8,128)(2,1)S(1)}, u32[]{:S(2)}, u32[]{:S(2)}) async-start(bf16[8,144,128]{2,1,0:T(8,128)(2,1)} %get-tuple-element.34), calls=%async_computation.3 | async-start | bytes 589824 | tf_op jit(solution)/shard_map/all_to_all | solution.py:328
  83.0 3.5 %collective-permute-start.5 = (bf16[4,64,640]{2,1,0:T(8,128)(2,1)S(1)}, bf16[4,64,640]{2,1,0:T(8,128)(2,1)S(1)}, u32[]{:S(2)}, u32[]{:S(2)}) collective-permute-start(bf16[4,64,640]{2,1,0:T(8,128)(2,1)S(1)} %get-tuple-element.33), channel_id=1, source_target_pairs={{0,1},{1,0},{2,3},{3,2},{4,5},{5,4},{6,7},{7,6},{8,9},{9,8},{10,11... | collective-permute-start | bytes 983048 | tf_op jit(solution)/shard_map/ppermute | solution.py:381
